TPU v7x, 768 devices: a whole 4x8x12 slice. The times are simulated.
768 devices in a mesh: dom: 48 (over x, z), grp: 16 (over y, core).
Axes of the slice: x: 4, y: 8, z: 12, core: 2. Of those that a mesh axis runs over, the one named last changes fastest.
Arguments:
- features: bfloat16 [393216, 128], P(('dom', 'grp')), may hold values from -6 to 6
- degrees: int32 [393216], P(('dom', 'grp')), may hold values from 1 to 64
- adj_tiles: bfloat16 [61440, 128, 128], P(('dom', 'grp')), may hold values from 0 to 1
- block_list: int32 [61440, 2], P(('dom', 'grp')), may hold values from 0 to 67, as said below
- send_dom: int32 [36864, 128], P(('dom', 'grp')), may hold values from 0 to 511
- send_grp: int32 [12288, 128], P(('dom', 'grp')), may hold values from 0 to 511
- weight: bfloat16 [128, 128], replicated, may hold values from -0.5 to 0.5
- bias_vec: float32 [128], replicated, may hold values from -3 to 3
- cotangent: bfloat16 [393216, 128], P(('dom', 'grp')), may hold values from -6 to 6
Outputs:
- activated: bfloat16 [393216, 128], P(('dom', 'grp'))
- grad_features: bfloat16 [393216, 128], P(('dom', 'grp'))
- grad_weight: float32 [128, 128], replicated
- grad_bias: float32 [128], replicated
Inputs may be any that keep to these rules, and one draw needn't show every extreme that they name: `block_list`: each row is (row tile, column slot). Row tile 4 marks an unused entry, whose slot is 0. Slots below 4 are the device's own row tiles, the next 48 slots the blocks from dom peers in order, the last 16 slots those from grp peers in order. Used entries come first; on every device the first 48 + 16 entries read the remote slots in order; some device uses all 80 entries.
All inputs are finite; a program needn't handle non-finite values.
Results may differ from a plain program's by a relative error of at most 0.012.
Values may be sent and summed in bfloat16 or wider, within the bound.
No kernel may reach another device: no remote copies, remote signals or barrier semaphores. Data moves between devices by JAX's collectives and lax.ppermute only.
A program may use at most 64 MiB of HBM per device.

v0:
```python
import math

import jax
import jax.numpy as jnp
from jax import lax
from jax.sharding import PartitionSpec as P


def tile_sum(tiles_dev, blocks_dev, sources, row_tiles):
    row_tile = blocks_dev[:, 0]
    col_slot = blocks_dev[:, 1]
    tile_side = tiles_dev.shape[1]
    picked = sources[col_slot]
    products = jnp.einsum("bij,bjf->bif", tiles_dev, picked, preferred_element_type=jnp.float32)
    summed = (
        jnp.zeros((row_tiles + 1, tile_side, products.shape[2]), jnp.float32)
        .at[row_tile]
        .add(products)
    )
    return summed[:row_tiles].reshape(row_tiles * tile_side, -1)


def slot_sums(tiles_dev, blocks_dev, own_back, slot_count):
    tile_side = tiles_dev.shape[1]
    row_tile = blocks_dev[:, 0]
    col_slot = blocks_dev[:, 1]
    padded = jnp.concatenate(
        [own_back, jnp.zeros((1, tile_side, own_back.shape[2]), own_back.dtype)], axis=0
    )
    per_tile = padded[row_tile]
    contrib = jnp.einsum("bij,bif->bjf", tiles_dev, per_tile, preferred_element_type=jnp.float32)
    return (
        jnp.zeros((slot_count, tile_side, contrib.shape[2]), jnp.float32).at[col_slot].add(contrib)
    )


def body(features, degrees, adj_tiles, block_list, send_dom, send_grp, weight, bias_vec, cotangent):
    dom_count = lax.axis_size("dom")
    grp_count = lax.axis_size("grp")
    own_rows, width = features.shape
    tile_side = adj_tiles.shape[1]
    row_tiles = own_rows // tile_side
    slot_count = row_tiles + dom_count + grp_count
    inv_root = lax.rsqrt(degrees.astype(jnp.float32) + 1.0)
    scaled = (inv_root[:, None] * features.astype(jnp.float32)).astype(jnp.bfloat16)
    own_tiles = scaled.reshape(row_tiles, tile_side, width)
    from_dom = lax.all_to_all(scaled[send_dom], "dom", split_axis=0, concat_axis=0, tiled=True)
    from_grp = lax.all_to_all(scaled[send_grp], "grp", split_axis=0, concat_axis=0, tiled=True)
    sources = jnp.concatenate([own_tiles, from_dom, from_grp], axis=0)
    summed = tile_sum(adj_tiles, block_list, sources, row_tiles)
    aggregated = (inv_root[:, None] * summed).astype(jnp.bfloat16)
    pre = jnp.dot(aggregated, weight, preferred_element_type=jnp.float32) + bias_vec
    sigmoid_pre = jax.nn.sigmoid(pre)
    activated = (pre * sigmoid_pre).astype(jnp.bfloat16)
    slope = sigmoid_pre * (1.0 + pre * (1.0 - sigmoid_pre))
    delta = (cotangent.astype(jnp.float32) * slope).astype(jnp.bfloat16)
    weight_term = lax.dot_general(
        aggregated, delta, (((0,), (0,)), ((), ())), preferred_element_type=jnp.float32
    )
    bias_term = jnp.sum(delta.astype(jnp.float32), axis=0)
    grad_scale = 1.0 / math.sqrt(own_rows * dom_count * grp_count)
    weight_sum, bias_sum = lax.psum((weight_term, bias_term), ("dom", "grp"))
    grad_weight = weight_sum * grad_scale
    grad_bias = bias_sum * grad_scale
    back = (
        inv_root[:, None]
        * lax.dot_general(
            delta, weight, (((1,), (1,)), ((), ())), preferred_element_type=jnp.float32
        )
    ).astype(jnp.bfloat16)
    slot_sum = slot_sums(
        adj_tiles, block_list, back.reshape(row_tiles, tile_side, width), slot_count
    )
    own_part = slot_sum[:row_tiles].reshape(own_rows, width)
    remote = slot_sum[row_tiles:].astype(jnp.bfloat16)
    returned_dom = lax.all_to_all(
        remote[:dom_count], "dom", split_axis=0, concat_axis=0, tiled=True
    )
    returned_grp = lax.all_to_all(
        remote[dom_count:], "grp", split_axis=0, concat_axis=0, tiled=True
    )
    accumulated = own_part.at[send_dom.reshape(-1)].add(
        returned_dom.reshape(-1, width).astype(jnp.float32)
    )
    accumulated = accumulated.at[send_grp.reshape(-1)].add(
        returned_grp.reshape(-1, width).astype(jnp.float32)
    )
    grad_features = (inv_root[:, None] * accumulated).astype(jnp.bfloat16)
    return (activated, grad_features, grad_weight, grad_bias)


def solution(mesh):
    placed = (
        P(("dom", "grp"), None),
        P(("dom", "grp")),
        P(("dom", "grp"), None, None),
        P(("dom", "grp"), None),
        P(("dom", "grp"), None),
        P(("dom", "grp"), None),
        P(),
        P(),
        P(("dom", "grp"), None),
    )
    return jax.shard_map(
        body,
        mesh=mesh,
        in_specs=placed,
        out_specs=(P(("dom", "grp"), None), P(("dom", "grp"), None), P(), P()),
        check_vma=False,
    )
```

profile of v0, /device:TPU:1, one launch (start us, length us, event | category | flops | bytes accessed | tf_op | source)
XLA Modules:
  0.0 773.9 jit_solution(14047621581252112181)
XLA Ops:
  7.2 0.8 add_rsqrt_fusion
  8.7 1.0 multiply_convert_fusion.3
  9.8 8.0 %gather_fusion.1 = bf16[2048,128]{1,0:T(8,128)(2,1)} fusion(bf16[512,128]{1,0:T(8,128)(2,1)S(1)} %multiply_convert_fusion.3, s32[2048]{0:T(1024)S(1)} %fusion.9), kind=kCustom, calls=%fused_computation.1 | custom fusion | bytes 1056768 | tf_op jit(solution)/shard_map/gather | solution.py:48
  17.8 13.9 %all-to-all-start.1 = ((bf16[16,128,128]{2,1,0:T(8,128)(2,1)}), bf16[16,128,128]{2,1,0:T(8,128)(2,1)S(1)}, u32[]{:S(2)}, u32[]{:S(2)}) async-start(bf16[16,128,128]{2,1,0:T(8,128)(2,1)} %bitcast.45), calls=%async_computation.1 | async-start | bytes 1048576 | tf_op jit(solution)/shard_map/all_to_all | solution.py:48
  31.7 22.2 %gather_fusion = bf16[6144,128]{1,0:T(8,128)(2,1)} fusion(bf16[512,128]{1,0:T(8,128)(2,1)S(1)} %multiply_convert_fusion.3, s32[6144]{0:T(1024)S(1)} %fusion.7), kind=kCustom, calls=%fused_computation | custom fusion | bytes 3170304 | tf_op jit(solution)/shard_map/gather | solution.py:47
  53.9 13.1 %all-to-all-start = ((bf16[48,128,128]{2,1,0:T(8,128)(2,1)}), bf16[48,128,128]{2,1,0:T(8,128)(2,1)}, u32[]{:S(2)}, u32[]{:S(2)}) async-start(bf16[48,128,128]{2,1,0:T(8,128)(2,1)} %bitcast.44), calls=%async_computation | async-start | bytes 3145728 | tf_op jit(solution)/shard_map/all_to_all | solution.py:47
  67.1 56.6 %all-to-all-done = bf16[48,128,128]{2,1,0:T(8,128)(2,1)} async-done(((bf16[48,128,128]{2,1,0:T(8,128)(2,1)}), bf16[48,128,128]{2,1,0:T(8,128)(2,1)}, u32[]{:S(2)}, u32[]{:S(2)}) %all-to-all-start) | async-done | bytes 1572896 | tf_op jit(solution)/shard_map/all_to_all | solution.py:47
  123.7 3.0 pad_maximum_fusion
  126.8 4.2 gather_fusion.2
  130.9 6.0 convolution_bitcast_fusion.1
  136.9 6.0 copy.16
  143.0 10.8 %scatter_fusion = f32[5,128,128]{2,1,0:T(8,128)S(1)} fusion(f32[5,128,128]{2,1,0:T(8,128)S(1)} %broadcast_in_dim.8, s32[80]{0:T(128)S(1)} %get-tuple-element.8, f32[80,128,128]{2,1,0:T(8,128)} %copy.16), kind=kCustom, calls=%fused_computation.4 | custom fusion | flops 1310720 | bytes 15728960 | tf_op jit(solution)/shard_map/scatter-add | solution.py:18
  154.0 0.9 convert_reduce_fusion
  155.2 2.6 gather_fusion.3
  157.7 5.1 convolution_bitcast_fusion
  162.8 5.9 copy.18
  168.7 2.6 broadcast_in_dim.11
  171.4 17.5 %scatter_fusion.1 = f32[68,128,128]{2,1,0:T(8,128)} fusion(f32[68,128,128]{2,1,0:T(8,128)} %broadcast_in_dim.11, s32[80]{0:T(128)S(1)} %get-tuple-element.7, f32[80,128,128]{2,1,0:T(8,128)} %copy.18), kind=kCustom, calls=%fused_computation.5 | custom fusion | flops 1310720 | bytes 15728960 | tf_op jit(solution)/shard_map/scatter-add | solution.py:33
  188.9 2.7 convert.5
  191.6 1.4 copy-done.1
  193.0 1.3 slice.40
  194.3 7.5 all-to-all-start.2
  201.8 1.9 slice.41
  203.7 50.4 %all-to-all-done.2 = bf16[48,128,128]{2,1,0:T(8,128)(2,1)} async-done(((bf16[48,128,128]{2,1,0:T(8,128)(2,1)}), bf16[48,128,128]{2,1,0:T(8,128)(2,1)}, u32[]{:S(2)}, u32[]{:S(2)}) %all-to-all-start.2) | async-done | bytes 1572896 | tf_op jit(solution)/shard_map/all_to_all | solution.py:76
  254.1 11.9 %all-to-all-start.3 = ((bf16[16,128,128]{2,1,0:T(8,128)(2,1)}), bf16[16,128,128]{2,1,0:T(8,128)(2,1)S(1)}, u32[]{:S(2)}, u32[]{:S(2)}) async-start(bf16[16,128,128]{2,1,0:T(8,128)(2,1)} %slice.41), calls=%async_computation.3 | async-start | bytes 1048576 | tf_op jit(solution)/shard_map/all_to_all | solution.py:79
  266.1 0.9 fusion.12
  266.9 114.3 %psum.15 = f32[128]{0:T(128)S(1)} all-reduce(f32[128]{0:T(128)S(1)} %get-tuple-element.4), channel_id=1, replica_groups=mesh['dom'=48,'grp'=16] {'dom','grp'}, use_global_device_ids=true, to_apply=%region_6.0 | all-reduce | flops 128 | bytes 1024 | tf_op jit(solution)/shard_map/psum | solution.py:62
  381.8 1.0 slice.39
  382.7 336.4 %all-reduce.3.cloned.1.call-done = f32[128,128]{1,0:T(8,128)} async-done(((f32[128,128]{1,0:T(8,128)}), f32[128,128]{1,0:T(8,128)}) %all-reduce.3.cloned.1.call-update) | async-done | bytes 65552 | tf_op jit(solution)/shard_map/psum | solution.py:62
  719.2 1.5 broadcast_multiply_fusion
  720.6 34.0 %scatter_custom_fusion.2 = f32[512,128]{1,0:T(8,128)S(1)} fusion(f32[512,128]{1,0:T(8,128)S(1)} %bitcast.47, s32[6144]{0:T(1024)S(1)} %bitcast.51, bf16[6144,128]{1,0:T(8,128)(2,1)} %bitcast.18), kind=kCustom, calls=%fused_computation.8 | custom fusion | flops 1572864 | bytes 1835008 | tf_op jit(solution)/shard_map/scatter-add | solution.py:82
  754.6 11.6 %scatter_custom_fusion.3 = f32[512,128]{1,0:T(8,128)S(1)} fusion(f32[512,128]{1,0:T(8,128)S(1)} %scatter_custom_fusion.2, s32[2048]{0:T(1024)S(1)} %bitcast.52, bf16[2048,128]{1,0:T(8,128)(2,1)S(1)} %bitcast.46), kind=kCustom, calls=%fused_computation.16 | custom fusion | flops 524288 | bytes 786432 | tf_op jit(solution)/shard_map/scatter-add | solution.py:85
  (33 shorter events, 2.6 us)
Async XLA Ops:
  7.2 123.8 %copy-start = (bf16[80,128,128]{2,1,0:T(8,128)(2,1)S(1)}, bf16[80,128,128]{2,1,0:T(8,128)(2,1)}, u32[]{:S(2)}) copy-start(bf16[80,128,128]{2,1,0:T(8,128)(2,1)} %param.11) | copy-start | bytes 7864324
  9.8 21.9 %copy-start.2 = (s32[48,128]{1,0:T(8,128)S(1)}, s32[48,128]{1,0:T(8,128)}, u32[]{:S(2)}) copy-start(s32[48,128]{1,0:T(8,128)} %param.13) | copy-start | bytes 73732
  17.8 36.1 %all-to-all-start.1 = ((bf16[16,128,128]{2,1,0:T(8,128)(2,1)}), bf16[16,128,128]{2,1,0:T(8,128)(2,1)S(1)}, u32[]{:S(2)}, u32[]{:S(2)}) async-start(bf16[16,128,128]{2,1,0:T(8,128)(2,1)} %bitcast.45), calls=%async_computation.1 | async-start | bytes 1048576 | tf_op jit(solution)/shard_map/all_to_all | solution.py:48
  53.9 13.1 %copy-start.5 = (s32[80,2]{0,1:T(2,128)S(1)}, s32[80,2]{0,1:T(2,128)}, u32[]{:S(2)}) copy-start(s32[80,2]{0,1:T(2,128)} %param.12) | copy-start | bytes 1924
  53.9 69.8 %all-to-all-start = ((bf16[48,128,128]{2,1,0:T(8,128)(2,1)}), bf16[48,128,128]{2,1,0:T(8,128)(2,1)}, u32[]{:S(2)}, u32[]{:S(2)}) async-start(bf16[48,128,128]{2,1,0:T(8,128)(2,1)} %bitcast.44), calls=%async_computation | async-start | bytes 3145728 | tf_op jit(solution)/shard_map/all_to_all | solution.py:47
  142.9 11.0 %copy-start.3 = (bf16[128,128]{1,0:T(8,128)(2,1)S(1)}, bf16[128,128]{1,0:T(8,128)(2,1)}, u32[]{:S(2)}) copy-start(bf16[128,128]{1,0:T(8,128)(2,1)} %param.15) | copy-start | bytes 98308
  142.9 11.0 %copy-start.6 = (bf16[512,128]{1,0:T(8,128)(2,1)S(1)}, bf16[512,128]{1,0:T(8,128)(2,1)}, u32[]{:S(2)}) copy-start(bf16[512,128]{1,0:T(8,128)(2,1)} %param.17) | copy-start | bytes 393220
  142.9 11.0 %copy-start.7 = (f32[128]{0:T(128)S(1)}, f32[128]{0:T(128)}, u32[]{:S(2)}) copy-start(f32[128]{0:T(128)} %param.16) | copy-start | bytes 1540
  191.6 1.4 copy-start.1
  194.3 71.7 %copy-start.4 = (s32[16,128]{1,0:T(8,128)S(1)}, s32[16,128]{1,0:T(8,128)}, u32[]{:S(2)}) copy-start(s32[16,128]{1,0:T(8,128)} %param.14) | copy-start | bytes 24580
  194.3 59.8 %all-to-all-start.2 = ((bf16[48,128,128]{2,1,0:T(8,128)(2,1)}), bf16[48,128,128]{2,1,0:T(8,128)(2,1)}, u32[]{:S(2)}, u32[]{:S(2)}) async-start(bf16[48,128,128]{2,1,0:T(8,128)(2,1)} %slice.40), calls=%async_computation.2 | async-start | bytes 3145728 | tf_op jit(solution)/shard_map/all_to_all | solution.py:76
  254.1 500.5 %all-to-all-start.3 = ((bf16[16,128,128]{2,1,0:T(8,128)(2,1)}), bf16[16,128,128]{2,1,0:T(8,128)(2,1)S(1)}, u32[]{:S(2)}, u32[]{:S(2)}) async-start(bf16[16,128,128]{2,1,0:T(8,128)(2,1)} %slice.41), calls=%async_computation.3 | async-start | bytes 1048576 | tf_op jit(solution)/shard_map/all_to_all | solution.py:79
  266.0 453.2 %all-reduce.3.cloned.1.call-start = ((), (), s32[]{:S(2)}) async-start(), calls=%async_computation.4 | async-start | bytes 131072 | tf_op jit(solution)/shard_map/psum | solution.py:62
Sparse Core Ops, SparseCore 0:
  272.8 446.3 all-reduce.2
where the time goes:
time: 777 us; the launch traced here: 774 us
  waiting for transfers between devices  443 us (57%)
  blocking collectives  114 us (15%)
  other arithmetic  85.2 us (11%)
  local copies, waits for them, and re-layouts  57.1 us (7%)
  starting transfers between devices  46.4 us (6%)
  between operations  14.3 us (2%)
  matrix products  13.1 us (2%)
    psum x1, waiting for transfers between devices, body(): weight_sum, bias_sum = lax.psum((weight_term, bias_term), ('dom', 'grp'))  336 us
    psum x1, blocking collectives, body(): weight_sum, bias_sum = lax.psum((weight_term, bias_term), ('dom', 'grp'))  114 us
    all_to_all x1, waiting for transfers between devices, body(): lax.all_to_all(scaled[send_dom], 'dom', split_axis=0, concat_axis=0, tile...  56.6 us
    all_to_all x1, waiting for transfers between devices, body(): lax.all_to_all(remote[:dom_count], 'dom', split_axis=0, concat_axis=0, ti...  50.4 us
    scatter-add x1, other arithmetic, body(): own_part.at[send_dom.reshape(-1)]  34 us
    gather x1, local copies, waits for them, and re-layouts, body(): scaled[send_dom]  22.2 us
    scatter-add x1, other arithmetic, slot_sums(): jnp.zeros((slot_count, tile_side, contrib.shape[2]), jnp.float32)  17.5 us
  transfers between devices with their start and end apart: 5, of which 3 were waited for; matrix products, arithmetic and copies ran while one was open for 8% of the time, Pallas kernels for 0%

commit v1 on v0

v1 whole, which is shorter than its diff:
```python
import functools
import math

import jax
import jax.numpy as jnp
from jax import lax
from jax.experimental import pallas as pl
from jax.experimental.pallas import tpu as pltpu
from jax.sharding import PartitionSpec as P

TILE = 128
ROW_TILES = 4
ROWS = TILE * ROW_TILES
NODE_DIM, LANE_DIM = 0, 1
VMEM_LIMIT = 48 * 1024 * 1024
VMEM = pl.BlockSpec(memory_space=pltpu.VMEM)
SMEM = pl.BlockSpec(memory_space=pltpu.SMEM)

NT = (((1,), (1,)), ((), ()))
NN = (((1,), (0,)), ((), ()))
TN = (((0,), (0,)), ((), ()))


def mul(left, right, dims):
    return lax.dot_general(left, right, dims, preferred_element_type=jnp.float32)


def call(kernel, out_shape, in_specs, scratch=(), flops=0, nbytes=0):
    return pl.pallas_call(
        kernel,
        out_shape=out_shape,
        in_specs=in_specs,
        out_specs=jax.tree.map(lambda _: VMEM, out_shape),
        scratch_shapes=list(scratch),
        compiler_params=pltpu.CompilerParams(vmem_limit_bytes=VMEM_LIMIT),
        cost_estimate=pl.CostEstimate(flops=flops, bytes_accessed=nbytes, transcendentals=0),
    )


def inverse_root(degrees_ref):
    return lax.rsqrt(degrees_ref[...].astype(jnp.float32) + 1.0)


def one_hot(rows):
    node = lax.broadcasted_iota(jnp.int32, (ROWS, TILE), 0)
    return jnp.concatenate(
        [jnp.where(node == row, 1.0, 0.0).astype(jnp.bfloat16) for row in rows], axis=1
    )


def group(count):
    return 8 if count % 8 == 0 else count


def scale_gather_dom(degrees_ref, features_ref, lists_ref, out_ref, scaled_ref):
    root = inverse_root(degrees_ref)
    for t in range(ROW_TILES):
        turned = features_ref[t * TILE : (t + 1) * TILE, :].astype(jnp.float32).T
        scaled_ref[t] = (turned * root[t : t + 1, :]).astype(jnp.bfloat16)
    scaled = jnp.concatenate([scaled_ref[t] for t in range(ROW_TILES)], axis=1)
    count = lists_ref.shape[0]
    step = group(count)

    @pl.loop(0, count // step)
    def _(part):
        first = part * step
        rows = lists_ref[pl.ds(pl.multiple_of(first, step), step), :]
        picked = mul(scaled, one_hot([rows[i : i + 1, :] for i in range(step)]), NN)
        picked = picked.astype(jnp.bfloat16)
        for i in range(step):
            out_ref[first + i] = picked[:, i * TILE : (i + 1) * TILE]


def gather_grp(me_ref, scaled_ref, lists_ref, *out_refs):
    me = me_ref[0]
    scaled = jnp.concatenate([scaled_ref[t] for t in range(ROW_TILES)], axis=1)
    for k, out_ref in enumerate(out_refs):
        row = lists_ref[pl.ds(jnp.bitwise_xor(me, k), 1), :]
        out_ref[...] = mul(scaled, one_hot([row]), NN).astype(jnp.bfloat16)


def near_sum(dom, grp, me_ref, blocks_ref, tiles_ref, scaled_ref, *refs):
    recv_refs, (out_ref, sources_ref) = refs[:grp], refs[grp:]
    me = me_ref[0]
    out_ref[...] = jnp.zeros_like(out_ref)
    for t in range(ROW_TILES):
        sources_ref[t] = scaled_ref[t]
    for k in range(grp):
        peer = jnp.bitwise_xor(me, k)
        block = recv_refs[k][...]
        sources_ref[ROW_TILES + peer] = block
        row_tile = blocks_ref[0, dom + peer]
        out_ref[row_tile] += mul(tiles_ref[dom + peer], block, NT)
    for b in range(dom + grp, tiles_ref.shape[0]):
        row_tile, slot = blocks_ref[0, b], blocks_ref[1, b]
        own = slot < ROW_TILES
        near = jnp.logical_or(own, slot >= ROW_TILES + dom)
        at = jnp.where(own, slot, jnp.where(near, slot - dom, 0))
        row_tile = jnp.where(near, row_tile, ROW_TILES)
        out_ref[row_tile] += mul(tiles_ref[b], sources_ref[at], NT)


def layer(
    dom,
    grp,
    blocks_ref,
    degrees_ref,
    tiles_ref,
    recv_ref,
    near_ref,
    weight_ref,
    bias_ref,
    cotangent_ref,
    activated_ref,
    return_ref,
    back_ref,
    weight_term_ref,
    bias_term_ref,
    acc_ref,
    slots_ref,
):
    acc_ref[...] = near_ref[...]
    for b in range(dom):
        acc_ref[blocks_ref[0, b]] += mul(tiles_ref[b], recv_ref[b], NT)
    for b in range(dom + grp, tiles_ref.shape[0]):
        row_tile, slot = blocks_ref[0, b], blocks_ref[1, b]
        far = jnp.logical_and(slot >= ROW_TILES, slot < ROW_TILES + dom)
        at = jnp.where(far, slot - ROW_TILES, 0)
        row_tile = jnp.where(far, row_tile, ROW_TILES)
        acc_ref[row_tile] += mul(tiles_ref[b], recv_ref[at], NT)

    root = inverse_root(degrees_ref)
    weight = weight_ref[...]
    weight_term = jnp.zeros((TILE, TILE), jnp.float32)
    bias_term = jnp.zeros((1, TILE), jnp.float32)
    for t in range(ROW_TILES):
        rows = slice(t * TILE, (t + 1) * TILE)
        root_rows = jnp.broadcast_to(root[t : t + 1, :], (TILE, TILE)).T
        aggregated = (root_rows * acc_ref[t]).astype(jnp.bfloat16)
        pre = mul(aggregated, weight, NN) + bias_ref[...]
        sigmoid_pre = jax.nn.sigmoid(pre)
        activated_ref[rows, :] = (pre * sigmoid_pre).astype(jnp.bfloat16)
        slope = sigmoid_pre * (1.0 + pre * (1.0 - sigmoid_pre))
        delta = (cotangent_ref[rows, :].astype(jnp.float32) * slope).astype(jnp.bfloat16)
        weight_term += mul(aggregated, delta, TN)
        bias_term += jnp.sum(delta.astype(jnp.float32), axis=0, keepdims=True)
        back_ref[t] = (root[t : t + 1, :] * mul(weight, delta, NT)).astype(jnp.bfloat16)
    back_ref[ROW_TILES] = jnp.zeros((TILE, TILE), jnp.bfloat16)
    weight_term_ref[...] = weight_term
    bias_term_ref[...] = bias_term

    for b in range(dom):
        slots_ref[b] = mul(back_ref[blocks_ref[0, b]], tiles_ref[b], NN)
    for b in range(dom + grp, tiles_ref.shape[0]):
        slot = blocks_ref[1, b]
        far = jnp.logical_and(slot >= ROW_TILES, slot < ROW_TILES + dom)
        at = jnp.where(far, slot - ROW_TILES, dom)
        slots_ref[at] += mul(back_ref[blocks_ref[0, b]], tiles_ref[b], NN)
    for b in range(dom):
        return_ref[b] = slots_ref[b].astype(jnp.bfloat16)


def near_back(dom, grp, me_ref, blocks_ref, tiles_ref, back_ref, weight_term_ref, bias_term_ref, *refs):
    own_ref, *out_refs, slots_ref = refs
    me = me_ref[0]
    slots_ref[0:ROW_TILES] = jnp.zeros((ROW_TILES, TILE, TILE), jnp.float32)
    for k in range(grp):
        b = dom + jnp.bitwise_xor(me, k)
        slots_ref[ROW_TILES + k] = mul(back_ref[blocks_ref[0, b]], tiles_ref[b], NN)
    for b in range(dom + grp, tiles_ref.shape[0]):
        slot = blocks_ref[1, b]
        own = slot < ROW_TILES
        lent = slot >= ROW_TILES + dom
        turn = jnp.bitwise_xor(jnp.maximum(slot - ROW_TILES - dom, 0), me)
        at = jnp.where(own, slot, jnp.where(lent, ROW_TILES + turn, ROW_TILES + grp))
        slots_ref[at] += mul(back_ref[blocks_ref[0, b]], tiles_ref[b], NN)
    for t in range(ROW_TILES):
        own_ref[t * TILE : (t + 1) * TILE, :] = slots_ref[t].T
    depth = TILE // grp
    bias_term = bias_term_ref[...]
    bias_high = bias_term.astype(jnp.bfloat16).astype(jnp.float32)
    line = lax.broadcasted_iota(jnp.int32, (16, TILE), 0)
    bias_rows = jnp.where(
        line == 0, bias_high, jnp.where(line == 1, bias_term - bias_high, 0.0)
    ).astype(jnp.bfloat16)
    for k, out_ref in enumerate(out_refs):
        out_ref[0:TILE, :] = slots_ref[ROW_TILES + k].astype(jnp.bfloat16)
        first = pl.multiple_of(jnp.bitwise_xor(me, k) * depth, depth)
        term = weight_term_ref[pl.ds(first, depth), :]
        high = term.astype(jnp.bfloat16).astype(jnp.float32)
        pair = jnp.concatenate([high, term - high], axis=0).astype(jnp.bfloat16)
        out_ref[TILE : TILE + 2 * depth, :] = pair
        out_ref[TILE + 2 * depth :, :] = bias_rows


def sum_terms(depth, *refs):
    *recv_refs, out_ref = refs
    total = jnp.zeros((2 * depth + 16, TILE), jnp.float32)
    for recv_ref in recv_refs:
        total += recv_ref[TILE:, :].astype(jnp.float32)
    out_ref[0:depth, :] = total[0:depth, :] + total[depth : 2 * depth, :]
    bias_term = total[2 * depth : 2 * depth + 1, :] + total[2 * depth + 1 : 2 * depth + 2, :]
    out_ref[depth:, :] = jnp.broadcast_to(bias_term, (8, TILE))


def place_chunks(me_ref, turned_ref, out_ref):
    for k in range(turned_ref.shape[0]):
        out_ref[jnp.bitwise_xor(me_ref[0], k)] = turned_ref[k]


def near_scatter(me_ref, lists_ref, own_ref, *refs):
    *recv_refs, out_ref = refs
    me = me_ref[0]
    rows = [lists_ref[pl.ds(jnp.bitwise_xor(me, k), 1), :] for k in range(len(recv_refs))]
    total = own_ref[...]
    step = group(len(recv_refs))
    for first in range(0, len(recv_refs), step):
        part = range(first, first + step)
        blocks = jnp.concatenate([recv_refs[k][0:TILE, :] for k in part], axis=1)
        total += mul(one_hot([rows[k] for k in part]), blocks, NT)
    out_ref[...] = total


def dom_scatter(degrees_ref, lists_ref, near_ref, recv_ref, out_ref, acc_ref):
    count = lists_ref.shape[0]
    step = group(count)
    acc_ref[...] = near_ref[...]

    @pl.loop(0, count // step)
    def _(part):
        first = part * step
        rows = lists_ref[pl.ds(pl.multiple_of(first, step), step), :]
        blocks = jnp.concatenate([recv_ref[first + i] for i in range(step)], axis=1)
        acc_ref[...] += mul(one_hot([rows[i : i + 1, :] for i in range(step)]), blocks, NT)

    root = inverse_root(degrees_ref)
    for t in range(ROW_TILES):
        rows = slice(t * TILE, (t + 1) * TILE)
        root_rows = jnp.broadcast_to(root[t : t + 1, :], (TILE, TILE)).T
        out_ref[rows, :] = (root_rows * acc_ref[rows, :]).astype(jnp.bfloat16)


def xor_permute(value, axis, size, k):
    return lax.ppermute(value, axis, [(i, i ^ k) for i in range(size)])


def digit_permute(value, axis, size, stride, radix, k):
    def target(i):
        digit = i // stride % radix
        return i + ((digit + k) % radix - digit) * stride

    return lax.ppermute(value, axis, [(i, target(i)) for i in range(size)])


def digits(size):
    out, stride = [], 1
    while size > 1:
        radix = next(r for r in (4, 3, 2, size) if size % r == 0)
        out.append((stride, radix))
        stride, size = stride * radix, size // radix
    return out


def body(features, degrees, adj_tiles, block_list, send_dom, send_grp, weight, bias_vec, cotangent):
    dom = lax.axis_size("dom")
    grp = lax.axis_size("grp")
    entries = adj_tiles.shape[0]
    bf16, f32 = jnp.bfloat16, jnp.float32
    shape = jax.ShapeDtypeStruct
    me = lax.axis_index("grp").astype(jnp.int32).reshape(1)
    degree_rows = degrees.reshape(ROW_TILES, TILE)
    blocks = block_list.T
    bias_row = bias_vec.reshape(1, TILE)
    product = 2 * TILE**3
    block_bytes = 2 * TILE * TILE

    to_dom, scaled = call(
        scale_gather_dom,
        (shape((dom, TILE, TILE), bf16), shape((ROW_TILES, TILE, TILE), bf16)),
        [VMEM] * 3,
        flops=4 * dom * product,
        nbytes=dom * block_bytes,
    )(degree_rows, features, send_dom)
    from_dom = lax.all_to_all(to_dom, "dom", split_axis=0, concat_axis=0, tiled=True)
    to_grp = call(
        gather_grp,
        [shape((TILE, TILE), bf16)] * grp,
        [SMEM, VMEM, VMEM],
        flops=4 * grp * product,
        nbytes=grp * block_bytes,
    )(me, scaled, send_grp)
    from_grp = [to_grp[0]] + [xor_permute(to_grp[k], "grp", grp, k) for k in range(1, grp)]
    near = call(
        functools.partial(near_sum, dom, grp),
        shape((ROW_TILES + 1, TILE, TILE), f32),
        [SMEM, SMEM] + [VMEM] * (2 + grp),
        [pltpu.VMEM((ROW_TILES + grp, TILE, TILE), bf16)],
        flops=(entries - dom) * product,
        nbytes=entries * block_bytes,
    )(me, blocks, adj_tiles, scaled, *from_grp)

    activated, to_lender, back, weight_term, bias_term = call(
        functools.partial(layer, dom, grp),
        (
            shape((ROWS, TILE), bf16),
            shape((dom, TILE, TILE), bf16),
            shape((ROW_TILES + 1, TILE, TILE), bf16),
            shape((TILE, TILE), f32),
            shape((1, TILE), f32),
        ),
        [SMEM] + [VMEM] * 7,
        [
            pltpu.VMEM((ROW_TILES + 1, TILE, TILE), f32),
            pltpu.VMEM((dom + 1, TILE, TILE), f32),
        ],
        flops=2 * entries * product,
        nbytes=3 * entries * block_bytes,
    )(blocks, degree_rows, adj_tiles, from_dom, near, weight, bias_row, cotangent)
    returned_dom = lax.all_to_all(to_lender, "dom", split_axis=0, concat_axis=0, tiled=True)

    depth = TILE // grp
    own, *to_near = call(
        functools.partial(near_back, dom, grp),
        [shape((ROWS, TILE), f32)] + [shape((TILE + 2 * depth + 16, TILE), bf16)] * grp,
        [SMEM, SMEM] + [VMEM] * 4,
        [pltpu.VMEM((ROW_TILES + grp + 1, TILE, TILE), f32)],
        flops=(entries - dom) * product,
        nbytes=entries * block_bytes,
    )(me, blocks, adj_tiles, back, weight_term, bias_term)
    returned_grp = [to_near[0]] + [xor_permute(to_near[k], "grp", grp, k) for k in range(1, grp)]

    grad_scale = 1.0 / math.sqrt(ROWS * dom * grp)
    chunk = call(
        functools.partial(sum_terms, depth),
        shape((depth + 8, TILE), f32),
        [VMEM] * grp,
        nbytes=grp * block_bytes,
    )(*returned_grp)
    for stride, radix in digits(dom):
        chunk = chunk + sum(
            digit_permute(chunk, "dom", dom, stride, radix, k) for k in range(1, radix)
        )
    chunk = chunk * grad_scale
    grad_bias = chunk[depth]
    gathered = chunk[:depth]
    for stride, radix in digits(grp):
        gathered = jnp.concatenate(
            [gathered]
            + [xor_permute(gathered, "grp", grp, k * stride) for k in range(1, radix)]
        )
    turned = gathered.reshape(grp, depth, TILE)
    grad_weight = call(
        place_chunks, shape((grp, depth, TILE), f32), [SMEM, VMEM], nbytes=2 * 4 * TILE * TILE
    )(me, turned).reshape(TILE, TILE)

    near_grad = call(
        near_scatter,
        shape((ROWS, TILE), f32),
        [SMEM] + [VMEM] * (2 + grp),
        flops=4 * grp * product,
        nbytes=grp * block_bytes,
    )(me, send_grp, own, *returned_grp)
    grad_features = call(
        dom_scatter,
        shape((ROWS, TILE), bf16),
        [VMEM] * 4,
        [pltpu.VMEM((ROWS, TILE), f32)],
        flops=4 * dom * product,
        nbytes=dom * block_bytes,
    )(degree_rows, send_dom, near_grad, returned_dom)
    return (activated, grad_features, grad_weight, grad_bias)


def solution(mesh):
    placed = (
        P(("dom", "grp"), None),
        P(("dom", "grp")),
        P(("dom", "grp"), None, None),
        P(("dom", "grp"), None),
        P(("dom", "grp"), None),
        P(("dom", "grp"), None),
        P(),
        P(),
        P(("dom", "grp"), None),
    )
    return jax.shard_map(
        body,
        mesh=mesh,
        in_specs=placed,
        out_specs=(P(("dom", "grp"), None), P(("dom", "grp"), None), P(), P()),
        check_vma=False,
    )
```

time: 777 us -> 253 us (0.33)
  waiting for transfers between devices: 443 us -> 25.6 us
  starting transfers between devices: 46.4 us -> 200 us
  blocking collectives: 114 us -> 0 us
  other arithmetic: 85.2 us -> 0.02 us
  local copies, waits for them, and re-layouts: 57.1 us -> 5.19 us
  Pallas kernels: 0 us -> 17.4 us
  matrix products: 13.1 us -> 0 us
  between operations: 14.3 us -> 1.43 us
    psum x1 -> x0, waiting for transfers between devices: 336 us -> none  [body(): weight_sum, bias_sum = lax.psum((weight_term, bias_term), ('dom', 'grp'))]
    ppermute x0 -> x44, starting transfers between devices: none -> 168 us  [the longest x36 133 us: xor_permute(): return lax.ppermute(value, axis, [(i, i ^ k) for i in range(size)])]
    psum x1 -> x0, blocking collectives: 114 us -> none  [body(): weight_sum, bias_sum = lax.psum((weight_term, bias_term), ('dom', 'grp'))]
    all_to_all x4 -> x2, waiting for transfers between devices: 107 us -> 0.01 us  [the longest x1 0.01 us: body(): lax.all_to_all(to_dom, 'dom', split_axis=0, concat_axis=0, tiled=True)]
    scatter-add x4 -> x0, other arithmetic: 73.9 us -> none  [the longest x1 34 us: body(): own_part.at[send_dom.reshape(-1)]]
    gather x4 -> x0, local copies, waits for them, and re-layouts: 37 us -> none  [the longest x1 22.2 us: body(): scaled[send_dom]]
    ppermute x0 -> x44, waiting for transfers between devices: none -> 25.6 us  [the longest x36 13.1 us: xor_permute(): return lax.ppermute(value, axis, [(i, i ^ k) for i in range(size)])]
    pallas_call x0 -> x9, Pallas kernels: none -> 17.4 us  [the longest x1 5.84 us: body(): call(functools.partial(layer, dom, grp), (shape((ROWS, TILE), bf16), shap...]
  transfers between devices with their start and end apart: 5 -> 46, of which waited for: 3 -> 9; matrix products, arithmetic and copies ran while one was open for 8% -> 0% of each run, Pallas kernels for 0% -> 2%
where the time goes in v1:
time: 253 us; the launch traced here: 249 us
  starting transfers between devices  200 us (79%)
  waiting for transfers between devices  25.6 us (10%)
  Pallas kernels  17.4 us (7%)
  local copies, waits for them, and re-layouts  5.19 us (2%)
    ppermute x36, starting transfers between devices, xor_permute(): return lax.ppermute(value, axis, [(i, i ^ k) for i in range(size)])  133 us
    ppermute x8, starting transfers between devices, digit_permute(): return lax.ppermute(value, axis, [(i, target(i)) for i in range(size)])  35 us
    all_to_all x1, starting transfers between devices, body(): lax.all_to_all(to_dom, 'dom', split_axis=0, concat_axis=0, tiled=True)  19.3 us
    ppermute x36, waiting for transfers between devices, xor_permute(): return lax.ppermute(value, axis, [(i, i ^ k) for i in range(size)])  13.1 us
    ppermute x8, waiting for transfers between devices, digit_permute(): return lax.ppermute(value, axis, [(i, target(i)) for i in range(size)])  12.5 us
    all_to_all x1, starting transfers between devices, body(): lax.all_to_all(to_lender, 'dom', split_axis=0, concat_axis=0, tiled=True)  12.4 us
    pallas_call x1, Pallas kernels, body(): call(functools.partial(layer, dom, grp), (shape((ROWS, TILE), bf16), shap...  5.84 us
  transfers between devices with their start and end apart: 46, of which 9 were waited for; matrix products, arithmetic and copies ran while one was open for 0% of the time, Pallas kernels for 2%

profile of v1, /device:TPU:1, one launch (start us, length us, event | category | flops | bytes accessed | tf_op | source)
XLA Modules:
  0.0 249.4 jit_solution(11561334931010765378)
XLA Ops:
  6.1 19.3 %all-to-all-start = ((bf16[48,128,128]{2,1,0:T(8,128)(2,1)}), bf16[48,128,128]{2,1,0:T(8,128)(2,1)}, u32[]{:S(2)}, u32[]{:S(2)}) async-start(bf16[48,128,128]{2,1,0:T(8,128)(2,1)} %copy-done.3), calls=%async_computation | async-start | bytes 3145728 | tf_op jit(solution)/shard_map/all_to_all | solution.py:284
  29.1 3.2 %collective-permute-start.1 = (bf16[128,128]{1,0:T(8,128)(2,1)S(1)}, bf16[128,128]{1,0:T(8,128)(2,1)S(1)}, u32[]{:S(2)}, u32[]{:S(2)}) collective-permute-start(bf16[128,128]{1,0:T(8,128)(2,1)S(1)} %get-tuple-element.48), channel_id=1, source_target_pairs={{0,2},{1,3},{2,0},{3,1},{4,6},{5,7},{6,4},{7,5},{8,10},{9,11},{10,... | collective-permute-start | bytes 98312 | tf_op jit(solution)/shard_map/ppermute | solution.py:244
  34.5 4.2 %collective-permute-start.3 = (bf16[128,128]{1,0:T(8,128)(2,1)S(1)}, bf16[128,128]{1,0:T(8,128)(2,1)S(1)}, u32[]{:S(2)}, u32[]{:S(2)}) collective-permute-start(bf16[128,128]{1,0:T(8,128)(2,1)S(1)} %get-tuple-element.50), channel_id=1, source_target_pairs={{0,4},{1,5},{2,6},{3,7},{4,0},{5,1},{6,2},{7,3},{8,12},{9,13},{10,... | collective-permute-start | bytes 98312 | tf_op jit(solution)/shard_map/ppermute | solution.py:244
  41.1 5.2 %collective-permute-start.5 = (bf16[128,128]{1,0:T(8,128)(2,1)S(1)}, bf16[128,128]{1,0:T(8,128)(2,1)S(1)}, u32[]{:S(2)}, u32[]{:S(2)}) collective-permute-start(bf16[128,128]{1,0:T(8,128)(2,1)S(1)} %get-tuple-element.52), channel_id=1, source_target_pairs={{0,6},{1,7},{2,4},{3,5},{4,2},{5,3},{6,0},{7,1},{8,14},{9,15},{10,... | collective-permute-start | bytes 98312 | tf_op jit(solution)/shard_map/ppermute | solution.py:244
  48.5 7.4 %collective-permute-start.7 = (bf16[128,128]{1,0:T(8,128)(2,1)S(1)}, bf16[128,128]{1,0:T(8,128)(2,1)S(1)}, u32[]{:S(2)}, u32[]{:S(2)}) collective-permute-start(bf16[128,128]{1,0:T(8,128)(2,1)S(1)} %get-tuple-element.54), channel_id=1, source_target_pairs={{0,8},{1,9},{2,10},{3,11},{4,12},{5,13},{6,14},{7,15},{8,0},{9,1},... | collective-permute-start | bytes 98312 | tf_op jit(solution)/shard_map/ppermute | solution.py:244
  58.1 4.8 %collective-permute-start.9 = (bf16[128,128]{1,0:T(8,128)(2,1)S(1)}, bf16[128,128]{1,0:T(8,128)(2,1)S(1)}, u32[]{:S(2)}, u32[]{:S(2)}) collective-permute-start(bf16[128,128]{1,0:T(8,128)(2,1)S(1)} %get-tuple-element.56), channel_id=1, source_target_pairs={{0,10},{1,11},{2,8},{3,9},{4,14},{5,15},{6,12},{7,13},{8,2},{9,3},... | collective-permute-start | bytes 98312 | tf_op jit(solution)/shard_map/ppermute | solution.py:244
  62.9 3.9 %collective-permute-start.10 = (bf16[128,128]{1,0:T(8,128)(2,1)S(1)}, bf16[128,128]{1,0:T(8,128)(2,1)S(1)}, u32[]{:S(2)}, u32[]{:S(2)}) collective-permute-start(bf16[128,128]{1,0:T(8,128)(2,1)S(1)} %get-tuple-element.57), channel_id=1, source_target_pairs={{0,11},{1,10},{2,9},{3,8},{4,15},{5,14},{6,13},{7,12},{8,3},{9,2},... | collective-permute-start | bytes 98312 | tf_op jit(solution)/shard_map/ppermute | solution.py:244
  66.8 3.8 %collective-permute-start.11 = (bf16[128,128]{1,0:T(8,128)(2,1)S(1)}, bf16[128,128]{1,0:T(8,128)(2,1)S(1)}, u32[]{:S(2)}, u32[]{:S(2)}) collective-permute-start(bf16[128,128]{1,0:T(8,128)(2,1)S(1)} %get-tuple-element.58), channel_id=1, source_target_pairs={{0,12},{1,13},{2,14},{3,15},{4,8},{5,9},{6,10},{7,11},{8,4},{9,5},... | collective-permute-start | bytes 98312 | tf_op jit(solution)/shard_map/ppermute | solution.py:244
  70.6 3.8 %collective-permute-start.12 = (bf16[128,128]{1,0:T(8,128)(2,1)S(1)}, bf16[128,128]{1,0:T(8,128)(2,1)S(1)}, u32[]{:S(2)}, u32[]{:S(2)}) collective-permute-start(bf16[128,128]{1,0:T(8,128)(2,1)S(1)} %get-tuple-element.59), channel_id=1, source_target_pairs={{0,13},{1,12},{2,15},{3,14},{4,9},{5,8},{6,11},{7,10},{8,5},{9,4},... | collective-permute-start | bytes 98312 | tf_op jit(solution)/shard_map/ppermute | solution.py:244
  74.4 5.0 %collective-permute-start.13 = (bf16[128,128]{1,0:T(8,128)(2,1)S(1)}, bf16[128,128]{1,0:T(8,128)(2,1)S(1)}, u32[]{:S(2)}, u32[]{:S(2)}) collective-permute-start(bf16[128,128]{1,0:T(8,128)(2,1)S(1)} %get-tuple-element.60), channel_id=1, source_target_pairs={{0,14},{1,15},{2,12},{3,13},{4,10},{5,11},{6,8},{7,9},{8,6},{9,7},... | collective-permute-start | bytes 98312 | tf_op jit(solution)/shard_map/ppermute | solution.py:244
  81.4 4.5 %collective-permute-done.14.refs_15_ = bf16[128,128]{1,0:T(8,128)(2,1)S(1)} collective-permute-done((bf16[128,128]{1,0:T(8,128)(2,1)S(1)}, bf16[128,128]{1,0:T(8,128)(2,1)S(1)}, u32[]{:S(2)}, u32[]{:S(2)}) %collective-permute-start.14) | collective-permute-done | bytes 32800 | tf_op jit(solution)/shard_map/ppermute | solution.py:244
  87.5 5.8 %shard_map.123 = (bf16[512,128]{1,0:T(8,128)(2,1)}, bf16[48,128,128]{2,1,0:T(8,128)(2,1)S(1)}, bf16[5,128,128]{2,1,0:T(8,128)(2,1)S(1)}, f32[128,128]{1,0:T(8,128)S(1)}, f32[1,128]{1,0:T(1,128)S(1)}) custom-call(s32[2,80]{1,0:T(2,128)S(1)} %bitcast.10, s32[4,128]{1,0:T(4,128)S(1)} %bitcast.13, bf16[80,128,128]{2,1,0:T(8,128)(2,1)} %tiles_ref.5, ...), custom_call_target="tpu_custom_call" | custom-call | flops 671088640 | bytes 7864320 | tf_op jit(solution)/shard_map/pallas_call | solution.py:302
  94.5 12.4 %all-to-all-start.1 = ((bf16[48,128,128]{2,1,0:T(8,128)(2,1)}), bf16[48,128,128]{2,1,0:T(8,128)(2,1)}, u32[]{:S(2)}, u32[]{:S(2)}) async-start(bf16[48,128,128]{2,1,0:T(8,128)(2,1)} %copy-done.2), calls=%async_computation.1 | async-start | bytes 3145728 | tf_op jit(solution)/shard_map/all_to_all | solution.py:319
  110.6 3.9 %collective-permute-start.16 = (bf16[160,128]{1,0:T(8,128)(2,1)S(1)}, bf16[160,128]{1,0:T(8,128)(2,1)S(1)}, u32[]{:S(2)}, u32[]{:S(2)}) collective-permute-start(bf16[160,128]{1,0:T(8,128)(2,1)S(1)} %get-tuple-element.69), channel_id=1, source_target_pairs={{0,2},{1,3},{2,0},{3,1},{4,6},{5,7},{6,4},{7,5},{8,10},{9,11},{10,... | collective-permute-start | bytes 122888 | tf_op jit(solution)/shard_map/ppermute | solution.py:244
  116.4 4.4 %collective-permute-start.18 = (bf16[160,128]{1,0:T(8,128)(2,1)S(1)}, bf16[160,128]{1,0:T(8,128)(2,1)S(1)}, u32[]{:S(2)}, u32[]{:S(2)}) collective-permute-start(bf16[160,128]{1,0:T(8,128)(2,1)S(1)} %get-tuple-element.71), channel_id=1, source_target_pairs={{0,4},{1,5},{2,6},{3,7},{4,0},{5,1},{6,2},{7,3},{8,12},{9,13},{10,... | collective-permute-start | bytes 122888 | tf_op jit(solution)/shard_map/ppermute | solution.py:244
  123.2 4.9 %collective-permute-start.20 = (bf16[160,128]{1,0:T(8,128)(2,1)S(1)}, bf16[160,128]{1,0:T(8,128)(2,1)S(1)}, u32[]{:S(2)}, u32[]{:S(2)}) collective-permute-start(bf16[160,128]{1,0:T(8,128)(2,1)S(1)} %get-tuple-element.73), channel_id=1, source_target_pairs={{0,6},{1,7},{2,4},{3,5},{4,2},{5,3},{6,0},{7,1},{8,14},{9,15},{10,... | collective-permute-start | bytes 122888 | tf_op jit(solution)/shard_map/ppermute | solution.py:244
  130.5 5.5 %collective-permute-start.22 = (bf16[160,128]{1,0:T(8,128)(2,1)S(1)}, bf16[160,128]{1,0:T(8,128)(2,1)S(1)}, u32[]{:S(2)}, u32[]{:S(2)}) collective-permute-start(bf16[160,128]{1,0:T(8,128)(2,1)S(1)} %get-tuple-element.75), channel_id=1, source_target_pairs={{0,8},{1,9},{2,10},{3,11},{4,12},{5,13},{6,14},{7,15},{8,0},{9,1},... | collective-permute-start | bytes 122888 | tf_op jit(solution)/shard_map/ppermute | solution.py:244
  136.0 4.1 %collective-permute-start.23 = (bf16[160,128]{1,0:T(8,128)(2,1)S(1)}, bf16[160,128]{1,0:T(8,128)(2,1)S(1)}, u32[]{:S(2)}, u32[]{:S(2)}) collective-permute-start(bf16[160,128]{1,0:T(8,128)(2,1)S(1)} %get-tuple-element.76), channel_id=1, source_target_pairs={{0,9},{1,8},{2,11},{3,10},{4,13},{5,12},{6,15},{7,14},{8,1},{9,0},... | collective-permute-start | bytes 122888 | tf_op jit(solution)/shard_map/ppermute | solution.py:244
  140.1 4.2 %collective-permute-start.24 = (bf16[160,128]{1,0:T(8,128)(2,1)S(1)}, bf16[160,128]{1,0:T(8,128)(2,1)S(1)}, u32[]{:S(2)}, u32[]{:S(2)}) collective-permute-start(bf16[160,128]{1,0:T(8,128)(2,1)S(1)} %get-tuple-element.77), channel_id=1, source_target_pairs={{0,10},{1,11},{2,8},{3,9},{4,14},{5,15},{6,12},{7,13},{8,2},{9,3},... | collective-permute-start | bytes 122888 | tf_op jit(solution)/shard_map/ppermute | solution.py:244
  144.3 4.4 %collective-permute-start.25 = (bf16[160,128]{1,0:T(8,128)(2,1)S(1)}, bf16[160,128]{1,0:T(8,128)(2,1)S(1)}, u32[]{:S(2)}, u32[]{:S(2)}) collective-permute-start(bf16[160,128]{1,0:T(8,128)(2,1)S(1)} %get-tuple-element.78), channel_id=1, source_target_pairs={{0,11},{1,10},{2,9},{3,8},{4,15},{5,14},{6,13},{7,12},{8,3},{9,2},... | collective-permute-start | bytes 122888 | tf_op jit(solution)/shard_map/ppermute | solution.py:244
  151.4 5.0 %collective-permute-start.27 = (bf16[160,128]{1,0:T(8,128)(2,1)S(1)}, bf16[160,128]{1,0:T(8,128)(2,1)S(1)}, u32[]{:S(2)}, u32[]{:S(2)}) collective-permute-start(bf16[160,128]{1,0:T(8,128)(2,1)S(1)} %get-tuple-element.80), channel_id=1, source_target_pairs={{0,13},{1,12},{2,15},{3,14},{4,9},{5,8},{6,11},{7,10},{8,5},{9,4},... | collective-permute-start | bytes 122888 | tf_op jit(solution)/shard_map/ppermute | solution.py:244
  156.4 3.6 %collective-permute-start.28 = (bf16[160,128]{1,0:T(8,128)(2,1)S(1)}, bf16[160,128]{1,0:T(8,128)(2,1)S(1)}, u32[]{:S(2)}, u32[]{:S(2)}) collective-permute-start(bf16[160,128]{1,0:T(8,128)(2,1)S(1)} %get-tuple-element.81), channel_id=1, source_target_pairs={{0,14},{1,15},{2,12},{3,13},{4,10},{5,11},{6,8},{7,9},{8,6},{9,7},... | collective-permute-start | bytes 122888 | tf_op jit(solution)/shard_map/ppermute | solution.py:244
  163.8 4.4 %collective-permute-done.29.refs_15_ = bf16[160,128]{1,0:T(8,128)(2,1)S(1)} collective-permute-done((bf16[160,128]{1,0:T(8,128)(2,1)S(1)}, bf16[160,128]{1,0:T(8,128)(2,1)S(1)}, u32[]{:S(2)}, u32[]{:S(2)}) %collective-permute-start.29) | collective-permute-done | bytes 40992 | tf_op jit(solution)/shard_map/ppermute | solution.py:244
  168.2 5.0 %collective-permute-start.32 = (f32[16,128]{1,0:T(8,128)S(1)}, f32[16,128]{1,0:T(8,128)S(1)}, u32[]{:S(2)}, u32[]{:S(2)}) collective-permute-start(f32[16,128]{1,0:T(8,128)S(1)} %shard_map.127), channel_id=1, source_target_pairs={{0,48},{16,0},{32,16},{48,32},{64,112},{80,64},{96,80},{112,96},{1... | collective-permute-start | bytes 24584 | tf_op jit(solution)/shard_map/ppermute | solution.py:252
  184.4 8.2 %collective-permute-start.34 = (f32[16,128]{1,0:T(8,128)S(1)}, f32[16,128]{1,0:T(8,128)S(1)}, u32[]{:S(2)}, u32[]{:S(2)}) collective-permute-start(f32[16,128]{1,0:T(8,128)S(1)} %add_add_fusion.1), channel_id=1, source_target_pairs={{0,128},{16,144},{32,160},{48,176},{64,192},{80,208},{96,224},{112... | collective-permute-start | bytes 24584 | tf_op jit(solution)/shard_map/ppermute | solution.py:252
  192.7 4.3 %collective-permute-start.33 = (f32[16,128]{1,0:T(8,128)S(1)}, f32[16,128]{1,0:T(8,128)S(1)}, u32[]{:S(2)}, u32[]{:S(2)}) collective-permute-start(f32[16,128]{1,0:T(8,128)S(1)} %add_add_fusion.1), channel_id=1, source_target_pairs={{0,64},{16,80},{32,96},{48,112},{64,128},{80,144},{96,160},{112,17... | collective-permute-start | bytes 24584 | tf_op jit(solution)/shard_map/ppermute | solution.py:252
  197.7 8.1 %collective-permute-start.37 = (f32[16,128]{1,0:T(8,128)S(1)}, f32[16,128]{1,0:T(8,128)S(1)}, u32[]{:S(2)}, u32[]{:S(2)}) collective-permute-start(f32[16,128]{1,0:T(8,128)S(1)} %add_add_fusion), channel_id=1, source_target_pairs={{0,512},{16,528},{32,544},{48,560},{64,576},{80,592},{96,608},{112... | collective-permute-start | bytes 24584 | tf_op jit(solution)/shard_map/ppermute | solution.py:252
  208.5 8.0 %collective-permute-done.36 = f32[16,128]{1,0:T(8,128)S(1)} collective-permute-done((f32[16,128]{1,0:T(8,128)S(1)}, f32[16,128]{1,0:T(8,128)S(1)}, u32[]{:S(2)}, u32[]{:S(2)}) %collective-permute-start.36) | collective-permute-done | bytes 8224 | tf_op jit(solution)/shard_map/ppermute | solution.py:252
  216.5 7.1 %collective-permute-start.40 = (f32[8,128]{1,0:T(8,128)S(1)}, f32[8,128]{1,0:T(8,128)S(1)}, u32[]{:S(2)}, u32[]{:S(2)}) collective-permute-start(f32[8,128]{1,0:T(8,128)S(1)} %get-tuple-element.84), channel_id=1, source_target_pairs={{0,3},{1,2},{2,1},{3,0},{4,7},{5,6},{6,5},{7,4},{8,11},{9,10},{10,... | collective-permute-start | bytes 12296 | tf_op jit(solution)/shard_map/ppermute | solution.py:244
  229.5 3.4 %collective-permute-start.43 = (f32[32,128]{1,0:T(8,128)S(1)}, f32[32,128]{1,0:T(8,128)S(1)}, u32[]{:S(2)}, u32[]{:S(2)}) collective-permute-start(f32[32,128]{1,0:T(8,128)S(1)} %pad_maximum_fusion), channel_id=1, source_target_pairs={{0,12},{1,13},{2,14},{3,15},{4,8},{5,9},{6,10},{7,11},{8,4},{9,5},... | collective-permute-start | bytes 49160 | tf_op jit(solution)/shard_map/ppermute | solution.py:244
  232.9 5.6 %collective-permute-start.42 = (f32[32,128]{1,0:T(8,128)S(1)}, f32[32,128]{1,0:T(8,128)S(1)}, u32[]{:S(2)}, u32[]{:S(2)}) collective-permute-start(f32[32,128]{1,0:T(8,128)S(1)} %pad_maximum_fusion), channel_id=1, source_target_pairs={{0,8},{1,9},{2,10},{3,11},{4,12},{5,13},{6,14},{7,15},{8,0},{9,1},... | collective-permute-start | bytes 49160 | tf_op jit(solution)/shard_map/ppermute | solution.py:244
  244.6 4.8 %shard_map.126 = bf16[512,128]{1,0:T(8,128)(2,1)} custom-call(s32[4,128]{1,0:T(4,128)S(1)} %bitcast.14, s32[48,128]{1,0:T(8,128)S(1)} %copy-done.13, f32[512,128]{1,0:T(8,128)S(1)} %shard_map.125.near_ref, bf16[48,128,128]{2,1,0:T(8,128)(2,1)} %all-to-all-done.1.recv_ref), custom_call_target="tpu_custom_call" | custom-call | flops 805306368 | bytes 1572864 | tf_op jit(solution)/shard_map/pallas_call | solution.py:363
  (109 shorter events, 65.9 us)
Async XLA Ops:
  6.1 81.3 %all-to-all-start = ((bf16[48,128,128]{2,1,0:T(8,128)(2,1)}), bf16[48,128,128]{2,1,0:T(8,128)(2,1)}, u32[]{:S(2)}, u32[]{:S(2)}) async-start(bf16[48,128,128]{2,1,0:T(8,128)(2,1)} %copy-done.3), calls=%async_computation | async-start | bytes 3145728 | tf_op jit(solution)/shard_map/all_to_all | solution.py:284
  26.2 14.9 %collective-permute-start = (bf16[128,128]{1,0:T(8,128)(2,1)S(1)}, bf16[128,128]{1,0:T(8,128)(2,1)S(1)}, u32[]{:S(2)}, u32[]{:S(2)}) collective-permute-start(bf16[128,128]{1,0:T(8,128)(2,1)S(1)} %get-tuple-element.47), channel_id=1, source_target_pairs={{0,1},{1,0},{2,3},{3,2},{4,5},{5,4},{6,7},{7,6},{8,9},{9,8},{10,11... | collective-permute-start | bytes 98312 | tf_op jit(solution)/shard_map/ppermute | solution.py:244
  29.1 17.3 %collective-permute-start.1 = (bf16[128,128]{1,0:T(8,128)(2,1)S(1)}, bf16[128,128]{1,0:T(8,128)(2,1)S(1)}, u32[]{:S(2)}, u32[]{:S(2)}) collective-permute-start(bf16[128,128]{1,0:T(8,128)(2,1)S(1)} %get-tuple-element.48), channel_id=1, source_target_pairs={{0,2},{1,3},{2,0},{3,1},{4,6},{5,7},{6,4},{7,5},{8,10},{9,11},{10,... | collective-permute-start | bytes 98312 | tf_op jit(solution)/shard_map/ppermute | solution.py:244
  32.3 16.2 %collective-permute-start.2 = (bf16[128,128]{1,0:T(8,128)(2,1)S(1)}, bf16[128,128]{1,0:T(8,128)(2,1)S(1)}, u32[]{:S(2)}, u32[]{:S(2)}) collective-permute-start(bf16[128,128]{1,0:T(8,128)(2,1)S(1)} %get-tuple-element.49), channel_id=1, source_target_pairs={{0,3},{1,2},{2,1},{3,0},{4,7},{5,6},{6,5},{7,4},{8,11},{9,10},{10,... | collective-permute-start | bytes 98312 | tf_op jit(solution)/shard_map/ppermute | solution.py:244
  34.5 21.3 %collective-permute-start.3 = (bf16[128,128]{1,0:T(8,128)(2,1)S(1)}, bf16[128,128]{1,0:T(8,128)(2,1)S(1)}, u32[]{:S(2)}, u32[]{:S(2)}) collective-permute-start(bf16[128,128]{1,0:T(8,128)(2,1)S(1)} %get-tuple-element.50), channel_id=1, source_target_pairs={{0,4},{1,5},{2,6},{3,7},{4,0},{5,1},{6,2},{7,3},{8,12},{9,13},{10,... | collective-permute-start | bytes 98312 | tf_op jit(solution)/shard_map/ppermute | solution.py:244
  38.8 19.3 %collective-permute-start.4 = (bf16[128,128]{1,0:T(8,128)(2,1)S(1)}, bf16[128,128]{1,0:T(8,128)(2,1)S(1)}, u32[]{:S(2)}, u32[]{:S(2)}) collective-permute-start(bf16[128,128]{1,0:T(8,128)(2,1)S(1)} %get-tuple-element.51), channel_id=1, source_target_pairs={{0,5},{1,4},{2,7},{3,6},{4,1},{5,0},{6,3},{7,2},{8,13},{9,12},{10,... | collective-permute-start | bytes 98312 | tf_op jit(solution)/shard_map/ppermute | solution.py:244
  41.1 21.8 %collective-permute-start.5 = (bf16[128,128]{1,0:T(8,128)(2,1)S(1)}, bf16[128,128]{1,0:T(8,128)(2,1)S(1)}, u32[]{:S(2)}, u32[]{:S(2)}) collective-permute-start(bf16[128,128]{1,0:T(8,128)(2,1)S(1)} %get-tuple-element.52), channel_id=1, source_target_pairs={{0,6},{1,7},{2,4},{3,5},{4,2},{5,3},{6,0},{7,1},{8,14},{9,15},{10,... | collective-permute-start | bytes 98312 | tf_op jit(solution)/shard_map/ppermute | solution.py:244
  46.4 20.4 %collective-permute-start.6 = (bf16[128,128]{1,0:T(8,128)(2,1)S(1)}, bf16[128,128]{1,0:T(8,128)(2,1)S(1)}, u32[]{:S(2)}, u32[]{:S(2)}) collective-permute-start(bf16[128,128]{1,0:T(8,128)(2,1)S(1)} %get-tuple-element.53), channel_id=1, source_target_pairs={{0,7},{1,6},{2,5},{3,4},{4,3},{5,2},{6,1},{7,0},{8,15},{9,14},{10,... | collective-permute-start | bytes 98312 | tf_op jit(solution)/shard_map/ppermute | solution.py:244
  48.5 22.1 %collective-permute-start.7 = (bf16[128,128]{1,0:T(8,128)(2,1)S(1)}, bf16[128,128]{1,0:T(8,128)(2,1)S(1)}, u32[]{:S(2)}, u32[]{:S(2)}) collective-permute-start(bf16[128,128]{1,0:T(8,128)(2,1)S(1)} %get-tuple-element.54), channel_id=1, source_target_pairs={{0,8},{1,9},{2,10},{3,11},{4,12},{5,13},{6,14},{7,15},{8,0},{9,1},... | collective-permute-start | bytes 98312 | tf_op jit(solution)/shard_map/ppermute | solution.py:244
  55.9 18.5 %collective-permute-start.8 = (bf16[128,128]{1,0:T(8,128)(2,1)S(1)}, bf16[128,128]{1,0:T(8,128)(2,1)S(1)}, u32[]{:S(2)}, u32[]{:S(2)}) collective-permute-start(bf16[128,128]{1,0:T(8,128)(2,1)S(1)} %get-tuple-element.55), channel_id=1, source_target_pairs={{0,9},{1,8},{2,11},{3,10},{4,13},{5,12},{6,15},{7,14},{8,1},{9,0},... | collective-permute-start | bytes 98312 | tf_op jit(solution)/shard_map/ppermute | solution.py:244
  58.1 21.4 %collective-permute-start.9 = (bf16[128,128]{1,0:T(8,128)(2,1)S(1)}, bf16[128,128]{1,0:T(8,128)(2,1)S(1)}, u32[]{:S(2)}, u32[]{:S(2)}) collective-permute-start(bf16[128,128]{1,0:T(8,128)(2,1)S(1)} %get-tuple-element.56), channel_id=1, source_target_pairs={{0,10},{1,11},{2,8},{3,9},{4,14},{5,15},{6,12},{7,13},{8,2},{9,3},... | collective-permute-start | bytes 98312 | tf_op jit(solution)/shard_map/ppermute | solution.py:244
  62.9 18.5 %collective-permute-start.10 = (bf16[128,128]{1,0:T(8,128)(2,1)S(1)}, bf16[128,128]{1,0:T(8,128)(2,1)S(1)}, u32[]{:S(2)}, u32[]{:S(2)}) collective-permute-start(bf16[128,128]{1,0:T(8,128)(2,1)S(1)} %get-tuple-element.57), channel_id=1, source_target_pairs={{0,11},{1,10},{2,9},{3,8},{4,15},{5,14},{6,13},{7,12},{8,3},{9,2},... | collective-permute-start | bytes 98312 | tf_op jit(solution)/shard_map/ppermute | solution.py:244
  66.8 14.6 %collective-permute-start.11 = (bf16[128,128]{1,0:T(8,128)(2,1)S(1)}, bf16[128,128]{1,0:T(8,128)(2,1)S(1)}, u32[]{:S(2)}, u32[]{:S(2)}) collective-permute-start(bf16[128,128]{1,0:T(8,128)(2,1)S(1)} %get-tuple-element.58), channel_id=1, source_target_pairs={{0,12},{1,13},{2,14},{3,15},{4,8},{5,9},{6,10},{7,11},{8,4},{9,5},... | collective-permute-start | bytes 98312 | tf_op jit(solution)/shard_map/ppermute | solution.py:244
  94.5 150.1 %all-to-all-start.1 = ((bf16[48,128,128]{2,1,0:T(8,128)(2,1)}), bf16[48,128,128]{2,1,0:T(8,128)(2,1)}, u32[]{:S(2)}, u32[]{:S(2)}) async-start(bf16[48,128,128]{2,1,0:T(8,128)(2,1)} %copy-done.2), calls=%async_computation.1 | async-start | bytes 3145728 | tf_op jit(solution)/shard_map/all_to_all | solution.py:319
  108.1 15.1 %collective-permute-start.15 = (bf16[160,128]{1,0:T(8,128)(2,1)S(1)}, bf16[160,128]{1,0:T(8,128)(2,1)S(1)}, u32[]{:S(2)}, u32[]{:S(2)}) collective-permute-start(bf16[160,128]{1,0:T(8,128)(2,1)S(1)} %get-tuple-element.68), channel_id=1, source_target_pairs={{0,1},{1,0},{2,3},{3,2},{4,5},{5,4},{6,7},{7,6},{8,9},{9,8},{10,11... | collective-permute-start | bytes 122888 | tf_op jit(solution)/shard_map/ppermute | solution.py:244
  110.6 17.5 %collective-permute-start.16 = (bf16[160,128]{1,0:T(8,128)(2,1)S(1)}, bf16[160,128]{1,0:T(8,128)(2,1)S(1)}, u32[]{:S(2)}, u32[]{:S(2)}) collective-permute-start(bf16[160,128]{1,0:T(8,128)(2,1)S(1)} %get-tuple-element.69), channel_id=1, source_target_pairs={{0,2},{1,3},{2,0},{3,1},{4,6},{5,7},{6,4},{7,5},{8,10},{9,11},{10,... | collective-permute-start | bytes 122888 | tf_op jit(solution)/shard_map/ppermute | solution.py:244
  114.5 16.1 %collective-permute-start.17 = (bf16[160,128]{1,0:T(8,128)(2,1)S(1)}, bf16[160,128]{1,0:T(8,128)(2,1)S(1)}, u32[]{:S(2)}, u32[]{:S(2)}) collective-permute-start(bf16[160,128]{1,0:T(8,128)(2,1)S(1)} %get-tuple-element.70), channel_id=1, source_target_pairs={{0,3},{1,2},{2,1},{3,0},{4,7},{5,6},{6,5},{7,4},{8,11},{9,10},{10,... | collective-permute-start | bytes 122888 | tf_op jit(solution)/shard_map/ppermute | solution.py:244
  116.4 19.6 %collective-permute-start.18 = (bf16[160,128]{1,0:T(8,128)(2,1)S(1)}, bf16[160,128]{1,0:T(8,128)(2,1)S(1)}, u32[]{:S(2)}, u32[]{:S(2)}) collective-permute-start(bf16[160,128]{1,0:T(8,128)(2,1)S(1)} %get-tuple-element.71), channel_id=1, source_target_pairs={{0,4},{1,5},{2,6},{3,7},{4,0},{5,1},{6,2},{7,3},{8,12},{9,13},{10,... | collective-permute-start | bytes 122888 | tf_op jit(solution)/shard_map/ppermute | solution.py:244
  120.8 19.3 %collective-permute-start.19 = (bf16[160,128]{1,0:T(8,128)(2,1)S(1)}, bf16[160,128]{1,0:T(8,128)(2,1)S(1)}, u32[]{:S(2)}, u32[]{:S(2)}) collective-permute-start(bf16[160,128]{1,0:T(8,128)(2,1)S(1)} %get-tuple-element.72), channel_id=1, source_target_pairs={{0,5},{1,4},{2,7},{3,6},{4,1},{5,0},{6,3},{7,2},{8,13},{9,12},{10,... | collective-permute-start | bytes 122888 | tf_op jit(solution)/shard_map/ppermute | solution.py:244
  123.2 21.1 %collective-permute-start.20 = (bf16[160,128]{1,0:T(8,128)(2,1)S(1)}, bf16[160,128]{1,0:T(8,128)(2,1)S(1)}, u32[]{:S(2)}, u32[]{:S(2)}) collective-permute-start(bf16[160,128]{1,0:T(8,128)(2,1)S(1)} %get-tuple-element.73), channel_id=1, source_target_pairs={{0,6},{1,7},{2,4},{3,5},{4,2},{5,3},{6,0},{7,1},{8,14},{9,15},{10,... | collective-permute-start | bytes 122888 | tf_op jit(solution)/shard_map/ppermute | solution.py:244
  128.1 20.6 %collective-permute-start.21 = (bf16[160,128]{1,0:T(8,128)(2,1)S(1)}, bf16[160,128]{1,0:T(8,128)(2,1)S(1)}, u32[]{:S(2)}, u32[]{:S(2)}) collective-permute-start(bf16[160,128]{1,0:T(8,128)(2,1)S(1)} %get-tuple-element.74), channel_id=1, source_target_pairs={{0,7},{1,6},{2,5},{3,4},{4,3},{5,2},{6,1},{7,0},{8,15},{9,14},{10,... | collective-permute-start | bytes 122888 | tf_op jit(solution)/shard_map/ppermute | solution.py:244
  130.5 20.9 %collective-permute-start.22 = (bf16[160,128]{1,0:T(8,128)(2,1)S(1)}, bf16[160,128]{1,0:T(8,128)(2,1)S(1)}, u32[]{:S(2)}, u32[]{:S(2)}) collective-permute-start(bf16[160,128]{1,0:T(8,128)(2,1)S(1)} %get-tuple-element.75), channel_id=1, source_target_pairs={{0,8},{1,9},{2,10},{3,11},{4,12},{5,13},{6,14},{7,15},{8,0},{9,1},... | collective-permute-start | bytes 122888 | tf_op jit(solution)/shard_map/ppermute | solution.py:244
  136.0 20.4 %collective-permute-start.23 = (bf16[160,128]{1,0:T(8,128)(2,1)S(1)}, bf16[160,128]{1,0:T(8,128)(2,1)S(1)}, u32[]{:S(2)}, u32[]{:S(2)}) collective-permute-start(bf16[160,128]{1,0:T(8,128)(2,1)S(1)} %get-tuple-element.76), channel_id=1, source_target_pairs={{0,9},{1,8},{2,11},{3,10},{4,13},{5,12},{6,15},{7,14},{8,1},{9,0},... | collective-permute-start | bytes 122888 | tf_op jit(solution)/shard_map/ppermute | solution.py:244
  140.1 19.9 %collective-permute-start.24 = (bf16[160,128]{1,0:T(8,128)(2,1)S(1)}, bf16[160,128]{1,0:T(8,128)(2,1)S(1)}, u32[]{:S(2)}, u32[]{:S(2)}) collective-permute-start(bf16[160,128]{1,0:T(8,128)(2,1)S(1)} %get-tuple-element.77), channel_id=1, source_target_pairs={{0,10},{1,11},{2,8},{3,9},{4,14},{5,15},{6,12},{7,13},{8,2},{9,3},... | collective-permute-start | bytes 122888 | tf_op jit(solution)/shard_map/ppermute | solution.py:244
  144.3 18.9 %collective-permute-start.25 = (bf16[160,128]{1,0:T(8,128)(2,1)S(1)}, bf16[160,128]{1,0:T(8,128)(2,1)S(1)}, u32[]{:S(2)}, u32[]{:S(2)}) collective-permute-start(bf16[160,128]{1,0:T(8,128)(2,1)S(1)} %get-tuple-element.78), channel_id=1, source_target_pairs={{0,11},{1,10},{2,9},{3,8},{4,15},{5,14},{6,13},{7,12},{8,3},{9,2},... | collective-permute-start | bytes 122888 | tf_op jit(solution)/shard_map/ppermute | solution.py:244
  148.7 14.5 %collective-permute-start.26 = (bf16[160,128]{1,0:T(8,128)(2,1)S(1)}, bf16[160,128]{1,0:T(8,128)(2,1)S(1)}, u32[]{:S(2)}, u32[]{:S(2)}) collective-permute-start(bf16[160,128]{1,0:T(8,128)(2,1)S(1)} %get-tuple-element.79), channel_id=1, source_target_pairs={{0,12},{1,13},{2,14},{3,15},{4,8},{5,9},{6,10},{7,11},{8,4},{9,5},... | collective-permute-start | bytes 122888 | tf_op jit(solution)/shard_map/ppermute | solution.py:244
  151.4 11.7 %collective-permute-start.27 = (bf16[160,128]{1,0:T(8,128)(2,1)S(1)}, bf16[160,128]{1,0:T(8,128)(2,1)S(1)}, u32[]{:S(2)}, u32[]{:S(2)}) collective-permute-start(bf16[160,128]{1,0:T(8,128)(2,1)S(1)} %get-tuple-element.80), channel_id=1, source_target_pairs={{0,13},{1,12},{2,15},{3,14},{4,9},{5,8},{6,11},{7,10},{8,5},{9,4},... | collective-permute-start | bytes 122888 | tf_op jit(solution)/shard_map/ppermute | solution.py:244
  181.3 15.6 %collective-permute-start.35 = (f32[16,128]{1,0:T(8,128)S(1)}, f32[16,128]{1,0:T(8,128)S(1)}, u32[]{:S(2)}, u32[]{:S(2)}) collective-permute-start(f32[16,128]{1,0:T(8,128)S(1)} %add_add_fusion.1), channel_id=1, source_target_pairs={{0,192},{16,208},{32,224},{48,240},{64,0},{80,16},{96,32},{112,48}... | collective-permute-start | bytes 24584 | tf_op jit(solution)/shard_map/ppermute | solution.py:252
  184.4 12.5 %collective-permute-start.34 = (f32[16,128]{1,0:T(8,128)S(1)}, f32[16,128]{1,0:T(8,128)S(1)}, u32[]{:S(2)}, u32[]{:S(2)}) collective-permute-start(f32[16,128]{1,0:T(8,128)S(1)} %add_add_fusion.1), channel_id=1, source_target_pairs={{0,128},{16,144},{32,160},{48,176},{64,192},{80,208},{96,224},{112... | collective-permute-start | bytes 24584 | tf_op jit(solution)/shard_map/ppermute | solution.py:252
  216.5 12.3 %collective-permute-start.40 = (f32[8,128]{1,0:T(8,128)S(1)}, f32[8,128]{1,0:T(8,128)S(1)}, u32[]{:S(2)}, u32[]{:S(2)}) collective-permute-start(f32[8,128]{1,0:T(8,128)S(1)} %get-tuple-element.84), channel_id=1, source_target_pairs={{0,3},{1,2},{2,1},{3,0},{4,7},{5,6},{6,5},{7,4},{8,11},{9,10},{10,... | collective-permute-start | bytes 12296 | tf_op jit(solution)/shard_map/ppermute | solution.py:244
  229.5 14.5 %collective-permute-start.43 = (f32[32,128]{1,0:T(8,128)S(1)}, f32[32,128]{1,0:T(8,128)S(1)}, u32[]{:S(2)}, u32[]{:S(2)}) collective-permute-start(f32[32,128]{1,0:T(8,128)S(1)} %pad_maximum_fusion), channel_id=1, source_target_pairs={{0,12},{1,13},{2,14},{3,15},{4,8},{5,9},{6,10},{7,11},{8,4},{9,5},... | collective-permute-start | bytes 49160 | tf_op jit(solution)/shard_map/ppermute | solution.py:244
  232.9 11.0 %collective-permute-start.42 = (f32[32,128]{1,0:T(8,128)S(1)}, f32[32,128]{1,0:T(8,128)S(1)}, u32[]{:S(2)}, u32[]{:S(2)}) collective-permute-start(f32[32,128]{1,0:T(8,128)S(1)} %pad_maximum_fusion), channel_id=1, source_target_pairs={{0,8},{1,9},{2,10},{3,11},{4,12},{5,13},{6,14},{7,15},{8,0},{9,1},... | collective-permute-start | bytes 49160 | tf_op jit(solution)/shard_map/ppermute | solution.py:244
  (28 other events, 439.4 us)

commit v2 on v1

--- a/solution.py
+++ b/solution.py
@@ -11,7 +11,6 @@
 TILE = 128
 ROW_TILES = 4
 ROWS = TILE * ROW_TILES
-NODE_DIM, LANE_DIM = 0, 1
 VMEM_LIMIT = 48 * 1024 * 1024
 VMEM = pl.BlockSpec(memory_space=pltpu.VMEM)
 SMEM = pl.BlockSpec(memory_space=pltpu.SMEM)
@@ -74,20 +73,29 @@
 def gather_grp(me_ref, scaled_ref, lists_ref, *out_refs):
     me = me_ref[0]
     scaled = jnp.concatenate([scaled_ref[t] for t in range(ROW_TILES)], axis=1)
-    for k, out_ref in enumerate(out_refs):
-        row = lists_ref[pl.ds(jnp.bitwise_xor(me, k), 1), :]
-        out_ref[...] = mul(scaled, one_hot([row]), NN).astype(jnp.bfloat16)
+    for high, out_ref in enumerate(out_refs):
+        for low in range(out_ref.shape[0]):
+            peer = jnp.bitwise_xor(me, high * out_ref.shape[0] + low)
+            row = lists_ref[pl.ds(peer, 1), :]
+            out_ref[low] = mul(scaled, one_hot([row]), NN).astype(jnp.bfloat16)
+
+
+def regroup(*refs):
+    in_refs, out_refs = refs[: refs[-1].shape[0]], refs[refs[-1].shape[0] :]
+    for high, in_ref in enumerate(in_refs):
+        for low, out_ref in enumerate(out_refs):
+            out_ref[high] = in_ref[low]
 
 
 def near_sum(dom, grp, me_ref, blocks_ref, tiles_ref, scaled_ref, *refs):
-    recv_refs, (out_ref, sources_ref) = refs[:grp], refs[grp:]
+    *recv_refs, out_ref, sources_ref = refs
     me = me_ref[0]
     out_ref[...] = jnp.zeros_like(out_ref)
     for t in range(ROW_TILES):
         sources_ref[t] = scaled_ref[t]
     for k in range(grp):
         peer = jnp.bitwise_xor(me, k)
-        block = recv_refs[k][...]
+        block = recv_refs[k % len(recv_refs)][k // len(recv_refs)]
         sources_ref[ROW_TILES + peer] = block
         row_tile = blocks_ref[0, dom + peer]
         out_ref[row_tile] += mul(tiles_ref[dom + peer], block, NT)
@@ -183,7 +191,8 @@
     bias_rows = jnp.where(
         line == 0, bias_high, jnp.where(line == 1, bias_term - bias_high, 0.0)
     ).astype(jnp.bfloat16)
-    for k, out_ref in enumerate(out_refs):
+    for k in range(grp):
+        out_ref = out_refs[k // out_refs[0].shape[0]].at[k % out_refs[0].shape[0]]
         out_ref[0:TILE, :] = slots_ref[ROW_TILES + k].astype(jnp.bfloat16)
         first = pl.multiple_of(jnp.bitwise_xor(me, k) * depth, depth)
         term = weight_term_ref[pl.ds(first, depth), :]
@@ -197,27 +206,24 @@
     *recv_refs, out_ref = refs
     total = jnp.zeros((2 * depth + 16, TILE), jnp.float32)
     for recv_ref in recv_refs:
-        total += recv_ref[TILE:, :].astype(jnp.float32)
+        for i in range(recv_ref.shape[0]):
+            total += recv_ref[i, TILE:, :].astype(jnp.float32)
     out_ref[0:depth, :] = total[0:depth, :] + total[depth : 2 * depth, :]
     bias_term = total[2 * depth : 2 * depth + 1, :] + total[2 * depth + 1 : 2 * depth + 2, :]
     out_ref[depth:, :] = jnp.broadcast_to(bias_term, (8, TILE))
 
 
-def place_chunks(me_ref, turned_ref, out_ref):
-    for k in range(turned_ref.shape[0]):
-        out_ref[jnp.bitwise_xor(me_ref[0], k)] = turned_ref[k]
-
-
 def near_scatter(me_ref, lists_ref, own_ref, *refs):
     *recv_refs, out_ref = refs
     me = me_ref[0]
-    rows = [lists_ref[pl.ds(jnp.bitwise_xor(me, k), 1), :] for k in range(len(recv_refs))]
+    radix = len(recv_refs)
     total = own_ref[...]
-    step = group(len(recv_refs))
-    for first in range(0, len(recv_refs), step):
-        part = range(first, first + step)
-        blocks = jnp.concatenate([recv_refs[k][0:TILE, :] for k in part], axis=1)
-        total += mul(one_hot([rows[k] for k in part]), blocks, NT)
+    for low, recv_ref in enumerate(recv_refs):
+        count = recv_ref.shape[0]
+        peers = [jnp.bitwise_xor(me, high * radix + low) for high in range(count)]
+        blocks = jnp.concatenate([recv_ref[high, 0:TILE, :] for high in range(count)], axis=1)
+        rows = [lists_ref[pl.ds(peer, 1), :] for peer in peers]
+        total += mul(one_hot(rows), blocks, NT)
     out_ref[...] = total
 
 
@@ -244,21 +250,30 @@
     return lax.ppermute(value, axis, [(i, i ^ k) for i in range(size)])
 
 
-def digit_permute(value, axis, size, stride, radix, k):
-    def target(i):
-        digit = i // stride % radix
-        return i + ((digit + k) % radix - digit) * stride
-
-    return lax.ppermute(value, axis, [(i, target(i)) for i in range(size)])
-
-
-def digits(size):
-    out, stride = [], 1
-    while size > 1:
-        radix = next(r for r in (4, 3, 2, size) if size % r == 0)
-        out.append((stride, radix))
-        stride, size = stride * radix, size // radix
-    return out
+def exchange(parts, grp, radix):
+    shape = parts[0].shape[1:]
+    far = [parts[0]]
+    far += [xor_permute(parts[k], "grp", grp, k * radix) for k in range(1, len(parts))]
+    turned = call(
+        regroup,
+        [jax.ShapeDtypeStruct((len(parts), *shape), parts[0].dtype)] * radix,
+        [VMEM] * len(parts),
+        nbytes=4 * grp * shape[0] * shape[1],
+    )(*far)
+    return [turned[0]] + [xor_permute(turned[k], "grp", grp, k) for k in range(1, radix)]
+
+
+def gathered_sum(value, axis, groups):
+    if len(groups[0]) == 1:
+        return value
+    return jnp.sum(lax.all_gather(value, axis, axis_index_groups=groups), axis=0)
+
+
+def dom_sum(value, dom):
+    inner = 12 if dom % 12 == 0 else dom
+    rows = [[o * inner + i for i in range(inner)] for o in range(dom // inner)]
+    value = gathered_sum(value, "dom", [list(column) for column in zip(*rows)])
+    return gathered_sum(value, "dom", rows)
 
 
 def body(features, degrees, adj_tiles, block_list, send_dom, send_grp, weight, bias_vec, cotangent):
@@ -271,6 +286,7 @@
     degree_rows = degrees.reshape(ROW_TILES, TILE)
     blocks = block_list.T
     bias_row = bias_vec.reshape(1, TILE)
+    radix = 4 if grp % 4 == 0 else 2
     product = 2 * TILE**3
     block_bytes = 2 * TILE * TILE
 
@@ -284,16 +300,16 @@
     from_dom = lax.all_to_all(to_dom, "dom", split_axis=0, concat_axis=0, tiled=True)
     to_grp = call(
         gather_grp,
-        [shape((TILE, TILE), bf16)] * grp,
+        [shape((radix, TILE, TILE), bf16)] * (grp // radix),
         [SMEM, VMEM, VMEM],
         flops=4 * grp * product,
         nbytes=grp * block_bytes,
     )(me, scaled, send_grp)
-    from_grp = [to_grp[0]] + [xor_permute(to_grp[k], "grp", grp, k) for k in range(1, grp)]
+    from_grp = exchange(to_grp, grp, radix)
     near = call(
         functools.partial(near_sum, dom, grp),
         shape((ROW_TILES + 1, TILE, TILE), f32),
-        [SMEM, SMEM] + [VMEM] * (2 + grp),
+        [SMEM, SMEM] + [VMEM] * (2 + radix),
         [pltpu.VMEM((ROW_TILES + grp, TILE, TILE), bf16)],
         flops=(entries - dom) * product,
         nbytes=entries * block_bytes,
@@ -321,42 +337,31 @@
     depth = TILE // grp
     own, *to_near = call(
         functools.partial(near_back, dom, grp),
-        [shape((ROWS, TILE), f32)] + [shape((TILE + 2 * depth + 16, TILE), bf16)] * grp,
+        [shape((ROWS, TILE), f32)] + [shape((radix, TILE + 2 * depth + 16, TILE), bf16)] * (grp // radix),
         [SMEM, SMEM] + [VMEM] * 4,
         [pltpu.VMEM((ROW_TILES + grp + 1, TILE, TILE), f32)],
         flops=(entries - dom) * product,
         nbytes=entries * block_bytes,
     )(me, blocks, adj_tiles, back, weight_term, bias_term)
-    returned_grp = [to_near[0]] + [xor_permute(to_near[k], "grp", grp, k) for k in range(1, grp)]
-
-    grad_scale = 1.0 / math.sqrt(ROWS * dom * grp)
+    returned_grp = exchange(to_near, grp, radix)
+
     chunk = call(
         functools.partial(sum_terms, depth),
         shape((depth + 8, TILE), f32),
-        [VMEM] * grp,
+        [VMEM] * radix,
         nbytes=grp * block_bytes,
     )(*returned_grp)
-    for stride, radix in digits(dom):
-        chunk = chunk + sum(
-            digit_permute(chunk, "dom", dom, stride, radix, k) for k in range(1, radix)
-        )
-    chunk = chunk * grad_scale
+    chunk = dom_sum(chunk, dom) * (1.0 / math.sqrt(ROWS * dom * grp))
+    chunk, returned_dom = lax.optimization_barrier((chunk, returned_dom))
     grad_bias = chunk[depth]
-    gathered = chunk[:depth]
-    for stride, radix in digits(grp):
-        gathered = jnp.concatenate(
-            [gathered]
-            + [xor_permute(gathered, "grp", grp, k * stride) for k in range(1, radix)]
-        )
-    turned = gathered.reshape(grp, depth, TILE)
-    grad_weight = call(
-        place_chunks, shape((grp, depth, TILE), f32), [SMEM, VMEM], nbytes=2 * 4 * TILE * TILE
-    )(me, turned).reshape(TILE, TILE)
+    copies = jnp.broadcast_to(chunk[:depth], (grp, depth, TILE))
+    grad_weight = lax.all_to_all(copies, "grp", split_axis=0, concat_axis=0, tiled=True)
+    grad_weight = grad_weight.reshape(TILE, TILE)
 
     near_grad = call(
         near_scatter,
         shape((ROWS, TILE), f32),
-        [SMEM] + [VMEM] * (2 + grp),
+        [SMEM] + [VMEM] * (2 + radix),
         flops=4 * grp * product,
         nbytes=grp * block_bytes,
     )(me, send_grp, own, *returned_grp)

time: 253 us -> 191 us (0.75)
  starting transfers between devices: 200 us -> 84.9 us
  blocking collectives: 0 us -> 28.9 us
  waiting for transfers between devices: 25.6 us -> 51.8 us
    ppermute x36 -> x12, starting transfers between devices: 133 us -> 40 us  [xor_permute(): return lax.ppermute(value, axis, [(i, i ^ k) for i in range(size)])]
    ppermute x8 -> x0, starting transfers between devices: 35 us -> none  [digit_permute(): return lax.ppermute(value, axis, [(i, target(i)) for i in range(size)])]
    all_gather x0 -> x2, blocking collectives: none -> 28.9 us  [gathered_sum(): lax.all_gather(value, axis, axis_index_groups=groups)]
    ppermute x36 -> x12, waiting for transfers between devices: 13.1 us -> 35.2 us  [xor_permute(): return lax.ppermute(value, axis, [(i, i ^ k) for i in range(size)])]
    all_to_all x1, waiting for transfers between devices: 0.01 us -> 14.1 us  [body(): lax.all_to_all(to_dom, 'dom', split_axis=0, concat_axis=0, tiled=True)]
    all_to_all x0 -> x1, starting transfers between devices: none -> 13.2 us  [body(): lax.all_to_all(copies, 'grp', split_axis=0, concat_axis=0, tiled=True)]
    ppermute x8 -> x0, waiting for transfers between devices: 12.5 us -> none  [digit_permute(): return lax.ppermute(value, axis, [(i, target(i)) for i in range(size)])]
    unnamed x33 -> x29, local copies, waits for them, and re-layouts: 4.67 us -> 5.27 us
  transfers between devices with their start and end apart: 46 -> 15, of which waited for: 9 -> 10; matrix products, arithmetic and copies ran while one was open for 0% -> 0% of each run, Pallas kernels for 2% -> 5%
where the time goes in v2:
time: 191 us; the launch traced here: 190 us
  starting transfers between devices  84.9 us (44%)
  waiting for transfers between devices  51.8 us (27%)
  blocking collectives  28.9 us (15%)
  Pallas kernels  16.8 us (9%)
  local copies, waits for them, and re-layouts  6.42 us (3%)
    ppermute x12, starting transfers between devices, xor_permute(): return lax.ppermute(value, axis, [(i, i ^ k) for i in range(size)])  40 us
    ppermute x12, waiting for transfers between devices, xor_permute(): return lax.ppermute(value, axis, [(i, i ^ k) for i in range(size)])  35.2 us
    all_gather x2, blocking collectives, gathered_sum(): lax.all_gather(value, axis, axis_index_groups=groups)  28.9 us
    all_to_all x1, starting transfers between devices, body(): lax.all_to_all(to_dom, 'dom', split_axis=0, concat_axis=0, tiled=True)  19.3 us
    all_to_all x1, waiting for transfers between devices, body(): lax.all_to_all(to_dom, 'dom', split_axis=0, concat_axis=0, tiled=True)  14.1 us
    all_to_all x1, starting transfers between devices, body(): lax.all_to_all(copies, 'grp', split_axis=0, concat_axis=0, tiled=True)  13.2 us
    all_to_all x1, starting transfers between devices, body(): lax.all_to_all(to_lender, 'dom', split_axis=0, concat_axis=0, tiled=True)  12.4 us
    pallas_call x1, Pallas kernels, body(): call(functools.partial(layer, dom, grp), (shape((ROWS, TILE), bf16), shap...  5.83 us
  transfers between devices with their start and end apart: 15, of which 10 were waited for; matrix products, arithmetic and copies ran while one was open for 0% of the time, Pallas kernels for 5%

profile of v2, /device:TPU:1, one launch (start us, length us, event | category | flops | bytes accessed | tf_op | source)
XLA Modules:
  0.0 189.8 jit_solution(6386215012065714324)
XLA Ops:
  3.0 2.0 %shard_map.120 = (bf16[48,128,128]{2,1,0:T(8,128)(2,1)S(1)}, bf16[4,128,128]{2,1,0:T(8,128)(2,1)S(1)}) custom-call(s32[4,128]{1,0:T(4,128)S(1)} %bitcast.12, bf16[512,128]{1,0:T(8,128)(2,1)S(1)} %copy-done.11, s32[48,128]{1,0:T(8,128)S(1)} %copy-done.12), custom_call_target="tpu_custom_call" | custom-call | flops 805306368 | bytes 1572864 | tf_op jit(solution)/shard_map/pallas_call | solution.py:293
  6.1 19.3 %all-to-all-start = ((bf16[48,128,128]{2,1,0:T(8,128)(2,1)}), bf16[48,128,128]{2,1,0:T(8,128)(2,1)}, u32[]{:S(2)}, u32[]{:S(2)}) async-start(bf16[48,128,128]{2,1,0:T(8,128)(2,1)} %copy-done.3), calls=%async_computation | async-start | bytes 3145728 | tf_op jit(solution)/shard_map/all_to_all | solution.py:300
  26.2 4.2 %collective-permute-start = (bf16[4,128,128]{2,1,0:T(8,128)(2,1)S(1)}, bf16[4,128,128]{2,1,0:T(8,128)(2,1)S(1)}, u32[]{:S(2)}, u32[]{:S(2)}) collective-permute-start(bf16[4,128,128]{2,1,0:T(8,128)(2,1)S(1)} %get-tuple-element.33), channel_id=1, source_target_pairs={{0,4},{1,5},{2,6},{3,7},{4,0},{5,1},{6,2},{7,3},{8,12},{9,13},{10,... | collective-permute-start | bytes 393224 | tf_op jit(solution)/shard_map/ppermute | solution.py:250
  30.4 5.7 %collective-permute-start.1 = (bf16[4,128,128]{2,1,0:T(8,128)(2,1)S(1)}, bf16[4,128,128]{2,1,0:T(8,128)(2,1)S(1)}, u32[]{:S(2)}, u32[]{:S(2)}) collective-permute-start(bf16[4,128,128]{2,1,0:T(8,128)(2,1)S(1)} %get-tuple-element.34), channel_id=1, source_target_pairs={{0,8},{1,9},{2,10},{3,11},{4,12},{5,13},{6,14},{7,15},{8,0},{9,1},... | collective-permute-start | bytes 393224 | tf_op jit(solution)/shard_map/ppermute | solution.py:250
  36.1 1.9 %collective-permute-start.2 = (bf16[4,128,128]{2,1,0:T(8,128)(2,1)S(1)}, bf16[4,128,128]{2,1,0:T(8,128)(2,1)S(1)}, u32[]{:S(2)}, u32[]{:S(2)}) collective-permute-start(bf16[4,128,128]{2,1,0:T(8,128)(2,1)S(1)} %get-tuple-element.35), channel_id=1, source_target_pairs={{0,12},{1,13},{2,14},{3,15},{4,8},{5,9},{6,10},{7,11},{8,4},{9,5},... | collective-permute-start | bytes 393224 | tf_op jit(solution)/shard_map/ppermute | solution.py:250
  38.0 2.5 %collective-permute-done.1.refs_2_ = bf16[4,128,128]{2,1,0:T(8,128)(2,1)S(1)} collective-permute-done((bf16[4,128,128]{2,1,0:T(8,128)(2,1)S(1)}, bf16[4,128,128]{2,1,0:T(8,128)(2,1)S(1)}, u32[]{:S(2)}, u32[]{:S(2)}) %collective-permute-start.1) | collective-permute-done | bytes 131104 | tf_op jit(solution)/shard_map/ppermute | solution.py:250
  40.5 7.5 %collective-permute-done.2.refs_3_ = bf16[4,128,128]{2,1,0:T(8,128)(2,1)S(1)} collective-permute-done((bf16[4,128,128]{2,1,0:T(8,128)(2,1)S(1)}, bf16[4,128,128]{2,1,0:T(8,128)(2,1)S(1)}, u32[]{:S(2)}, u32[]{:S(2)}) %collective-permute-start.2) | collective-permute-done | bytes 131104 | tf_op jit(solution)/shard_map/ppermute | solution.py:250
  48.0 2.4 %collective-permute-start.3 = (bf16[4,128,128]{2,1,0:T(8,128)(2,1)S(1)}, bf16[4,128,128]{2,1,0:T(8,128)(2,1)S(1)}, u32[]{:S(2)}, u32[]{:S(2)}) collective-permute-start(bf16[4,128,128]{2,1,0:T(8,128)(2,1)S(1)} %get-tuple-element.37), channel_id=1, source_target_pairs={{0,1},{1,0},{2,3},{3,2},{4,5},{5,4},{6,7},{7,6},{8,9},{9,8},{10,11... | collective-permute-start | bytes 393224 | tf_op jit(solution)/shard_map/ppermute | solution.py:250
  50.4 4.2 %collective-permute-start.4 = (bf16[4,128,128]{2,1,0:T(8,128)(2,1)S(1)}, bf16[4,128,128]{2,1,0:T(8,128)(2,1)S(1)}, u32[]{:S(2)}, u32[]{:S(2)}) collective-permute-start(bf16[4,128,128]{2,1,0:T(8,128)(2,1)S(1)} %get-tuple-element.38), channel_id=1, source_target_pairs={{0,2},{1,3},{2,0},{3,1},{4,6},{5,7},{6,4},{7,5},{8,10},{9,11},{10,... | collective-permute-start | bytes 393224 | tf_op jit(solution)/shard_map/ppermute | solution.py:250
  54.6 1.9 %collective-permute-start.5 = (bf16[4,128,128]{2,1,0:T(8,128)(2,1)S(1)}, bf16[4,128,128]{2,1,0:T(8,128)(2,1)S(1)}, u32[]{:S(2)}, u32[]{:S(2)}) collective-permute-start(bf16[4,128,128]{2,1,0:T(8,128)(2,1)S(1)} %get-tuple-element.39), channel_id=1, source_target_pairs={{0,3},{1,2},{2,1},{3,0},{4,7},{5,6},{6,5},{7,4},{8,11},{9,10},{10,... | collective-permute-start | bytes 393224 | tf_op jit(solution)/shard_map/ppermute | solution.py:250
  56.6 2.0 %collective-permute-done.4.refs_2_ = bf16[4,128,128]{2,1,0:T(8,128)(2,1)S(1)} collective-permute-done((bf16[4,128,128]{2,1,0:T(8,128)(2,1)S(1)}, bf16[4,128,128]{2,1,0:T(8,128)(2,1)S(1)}, u32[]{:S(2)}, u32[]{:S(2)}) %collective-permute-start.4) | collective-permute-done | bytes 131104 | tf_op jit(solution)/shard_map/ppermute | solution.py:250
  58.6 3.7 %collective-permute-done.5.refs_3_ = bf16[4,128,128]{2,1,0:T(8,128)(2,1)S(1)} collective-permute-done((bf16[4,128,128]{2,1,0:T(8,128)(2,1)S(1)}, bf16[4,128,128]{2,1,0:T(8,128)(2,1)S(1)}, u32[]{:S(2)}, u32[]{:S(2)}) %collective-permute-start.5) | collective-permute-done | bytes 131104 | tf_op jit(solution)/shard_map/ppermute | solution.py:250
  62.4 1.5 shard_map.123.near_ref
  63.8 14.1 %all-to-all-done.recv_ref = bf16[48,128,128]{2,1,0:T(8,128)(2,1)} async-done(((bf16[48,128,128]{2,1,0:T(8,128)(2,1)}), bf16[48,128,128]{2,1,0:T(8,128)(2,1)}, u32[]{:S(2)}, u32[]{:S(2)}) %all-to-all-start) | async-done | bytes 1572896 | tf_op jit(solution)/shard_map/all_to_all | solution.py:300
  78.0 5.8 %shard_map.124 = (bf16[512,128]{1,0:T(8,128)(2,1)}, bf16[48,128,128]{2,1,0:T(8,128)(2,1)S(1)}, bf16[5,128,128]{2,1,0:T(8,128)(2,1)S(1)}, f32[128,128]{1,0:T(8,128)S(1)}, f32[1,128]{1,0:T(1,128)S(1)}) custom-call(s32[2,80]{1,0:T(2,128)S(1)} %bitcast.10, s32[4,128]{1,0:T(4,128)S(1)} %bitcast.13, bf16[80,128,128]{2,1,0:T(8,128)(2,1)} %tiles_ref.5, ...), custom_call_target="tpu_custom_call" | custom-call | flops 671088640 | bytes 7864320 | tf_op jit(solution)/shard_map/pallas_call | solution.py:318
  83.8 1.1 copy-done.2
  85.0 12.4 %all-to-all-start.1 = ((bf16[48,128,128]{2,1,0:T(8,128)(2,1)}), bf16[48,128,128]{2,1,0:T(8,128)(2,1)}, u32[]{:S(2)}, u32[]{:S(2)}) async-start(bf16[48,128,128]{2,1,0:T(8,128)(2,1)} %copy-done.2), calls=%async_computation.1 | async-start | bytes 3145728 | tf_op jit(solution)/shard_map/all_to_all | solution.py:335
  98.5 4.2 %collective-permute-start.6 = (bf16[4,160,128]{2,1,0:T(8,128)(2,1)S(1)}, bf16[4,160,128]{2,1,0:T(8,128)(2,1)S(1)}, u32[]{:S(2)}, u32[]{:S(2)}) collective-permute-start(bf16[4,160,128]{2,1,0:T(8,128)(2,1)S(1)} %get-tuple-element.46), channel_id=1, source_target_pairs={{0,4},{1,5},{2,6},{3,7},{4,0},{5,1},{6,2},{7,3},{8,12},{9,13},{10,... | collective-permute-start | bytes 491528 | tf_op jit(solution)/shard_map/ppermute | solution.py:250
  102.7 5.7 %collective-permute-start.7 = (bf16[4,160,128]{2,1,0:T(8,128)(2,1)S(1)}, bf16[4,160,128]{2,1,0:T(8,128)(2,1)S(1)}, u32[]{:S(2)}, u32[]{:S(2)}) collective-permute-start(bf16[4,160,128]{2,1,0:T(8,128)(2,1)S(1)} %get-tuple-element.47), channel_id=1, source_target_pairs={{0,8},{1,9},{2,10},{3,11},{4,12},{5,13},{6,14},{7,15},{8,0},{9,1},... | collective-permute-start | bytes 491528 | tf_op jit(solution)/shard_map/ppermute | solution.py:250
  108.4 1.9 %collective-permute-start.8 = (bf16[4,160,128]{2,1,0:T(8,128)(2,1)S(1)}, bf16[4,160,128]{2,1,0:T(8,128)(2,1)S(1)}, u32[]{:S(2)}, u32[]{:S(2)}) collective-permute-start(bf16[4,160,128]{2,1,0:T(8,128)(2,1)S(1)} %get-tuple-element.48), channel_id=1, source_target_pairs={{0,12},{1,13},{2,14},{3,15},{4,8},{5,9},{6,10},{7,11},{8,4},{9,5},... | collective-permute-start | bytes 491528 | tf_op jit(solution)/shard_map/ppermute | solution.py:250
  110.3 3.4 %collective-permute-done.7.refs_2_ = bf16[4,160,128]{2,1,0:T(8,128)(2,1)S(1)} collective-permute-done((bf16[4,160,128]{2,1,0:T(8,128)(2,1)S(1)}, bf16[4,160,128]{2,1,0:T(8,128)(2,1)S(1)}, u32[]{:S(2)}, u32[]{:S(2)}) %collective-permute-start.7) | collective-permute-done | bytes 163872 | tf_op jit(solution)/shard_map/ppermute | solution.py:250
  113.8 10.2 %collective-permute-done.8.refs_3_ = bf16[4,160,128]{2,1,0:T(8,128)(2,1)S(1)} collective-permute-done((bf16[4,160,128]{2,1,0:T(8,128)(2,1)S(1)}, bf16[4,160,128]{2,1,0:T(8,128)(2,1)S(1)}, u32[]{:S(2)}, u32[]{:S(2)}) %collective-permute-start.8) | collective-permute-done | bytes 163872 | tf_op jit(solution)/shard_map/ppermute | solution.py:250
  124.0 2.4 %collective-permute-start.9 = (bf16[4,160,128]{2,1,0:T(8,128)(2,1)S(1)}, bf16[4,160,128]{2,1,0:T(8,128)(2,1)S(1)}, u32[]{:S(2)}, u32[]{:S(2)}) collective-permute-start(bf16[4,160,128]{2,1,0:T(8,128)(2,1)S(1)} %get-tuple-element.50), channel_id=1, source_target_pairs={{0,1},{1,0},{2,3},{3,2},{4,5},{5,4},{6,7},{7,6},{8,9},{9,8},{10,11... | collective-permute-start | bytes 491528 | tf_op jit(solution)/shard_map/ppermute | solution.py:250
  126.4 2.5 %collective-permute-start.10 = (bf16[4,160,128]{2,1,0:T(8,128)(2,1)S(1)}, bf16[4,160,128]{2,1,0:T(8,128)(2,1)S(1)}, u32[]{:S(2)}, u32[]{:S(2)}) collective-permute-start(bf16[4,160,128]{2,1,0:T(8,128)(2,1)S(1)} %get-tuple-element.51), channel_id=1, source_target_pairs={{0,2},{1,3},{2,0},{3,1},{4,6},{5,7},{6,4},{7,5},{8,10},{9,11},{10,... | collective-permute-start | bytes 491528 | tf_op jit(solution)/shard_map/ppermute | solution.py:250
  128.9 3.0 %collective-permute-start.11 = (bf16[4,160,128]{2,1,0:T(8,128)(2,1)S(1)}, bf16[4,160,128]{2,1,0:T(8,128)(2,1)S(1)}, u32[]{:S(2)}, u32[]{:S(2)}) collective-permute-start(bf16[4,160,128]{2,1,0:T(8,128)(2,1)S(1)} %get-tuple-element.52), channel_id=1, source_target_pairs={{0,3},{1,2},{2,1},{3,0},{4,7},{5,6},{6,5},{7,4},{8,11},{9,10},{10,... | collective-permute-start | bytes 491528 | tf_op jit(solution)/shard_map/ppermute | solution.py:250
  131.9 2.3 %collective-permute-done.10.refs_2_ = bf16[4,160,128]{2,1,0:T(8,128)(2,1)S(1)} collective-permute-done((bf16[4,160,128]{2,1,0:T(8,128)(2,1)S(1)}, bf16[4,160,128]{2,1,0:T(8,128)(2,1)S(1)}, u32[]{:S(2)}, u32[]{:S(2)}) %collective-permute-start.10) | collective-permute-done | bytes 163872 | tf_op jit(solution)/shard_map/ppermute | solution.py:250
  134.2 3.5 %collective-permute-done.11.refs_3_ = bf16[4,160,128]{2,1,0:T(8,128)(2,1)S(1)} collective-permute-done((bf16[4,160,128]{2,1,0:T(8,128)(2,1)S(1)}, bf16[4,160,128]{2,1,0:T(8,128)(2,1)S(1)}, u32[]{:S(2)}, u32[]{:S(2)}) %collective-permute-start.11) | collective-permute-done | bytes 163872 | tf_op jit(solution)/shard_map/ppermute | solution.py:250
  137.8 10.3 %all-gather = f32[64,128]{1,0:T(8,128)S(1)} all-gather(f32[16,128]{1,0:T(8,128)S(1)} %shard_map.128), channel_id=2, replica_groups={{0,192,384,576},{16,208,400,592},{32,224,416,608},{48,240,432,624},{64,..., dimensions={0}, use_global_device_ids=true | all-gather | bytes 40960 | tf_op jit(solution)/shard_map/all_gather | solution.py:269
  148.1 18.6 %all-gather.1 = f32[192,128]{1,0:T(8,128)S(1)} all-gather(f32[16,128]{1,0:T(8,128)S(1)} %reduce_sum.18), channel_id=3, replica_groups={{0,16,32,48,64,80,96,112,128,144,160,176},{192,208,224,240,256,272,288,..., dimensions={0}, use_global_device_ids=true | all-gather | bytes 106496 | tf_op jit(solution)/shard_map/all_gather | solution.py:269
  168.1 13.2 %all-to-all-start.2 = ((f32[16,8,128]{2,1,0:T(8,128)}), f32[16,8,128]{2,1,0:T(8,128)S(1)}, u32[]{:S(2)}, u32[]{:S(2)}) async-start(f32[16,8,128]{2,1,0:T(8,128)} %broadcast_in_dim.3), calls=%async_computation.2 | async-start | bytes 131072 | tf_op jit(solution)/shard_map/all_to_all | solution.py:358
  181.9 4.8 %shard_map.129 = bf16[512,128]{1,0:T(8,128)(2,1)} custom-call(s32[4,128]{1,0:T(4,128)S(1)} %bitcast.14, s32[48,128]{1,0:T(8,128)S(1)} %copy-done.13, f32[512,128]{1,0:T(8,128)S(1)} %shard_map.127.near_ref, bf16[48,128,128]{2,1,0:T(8,128)(2,1)} %all-to-all-done.1.recv_ref), custom_call_target="tpu_custom_call" | custom-call | flops 805306368 | bytes 1572864 | tf_op jit(solution)/shard_map/pallas_call | solution.py:368
  186.7 2.5 %all-to-all-done.2 = f32[16,8,128]{2,1,0:T(8,128)S(1)} async-done(((f32[16,8,128]{2,1,0:T(8,128)}), f32[16,8,128]{2,1,0:T(8,128)S(1)}, u32[]{:S(2)}, u32[]{:S(2)}) %all-to-all-start.2) | async-done | bytes 65568 | tf_op jit(solution)/shard_map/all_to_all | solution.py:358
  (45 shorter events, 8.0 us)
Async XLA Ops:
  0.6 0.7 copy-start.8
  1.3 0.9 copy-start.11
  2.2 0.7 copy-start.12
  5.0 1.1 copy-start.3
  6.1 19.3 %copy-start.7 = (s32[16,128]{1,0:T(8,128)S(1)}, s32[16,128]{1,0:T(8,128)}, u32[]{:S(2)}) copy-start(s32[16,128]{1,0:T(8,128)} %lists_ref.6) | copy-start | bytes 24580
  6.1 56.2 %copy-start = (bf16[80,128,128]{2,1,0:T(8,128)(2,1)S(1)}, bf16[80,128,128]{2,1,0:T(8,128)(2,1)}, u32[]{:S(2)}) copy-start(bf16[80,128,128]{2,1,0:T(8,128)(2,1)} %tiles_ref.5) | copy-start | bytes 7864324
  6.1 56.2 %copy-start.6 = (s32[80,2]{0,1:T(2,128)S(1)}, s32[80,2]{0,1:T(2,128)}, u32[]{:S(2)}) copy-start(s32[80,2]{0,1:T(2,128)} %param.12) | copy-start | bytes 1924
  6.1 71.8 %all-to-all-start = ((bf16[48,128,128]{2,1,0:T(8,128)(2,1)}), bf16[48,128,128]{2,1,0:T(8,128)(2,1)}, u32[]{:S(2)}, u32[]{:S(2)}) async-start(bf16[48,128,128]{2,1,0:T(8,128)(2,1)} %copy-done.3), calls=%async_computation | async-start | bytes 3145728 | tf_op jit(solution)/shard_map/all_to_all | solution.py:300
  26.2 11.8 %collective-permute-start = (bf16[4,128,128]{2,1,0:T(8,128)(2,1)S(1)}, bf16[4,128,128]{2,1,0:T(8,128)(2,1)S(1)}, u32[]{:S(2)}, u32[]{:S(2)}) collective-permute-start(bf16[4,128,128]{2,1,0:T(8,128)(2,1)S(1)} %get-tuple-element.33), channel_id=1, source_target_pairs={{0,4},{1,5},{2,6},{3,7},{4,0},{5,1},{6,2},{7,3},{8,12},{9,13},{10,... | collective-permute-start | bytes 393224 | tf_op jit(solution)/shard_map/ppermute | solution.py:250
  30.4 10.1 %collective-permute-start.1 = (bf16[4,128,128]{2,1,0:T(8,128)(2,1)S(1)}, bf16[4,128,128]{2,1,0:T(8,128)(2,1)S(1)}, u32[]{:S(2)}, u32[]{:S(2)}) collective-permute-start(bf16[4,128,128]{2,1,0:T(8,128)(2,1)S(1)} %get-tuple-element.34), channel_id=1, source_target_pairs={{0,8},{1,9},{2,10},{3,11},{4,12},{5,13},{6,14},{7,15},{8,0},{9,1},... | collective-permute-start | bytes 393224 | tf_op jit(solution)/shard_map/ppermute | solution.py:250
  36.1 11.9 %collective-permute-start.2 = (bf16[4,128,128]{2,1,0:T(8,128)(2,1)S(1)}, bf16[4,128,128]{2,1,0:T(8,128)(2,1)S(1)}, u32[]{:S(2)}, u32[]{:S(2)}) collective-permute-start(bf16[4,128,128]{2,1,0:T(8,128)(2,1)S(1)} %get-tuple-element.35), channel_id=1, source_target_pairs={{0,12},{1,13},{2,14},{3,15},{4,8},{5,9},{6,10},{7,11},{8,4},{9,5},... | collective-permute-start | bytes 393224 | tf_op jit(solution)/shard_map/ppermute | solution.py:250
  48.0 8.6 %collective-permute-start.3 = (bf16[4,128,128]{2,1,0:T(8,128)(2,1)S(1)}, bf16[4,128,128]{2,1,0:T(8,128)(2,1)S(1)}, u32[]{:S(2)}, u32[]{:S(2)}) collective-permute-start(bf16[4,128,128]{2,1,0:T(8,128)(2,1)S(1)} %get-tuple-element.37), channel_id=1, source_target_pairs={{0,1},{1,0},{2,3},{3,2},{4,5},{5,4},{6,7},{7,6},{8,9},{9,8},{10,11... | collective-permute-start | bytes 393224 | tf_op jit(solution)/shard_map/ppermute | solution.py:250
  50.4 8.2 %collective-permute-start.4 = (bf16[4,128,128]{2,1,0:T(8,128)(2,1)S(1)}, bf16[4,128,128]{2,1,0:T(8,128)(2,1)S(1)}, u32[]{:S(2)}, u32[]{:S(2)}) collective-permute-start(bf16[4,128,128]{2,1,0:T(8,128)(2,1)S(1)} %get-tuple-element.38), channel_id=1, source_target_pairs={{0,2},{1,3},{2,0},{3,1},{4,6},{5,7},{6,4},{7,5},{8,10},{9,11},{10,... | collective-permute-start | bytes 393224 | tf_op jit(solution)/shard_map/ppermute | solution.py:250
  54.6 7.7 %collective-permute-start.5 = (bf16[4,128,128]{2,1,0:T(8,128)(2,1)S(1)}, bf16[4,128,128]{2,1,0:T(8,128)(2,1)S(1)}, u32[]{:S(2)}, u32[]{:S(2)}) collective-permute-start(bf16[4,128,128]{2,1,0:T(8,128)(2,1)S(1)} %get-tuple-element.39), channel_id=1, source_target_pairs={{0,3},{1,2},{2,1},{3,0},{4,7},{5,6},{6,5},{7,4},{8,11},{9,10},{10,... | collective-permute-start | bytes 393224 | tf_op jit(solution)/shard_map/ppermute | solution.py:250
  62.3 15.7 %copy-start.4 = (bf16[512,128]{1,0:T(8,128)(2,1)S(1)}, bf16[512,128]{1,0:T(8,128)(2,1)}, u32[]{:S(2)}) copy-start(bf16[512,128]{1,0:T(8,128)(2,1)} %cotangent_ref.1) | copy-start | bytes 393220
  62.3 15.7 %copy-start.5 = (bf16[128,128]{1,0:T(8,128)(2,1)S(1)}, bf16[128,128]{1,0:T(8,128)(2,1)}, u32[]{:S(2)}) copy-start(bf16[128,128]{1,0:T(8,128)(2,1)} %weight_ref.1) | copy-start | bytes 98308
  62.3 15.6 %copy-start.9 = (s32[512]{0:T(512)S(1)}, s32[512]{0:T(512)}, u32[]{:S(2)}) copy-start(s32[512]{0:T(512)} %param.10) | copy-start | bytes 6148
  62.3 15.6 %copy-start.10 = (f32[128]{0:T(128)S(1)}, f32[128]{0:T(128)}, u32[]{:S(2)}) copy-start(f32[128]{0:T(128)} %param.16) | copy-start | bytes 1540
  83.8 1.1 copy-start.2
  85.0 12.4 %copy-start.1 = (bf16[80,128,128]{2,1,0:T(8,128)(2,1)S(1)}, bf16[80,128,128]{2,1,0:T(8,128)(2,1)}, u32[]{:S(2)}) copy-start(bf16[80,128,128]{2,1,0:T(8,128)(2,1)} %tiles_ref.5) | copy-start | bytes 7864324
  85.0 82.5 %all-to-all-start.1 = ((bf16[48,128,128]{2,1,0:T(8,128)(2,1)}), bf16[48,128,128]{2,1,0:T(8,128)(2,1)}, u32[]{:S(2)}, u32[]{:S(2)}) async-start(bf16[48,128,128]{2,1,0:T(8,128)(2,1)} %copy-done.2), calls=%async_computation.1 | async-start | bytes 3145728 | tf_op jit(solution)/shard_map/all_to_all | solution.py:335
  98.5 83.4 %copy-start.13 = (s32[48,128]{1,0:T(8,128)S(1)}, s32[48,128]{1,0:T(8,128)}, u32[]{:S(2)}) copy-start(s32[48,128]{1,0:T(8,128)} %lists_ref.7) | copy-start | bytes 73732
  98.5 11.8 %collective-permute-start.6 = (bf16[4,160,128]{2,1,0:T(8,128)(2,1)S(1)}, bf16[4,160,128]{2,1,0:T(8,128)(2,1)S(1)}, u32[]{:S(2)}, u32[]{:S(2)}) collective-permute-start(bf16[4,160,128]{2,1,0:T(8,128)(2,1)S(1)} %get-tuple-element.46), channel_id=1, source_target_pairs={{0,4},{1,5},{2,6},{3,7},{4,0},{5,1},{6,2},{7,3},{8,12},{9,13},{10,... | collective-permute-start | bytes 491528 | tf_op jit(solution)/shard_map/ppermute | solution.py:250
  102.7 11.0 %collective-permute-start.7 = (bf16[4,160,128]{2,1,0:T(8,128)(2,1)S(1)}, bf16[4,160,128]{2,1,0:T(8,128)(2,1)S(1)}, u32[]{:S(2)}, u32[]{:S(2)}) collective-permute-start(bf16[4,160,128]{2,1,0:T(8,128)(2,1)S(1)} %get-tuple-element.47), channel_id=1, source_target_pairs={{0,8},{1,9},{2,10},{3,11},{4,12},{5,13},{6,14},{7,15},{8,0},{9,1},... | collective-permute-start | bytes 491528 | tf_op jit(solution)/shard_map/ppermute | solution.py:250
  108.4 15.6 %collective-permute-start.8 = (bf16[4,160,128]{2,1,0:T(8,128)(2,1)S(1)}, bf16[4,160,128]{2,1,0:T(8,128)(2,1)S(1)}, u32[]{:S(2)}, u32[]{:S(2)}) collective-permute-start(bf16[4,160,128]{2,1,0:T(8,128)(2,1)S(1)} %get-tuple-element.48), channel_id=1, source_target_pairs={{0,12},{1,13},{2,14},{3,15},{4,8},{5,9},{6,10},{7,11},{8,4},{9,5},... | collective-permute-start | bytes 491528 | tf_op jit(solution)/shard_map/ppermute | solution.py:250
  124.0 7.9 %collective-permute-start.9 = (bf16[4,160,128]{2,1,0:T(8,128)(2,1)S(1)}, bf16[4,160,128]{2,1,0:T(8,128)(2,1)S(1)}, u32[]{:S(2)}, u32[]{:S(2)}) collective-permute-start(bf16[4,160,128]{2,1,0:T(8,128)(2,1)S(1)} %get-tuple-element.50), channel_id=1, source_target_pairs={{0,1},{1,0},{2,3},{3,2},{4,5},{5,4},{6,7},{7,6},{8,9},{9,8},{10,11... | collective-permute-start | bytes 491528 | tf_op jit(solution)/shard_map/ppermute | solution.py:250
  126.4 7.8 %collective-permute-start.10 = (bf16[4,160,128]{2,1,0:T(8,128)(2,1)S(1)}, bf16[4,160,128]{2,1,0:T(8,128)(2,1)S(1)}, u32[]{:S(2)}, u32[]{:S(2)}) collective-permute-start(bf16[4,160,128]{2,1,0:T(8,128)(2,1)S(1)} %get-tuple-element.51), channel_id=1, source_target_pairs={{0,2},{1,3},{2,0},{3,1},{4,6},{5,7},{6,4},{7,5},{8,10},{9,11},{10,... | collective-permute-start | bytes 491528 | tf_op jit(solution)/shard_map/ppermute | solution.py:250
  128.9 8.8 %collective-permute-start.11 = (bf16[4,160,128]{2,1,0:T(8,128)(2,1)S(1)}, bf16[4,160,128]{2,1,0:T(8,128)(2,1)S(1)}, u32[]{:S(2)}, u32[]{:S(2)}) collective-permute-start(bf16[4,160,128]{2,1,0:T(8,128)(2,1)S(1)} %get-tuple-element.52), channel_id=1, source_target_pairs={{0,3},{1,2},{2,1},{3,0},{4,7},{5,6},{6,5},{7,4},{8,11},{9,10},{10,... | collective-permute-start | bytes 491528 | tf_op jit(solution)/shard_map/ppermute | solution.py:250
  168.1 21.1 %all-to-all-start.2 = ((f32[16,8,128]{2,1,0:T(8,128)}), f32[16,8,128]{2,1,0:T(8,128)S(1)}, u32[]{:S(2)}, u32[]{:S(2)}) async-start(f32[16,8,128]{2,1,0:T(8,128)} %broadcast_in_dim.3), calls=%async_computation.2 | async-start | bytes 131072 | tf_op jit(solution)/shard_map/all_to_all | solution.py:358

commit v3 on v2

--- a/solution.py
+++ b/solution.py
@@ -12,8 +12,10 @@
 ROW_TILES = 4
 ROWS = TILE * ROW_TILES
 VMEM_LIMIT = 48 * 1024 * 1024
+VMEM_WHOLE = 60 * 1024 * 1024
 VMEM = pl.BlockSpec(memory_space=pltpu.VMEM)
 SMEM = pl.BlockSpec(memory_space=pltpu.SMEM)
+ANY = pl.BlockSpec(memory_space=pl.ANY)
 
 NT = (((1,), (1,)), ((), ()))
 NN = (((1,), (0,)), ((), ()))
@@ -24,14 +26,14 @@
     return lax.dot_general(left, right, dims, preferred_element_type=jnp.float32)
 
 
-def call(kernel, out_shape, in_specs, scratch=(), flops=0, nbytes=0):
+def call(kernel, out_shape, in_specs, scratch=(), flops=0, nbytes=0, out_specs=None, limit=VMEM_LIMIT):
     return pl.pallas_call(
         kernel,
         out_shape=out_shape,
         in_specs=in_specs,
-        out_specs=jax.tree.map(lambda _: VMEM, out_shape),
+        out_specs=jax.tree.map(lambda _: VMEM, out_shape) if out_specs is None else out_specs,
         scratch_shapes=list(scratch),
-        compiler_params=pltpu.CompilerParams(vmem_limit_bytes=VMEM_LIMIT),
+        compiler_params=pltpu.CompilerParams(vmem_limit_bytes=limit),
         cost_estimate=pl.CostEstimate(flops=flops, bytes_accessed=nbytes, transcendentals=0),
     )
 
@@ -51,23 +53,47 @@
     return 8 if count % 8 == 0 else count
 
 
-def scale_gather_dom(degrees_ref, features_ref, lists_ref, out_ref, scaled_ref):
+def scale_gather_dom(
+    degrees_hbm,
+    features_hbm,
+    lists_hbm,
+    out_hbm,
+    scaled_ref,
+    degrees_ref,
+    features_ref,
+    lists_ref,
+    out_ref,
+    in_sems,
+    out_sems,
+):
+    pairs = ((degrees_hbm, degrees_ref), (features_hbm, features_ref), (lists_hbm, lists_ref))
+    loads = [pltpu.make_async_copy(*pair, in_sems.at[i]) for i, pair in enumerate(pairs)]
+    for load in loads:
+        load.start()
+    loads[0].wait()
+    loads[1].wait()
     root = inverse_root(degrees_ref)
     for t in range(ROW_TILES):
         turned = features_ref[t * TILE : (t + 1) * TILE, :].astype(jnp.float32).T
         scaled_ref[t] = (turned * root[t : t + 1, :]).astype(jnp.bfloat16)
     scaled = jnp.concatenate([scaled_ref[t] for t in range(ROW_TILES)], axis=1)
+    loads[2].wait()
     count = lists_ref.shape[0]
     step = group(count)
 
-    @pl.loop(0, count // step)
-    def _(part):
-        first = part * step
-        rows = lists_ref[pl.ds(pl.multiple_of(first, step), step), :]
+    def store(part):
+        blocks = pl.ds(part * step, step)
+        return pltpu.make_async_copy(out_ref.at[blocks], out_hbm.at[blocks], out_sems.at[part])
+
+    for part in range(count // step):
+        rows = lists_ref[part * step : (part + 1) * step, :]
         picked = mul(scaled, one_hot([rows[i : i + 1, :] for i in range(step)]), NN)
         picked = picked.astype(jnp.bfloat16)
         for i in range(step):
-            out_ref[first + i] = picked[:, i * TILE : (i + 1) * TILE]
+            out_ref[part * step + i] = picked[:, i * TILE : (i + 1) * TILE]
+        store(part).start()
+    for part in range(count // step):
+        store(part).wait()
 
 
 def gather_grp(me_ref, scaled_ref, lists_ref, *out_refs):
@@ -263,17 +289,10 @@
     return [turned[0]] + [xor_permute(turned[k], "grp", grp, k) for k in range(1, radix)]
 
 
-def gathered_sum(value, axis, groups):
-    if len(groups[0]) == 1:
-        return value
-    return jnp.sum(lax.all_gather(value, axis, axis_index_groups=groups), axis=0)
-
-
-def dom_sum(value, dom):
+def dom_groups(dom):
     inner = 12 if dom % 12 == 0 else dom
-    rows = [[o * inner + i for i in range(inner)] for o in range(dom // inner)]
-    value = gathered_sum(value, "dom", [list(column) for column in zip(*rows)])
-    return gathered_sum(value, "dom", rows)
+    along_z = [[o * inner + i for i in range(inner)] for o in range(dom // inner)]
+    return [list(column) for column in zip(*along_z)], along_z
 
 
 def body(features, degrees, adj_tiles, block_list, send_dom, send_grp, weight, bias_vec, cotangent):
@@ -293,7 +312,17 @@
     to_dom, scaled = call(
         scale_gather_dom,
         (shape((dom, TILE, TILE), bf16), shape((ROW_TILES, TILE, TILE), bf16)),
-        [VMEM] * 3,
+        [ANY] * 3,
+        [
+            pltpu.VMEM((ROW_TILES, TILE), jnp.int32),
+            pltpu.VMEM((ROWS, TILE), bf16),
+            pltpu.VMEM((dom, TILE), jnp.int32),
+            pltpu.VMEM((dom, TILE, TILE), bf16),
+            pltpu.SemaphoreType.DMA((3,)),
+            pltpu.SemaphoreType.DMA((dom // group(dom),)),
+        ],
+        out_specs=(ANY, VMEM),
+        limit=VMEM_WHOLE,
         flops=4 * dom * product,
         nbytes=dom * block_bytes,
     )(degree_rows, features, send_dom)
@@ -351,8 +380,13 @@
         [VMEM] * radix,
         nbytes=grp * block_bytes,
     )(*returned_grp)
-    chunk = dom_sum(chunk, dom) * (1.0 / math.sqrt(ROWS * dom * grp))
-    chunk, returned_dom = lax.optimization_barrier((chunk, returned_dom))
+    along_x, along_z = dom_groups(dom)
+    if len(along_x[0]) > 1:
+        chunk = jnp.sum(lax.all_gather(chunk, "dom", axis_index_groups=along_x), axis=0)
+    copies = jnp.broadcast_to(chunk, (len(along_z[0]), *chunk.shape))
+    copies, returned_dom = lax.optimization_barrier((copies, returned_dom))
+    pieces = lax.all_to_all(copies, "dom", 0, 0, axis_index_groups=along_z, tiled=True)
+    chunk = jnp.sum(pieces, axis=0) * (1.0 / math.sqrt(ROWS * dom * grp))
     grad_bias = chunk[depth]
     copies = jnp.broadcast_to(chunk[:depth], (grp, depth, TILE))
     grad_weight = lax.all_to_all(copies, "grp", split_axis=0, concat_axis=0, tiled=True)

time: 191 us -> 188 us (0.984)
  blocking collectives: 28.9 us -> 10.3 us
  waiting for transfers between devices: 51.8 us -> 63.2 us
  starting transfers between devices: 84.9 us -> 90.7 us
  local copies, waits for them, and re-layouts: 6.42 us -> 3.62 us
    all_gather x2 -> x1, blocking collectives: 28.9 us -> 10.3 us  [body(): lax.all_gather(chunk, 'dom', axis_index_groups=along_x)]
    all_to_all x0 -> x1, starting transfers between devices: none -> 9.11 us  [body(): lax.all_to_all(copies, 'dom', 0, 0, axis_index_groups=along_z, tiled=True)]
    all_to_all x1, waiting for transfers between devices: 2.45 us -> 7.3 us  [body(): lax.all_to_all(copies, 'grp', split_axis=0, concat_axis=0, tiled=True)]
    all_to_all x0 -> x1, waiting for transfers between devices: none -> 4.55 us  [body(): lax.all_to_all(copies, 'dom', 0, 0, axis_index_groups=along_z, tiled=True)]
    unnamed x29 -> x23, local copies, waits for them, and re-layouts: 5.27 us -> 1.83 us
    all_to_all x1, starting transfers between devices: 13.2 us -> 9.95 us  [body(): lax.all_to_all(copies, 'grp', split_axis=0, concat_axis=0, tiled=True)]
    all_to_all x1, waiting for transfers between devices: 0.01 us -> 2.02 us  [body(): lax.all_to_all(to_lender, 'dom', split_axis=0, concat_axis=0, tiled=True)]
  transfers between devices with their start and end apart: 15 -> 16, of which waited for: 10 -> 12; matrix products, arithmetic and copies ran while one was open for 0% -> 0% of each run, Pallas kernels for 5% -> 5%
where the time goes in v3:
time: 188 us; the launch traced here: 187 us
  starting transfers between devices  90.7 us (48%)
  waiting for transfers between devices  63.2 us (34%)
  Pallas kernels  18.3 us (10%)
  blocking collectives  10.3 us (5%)
  local copies, waits for them, and re-layouts  3.62 us (2%)
    ppermute x12, starting transfers between devices, xor_permute(): return lax.ppermute(value, axis, [(i, i ^ k) for i in range(size)])  40 us
    ppermute x12, waiting for transfers between devices, xor_permute(): return lax.ppermute(value, axis, [(i, i ^ k) for i in range(size)])  35.2 us
    all_to_all x1, starting transfers between devices, body(): lax.all_to_all(to_dom, 'dom', split_axis=0, concat_axis=0, tiled=True)  19.3 us
    all_to_all x1, waiting for transfers between devices, body(): lax.all_to_all(to_dom, 'dom', split_axis=0, concat_axis=0, tiled=True)  14.1 us
    all_to_all x1, starting transfers between devices, body(): lax.all_to_all(to_lender, 'dom', split_axis=0, concat_axis=0, tiled=True)  12.3 us
    all_gather x1, blocking collectives, body(): lax.all_gather(chunk, 'dom', axis_index_groups=along_x)  10.3 us
    all_to_all x1, starting transfers between devices, body(): lax.all_to_all(copies, 'grp', split_axis=0, concat_axis=0, tiled=True)  9.95 us
    all_to_all x1, starting transfers between devices, body(): lax.all_to_all(copies, 'dom', 0, 0, axis_index_groups=along_z, tiled=True)  9.11 us
  transfers between devices with their start and end apart: 16, of which 12 were waited for; matrix products, arithmetic and copies ran while one was open for 0% of the time, Pallas kernels for 5%

profile of v3, /device:TPU:1, one launch (start us, length us, event | category | flops | bytes accessed | tf_op | source)
XLA Modules:
  0.0 187.1 jit_solution(15697258920525110928)
XLA Ops:
  0.6 3.5 %shard_map.120 = (bf16[48,128,128]{2,1,0:T(8,128)(2,1)}, bf16[4,128,128]{2,1,0:T(8,128)(2,1)}) custom-call(s32[4,128]{1,0:T(4,128)} %bitcast.11, bf16[512,128]{1,0:T(8,128)(2,1)} %features_hbm.1, s32[48,128]{1,0:T(8,128)} %lists_ref.5), custom_call_target="tpu_custom_call" | custom-call | flops 805306368 | bytes 1572864 | tf_op jit(solution)/shard_map/pallas_call | solution.py:312
  4.2 19.3 %all-to-all-start = ((bf16[48,128,128]{2,1,0:T(8,128)(2,1)}), bf16[48,128,128]{2,1,0:T(8,128)(2,1)}, u32[]{:S(2)}, u32[]{:S(2)}) async-start(bf16[48,128,128]{2,1,0:T(8,128)(2,1)} %get-tuple-element.30), calls=%async_computation | async-start | bytes 3145728 | tf_op jit(solution)/shard_map/all_to_all | solution.py:329
  24.2 4.2 %collective-permute-start = (bf16[4,128,128]{2,1,0:T(8,128)(2,1)S(1)}, bf16[4,128,128]{2,1,0:T(8,128)(2,1)S(1)}, u32[]{:S(2)}, u32[]{:S(2)}) collective-permute-start(bf16[4,128,128]{2,1,0:T(8,128)(2,1)S(1)} %get-tuple-element.33), channel_id=1, source_target_pairs={{0,4},{1,5},{2,6},{3,7},{4,0},{5,1},{6,2},{7,3},{8,12},{9,13},{10,... | collective-permute-start | bytes 393224 | tf_op jit(solution)/shard_map/ppermute | solution.py:276
  28.5 5.7 %collective-permute-start.1 = (bf16[4,128,128]{2,1,0:T(8,128)(2,1)S(1)}, bf16[4,128,128]{2,1,0:T(8,128)(2,1)S(1)}, u32[]{:S(2)}, u32[]{:S(2)}) collective-permute-start(bf16[4,128,128]{2,1,0:T(8,128)(2,1)S(1)} %get-tuple-element.34), channel_id=1, source_target_pairs={{0,8},{1,9},{2,10},{3,11},{4,12},{5,13},{6,14},{7,15},{8,0},{9,1},... | collective-permute-start | bytes 393224 | tf_op jit(solution)/shard_map/ppermute | solution.py:276
  34.1 1.9 %collective-permute-start.2 = (bf16[4,128,128]{2,1,0:T(8,128)(2,1)S(1)}, bf16[4,128,128]{2,1,0:T(8,128)(2,1)S(1)}, u32[]{:S(2)}, u32[]{:S(2)}) collective-permute-start(bf16[4,128,128]{2,1,0:T(8,128)(2,1)S(1)} %get-tuple-element.35), channel_id=1, source_target_pairs={{0,12},{1,13},{2,14},{3,15},{4,8},{5,9},{6,10},{7,11},{8,4},{9,5},... | collective-permute-start | bytes 393224 | tf_op jit(solution)/shard_map/ppermute | solution.py:276
  36.1 2.5 %collective-permute-done.1.refs_2_ = bf16[4,128,128]{2,1,0:T(8,128)(2,1)S(1)} collective-permute-done((bf16[4,128,128]{2,1,0:T(8,128)(2,1)S(1)}, bf16[4,128,128]{2,1,0:T(8,128)(2,1)S(1)}, u32[]{:S(2)}, u32[]{:S(2)}) %collective-permute-start.1) | collective-permute-done | bytes 131104 | tf_op jit(solution)/shard_map/ppermute | solution.py:276
  38.6 7.5 %collective-permute-done.2.refs_3_ = bf16[4,128,128]{2,1,0:T(8,128)(2,1)S(1)} collective-permute-done((bf16[4,128,128]{2,1,0:T(8,128)(2,1)S(1)}, bf16[4,128,128]{2,1,0:T(8,128)(2,1)S(1)}, u32[]{:S(2)}, u32[]{:S(2)}) %collective-permute-start.2) | collective-permute-done | bytes 131104 | tf_op jit(solution)/shard_map/ppermute | solution.py:276
  46.1 2.4 %collective-permute-start.3 = (bf16[4,128,128]{2,1,0:T(8,128)(2,1)S(1)}, bf16[4,128,128]{2,1,0:T(8,128)(2,1)S(1)}, u32[]{:S(2)}, u32[]{:S(2)}) collective-permute-start(bf16[4,128,128]{2,1,0:T(8,128)(2,1)S(1)} %get-tuple-element.37), channel_id=1, source_target_pairs={{0,1},{1,0},{2,3},{3,2},{4,5},{5,4},{6,7},{7,6},{8,9},{9,8},{10,11... | collective-permute-start | bytes 393224 | tf_op jit(solution)/shard_map/ppermute | solution.py:276
  48.5 4.2 %collective-permute-start.4 = (bf16[4,128,128]{2,1,0:T(8,128)(2,1)S(1)}, bf16[4,128,128]{2,1,0:T(8,128)(2,1)S(1)}, u32[]{:S(2)}, u32[]{:S(2)}) collective-permute-start(bf16[4,128,128]{2,1,0:T(8,128)(2,1)S(1)} %get-tuple-element.38), channel_id=1, source_target_pairs={{0,2},{1,3},{2,0},{3,1},{4,6},{5,7},{6,4},{7,5},{8,10},{9,11},{10,... | collective-permute-start | bytes 393224 | tf_op jit(solution)/shard_map/ppermute | solution.py:276
  52.7 1.9 %collective-permute-start.5 = (bf16[4,128,128]{2,1,0:T(8,128)(2,1)S(1)}, bf16[4,128,128]{2,1,0:T(8,128)(2,1)S(1)}, u32[]{:S(2)}, u32[]{:S(2)}) collective-permute-start(bf16[4,128,128]{2,1,0:T(8,128)(2,1)S(1)} %get-tuple-element.39), channel_id=1, source_target_pairs={{0,3},{1,2},{2,1},{3,0},{4,7},{5,6},{6,5},{7,4},{8,11},{9,10},{10,... | collective-permute-start | bytes 393224 | tf_op jit(solution)/shard_map/ppermute | solution.py:276
  54.6 2.0 %collective-permute-done.4.refs_2_ = bf16[4,128,128]{2,1,0:T(8,128)(2,1)S(1)} collective-permute-done((bf16[4,128,128]{2,1,0:T(8,128)(2,1)S(1)}, bf16[4,128,128]{2,1,0:T(8,128)(2,1)S(1)}, u32[]{:S(2)}, u32[]{:S(2)}) %collective-permute-start.4) | collective-permute-done | bytes 131104 | tf_op jit(solution)/shard_map/ppermute | solution.py:276
  56.7 3.7 %collective-permute-done.5.refs_3_ = bf16[4,128,128]{2,1,0:T(8,128)(2,1)S(1)} collective-permute-done((bf16[4,128,128]{2,1,0:T(8,128)(2,1)S(1)}, bf16[4,128,128]{2,1,0:T(8,128)(2,1)S(1)}, u32[]{:S(2)}, u32[]{:S(2)}) %collective-permute-start.5) | collective-permute-done | bytes 131104 | tf_op jit(solution)/shard_map/ppermute | solution.py:276
  61.9 14.1 %all-to-all-done.recv_ref = bf16[48,128,128]{2,1,0:T(8,128)(2,1)} async-done(((bf16[48,128,128]{2,1,0:T(8,128)(2,1)}), bf16[48,128,128]{2,1,0:T(8,128)(2,1)}, u32[]{:S(2)}, u32[]{:S(2)}) %all-to-all-start) | async-done | bytes 1572896 | tf_op jit(solution)/shard_map/all_to_all | solution.py:329
  76.1 5.8 %shard_map.124 = (bf16[512,128]{1,0:T(8,128)(2,1)}, bf16[48,128,128]{2,1,0:T(8,128)(2,1)S(1)}, bf16[5,128,128]{2,1,0:T(8,128)(2,1)S(1)}, f32[128,128]{1,0:T(8,128)S(1)}, f32[1,128]{1,0:T(1,128)S(1)}) custom-call(s32[2,80]{1,0:T(2,128)S(1)} %bitcast.9, s32[4,128]{1,0:T(4,128)S(1)} %bitcast.12, bf16[80,128,128]{2,1,0:T(8,128)(2,1)} %tiles_ref.5, ...), custom_call_target="tpu_custom_call" | custom-call | flops 671088640 | bytes 7864320 | tf_op jit(solution)/shard_map/pallas_call | solution.py:347
  83.1 12.3 %all-to-all-start.1 = ((bf16[48,128,128]{2,1,0:T(8,128)(2,1)}), bf16[48,128,128]{2,1,0:T(8,128)(2,1)}, u32[]{:S(2)}, u32[]{:S(2)}) async-start(bf16[48,128,128]{2,1,0:T(8,128)(2,1)} %copy-done.2), calls=%async_computation.1 | async-start | bytes 3145728 | tf_op jit(solution)/shard_map/all_to_all | solution.py:364
  96.6 4.2 %collective-permute-start.6 = (bf16[4,160,128]{2,1,0:T(8,128)(2,1)S(1)}, bf16[4,160,128]{2,1,0:T(8,128)(2,1)S(1)}, u32[]{:S(2)}, u32[]{:S(2)}) collective-permute-start(bf16[4,160,128]{2,1,0:T(8,128)(2,1)S(1)} %get-tuple-element.46), channel_id=1, source_target_pairs={{0,4},{1,5},{2,6},{3,7},{4,0},{5,1},{6,2},{7,3},{8,12},{9,13},{10,... | collective-permute-start | bytes 491528 | tf_op jit(solution)/shard_map/ppermute | solution.py:276
  100.8 5.7 %collective-permute-start.7 = (bf16[4,160,128]{2,1,0:T(8,128)(2,1)S(1)}, bf16[4,160,128]{2,1,0:T(8,128)(2,1)S(1)}, u32[]{:S(2)}, u32[]{:S(2)}) collective-permute-start(bf16[4,160,128]{2,1,0:T(8,128)(2,1)S(1)} %get-tuple-element.47), channel_id=1, source_target_pairs={{0,8},{1,9},{2,10},{3,11},{4,12},{5,13},{6,14},{7,15},{8,0},{9,1},... | collective-permute-start | bytes 491528 | tf_op jit(solution)/shard_map/ppermute | solution.py:276
  106.5 1.9 %collective-permute-start.8 = (bf16[4,160,128]{2,1,0:T(8,128)(2,1)S(1)}, bf16[4,160,128]{2,1,0:T(8,128)(2,1)S(1)}, u32[]{:S(2)}, u32[]{:S(2)}) collective-permute-start(bf16[4,160,128]{2,1,0:T(8,128)(2,1)S(1)} %get-tuple-element.48), channel_id=1, source_target_pairs={{0,12},{1,13},{2,14},{3,15},{4,8},{5,9},{6,10},{7,11},{8,4},{9,5},... | collective-permute-start | bytes 491528 | tf_op jit(solution)/shard_map/ppermute | solution.py:276
  108.4 3.4 %collective-permute-done.7.refs_2_ = bf16[4,160,128]{2,1,0:T(8,128)(2,1)S(1)} collective-permute-done((bf16[4,160,128]{2,1,0:T(8,128)(2,1)S(1)}, bf16[4,160,128]{2,1,0:T(8,128)(2,1)S(1)}, u32[]{:S(2)}, u32[]{:S(2)}) %collective-permute-start.7) | collective-permute-done | bytes 163872 | tf_op jit(solution)/shard_map/ppermute | solution.py:276
  111.9 10.2 %collective-permute-done.8.refs_3_ = bf16[4,160,128]{2,1,0:T(8,128)(2,1)S(1)} collective-permute-done((bf16[4,160,128]{2,1,0:T(8,128)(2,1)S(1)}, bf16[4,160,128]{2,1,0:T(8,128)(2,1)S(1)}, u32[]{:S(2)}, u32[]{:S(2)}) %collective-permute-start.8) | collective-permute-done | bytes 163872 | tf_op jit(solution)/shard_map/ppermute | solution.py:276
  122.1 2.4 %collective-permute-start.9 = (bf16[4,160,128]{2,1,0:T(8,128)(2,1)S(1)}, bf16[4,160,128]{2,1,0:T(8,128)(2,1)S(1)}, u32[]{:S(2)}, u32[]{:S(2)}) collective-permute-start(bf16[4,160,128]{2,1,0:T(8,128)(2,1)S(1)} %get-tuple-element.50), channel_id=1, source_target_pairs={{0,1},{1,0},{2,3},{3,2},{4,5},{5,4},{6,7},{7,6},{8,9},{9,8},{10,11... | collective-permute-start | bytes 491528 | tf_op jit(solution)/shard_map/ppermute | solution.py:276
  124.5 2.5 %collective-permute-start.10 = (bf16[4,160,128]{2,1,0:T(8,128)(2,1)S(1)}, bf16[4,160,128]{2,1,0:T(8,128)(2,1)S(1)}, u32[]{:S(2)}, u32[]{:S(2)}) collective-permute-start(bf16[4,160,128]{2,1,0:T(8,128)(2,1)S(1)} %get-tuple-element.51), channel_id=1, source_target_pairs={{0,2},{1,3},{2,0},{3,1},{4,6},{5,7},{6,4},{7,5},{8,10},{9,11},{10,... | collective-permute-start | bytes 491528 | tf_op jit(solution)/shard_map/ppermute | solution.py:276
  127.0 3.0 %collective-permute-start.11 = (bf16[4,160,128]{2,1,0:T(8,128)(2,1)S(1)}, bf16[4,160,128]{2,1,0:T(8,128)(2,1)S(1)}, u32[]{:S(2)}, u32[]{:S(2)}) collective-permute-start(bf16[4,160,128]{2,1,0:T(8,128)(2,1)S(1)} %get-tuple-element.52), channel_id=1, source_target_pairs={{0,3},{1,2},{2,1},{3,0},{4,7},{5,6},{6,5},{7,4},{8,11},{9,10},{10,... | collective-permute-start | bytes 491528 | tf_op jit(solution)/shard_map/ppermute | solution.py:276
  130.0 2.3 %collective-permute-done.10.refs_2_ = bf16[4,160,128]{2,1,0:T(8,128)(2,1)S(1)} collective-permute-done((bf16[4,160,128]{2,1,0:T(8,128)(2,1)S(1)}, bf16[4,160,128]{2,1,0:T(8,128)(2,1)S(1)}, u32[]{:S(2)}, u32[]{:S(2)}) %collective-permute-start.10) | collective-permute-done | bytes 163872 | tf_op jit(solution)/shard_map/ppermute | solution.py:276
  132.3 3.5 %collective-permute-done.11.refs_3_ = bf16[4,160,128]{2,1,0:T(8,128)(2,1)S(1)} collective-permute-done((bf16[4,160,128]{2,1,0:T(8,128)(2,1)S(1)}, bf16[4,160,128]{2,1,0:T(8,128)(2,1)S(1)}, u32[]{:S(2)}, u32[]{:S(2)}) %collective-permute-start.11) | collective-permute-done | bytes 163872 | tf_op jit(solution)/shard_map/ppermute | solution.py:276
  135.9 10.3 %all-gather = f32[64,128]{1,0:T(8,128)S(1)} all-gather(f32[16,128]{1,0:T(8,128)S(1)} %shard_map.128), channel_id=2, replica_groups={{0,192,384,576},{16,208,400,592},{32,224,416,608},{48,240,432,624},{64,..., dimensions={0}, use_global_device_ids=true | all-gather | bytes 40960 | tf_op jit(solution)/shard_map/all_gather | solution.py:385
  146.2 2.0 %all-to-all-done.1.recv_ref = bf16[48,128,128]{2,1,0:T(8,128)(2,1)} async-done(((bf16[48,128,128]{2,1,0:T(8,128)(2,1)}), bf16[48,128,128]{2,1,0:T(8,128)(2,1)}, u32[]{:S(2)}, u32[]{:S(2)}) %all-to-all-start.1) | async-done | bytes 1572896 | tf_op jit(solution)/shard_map/all_to_all | solution.py:364
  148.8 9.1 %all-to-all-start.2 = ((f32[12,16,128]{2,1,0:T(8,128)}), f32[12,16,128]{2,1,0:T(8,128)S(1)}, u32[]{:S(2)}, u32[]{:S(2)}) async-start(f32[12,16,128]{2,1,0:T(8,128)} %broadcast_in_dim.6), calls=%async_computation.2 | async-start | bytes 196608 | tf_op jit(solution)/shard_map/all_to_all | solution.py:388
  158.7 4.8 %shard_map.129 = bf16[512,128]{1,0:T(8,128)(2,1)} custom-call(s32[4,128]{1,0:T(4,128)S(1)} %bitcast.13, s32[48,128]{1,0:T(8,128)S(1)} %copy-done.10, f32[512,128]{1,0:T(8,128)S(1)} %shard_map.127.near_ref, bf16[48,128,128]{2,1,0:T(8,128)(2,1)} %all-to-all-done.1.recv_ref), custom_call_target="tpu_custom_call" | custom-call | flops 805306368 | bytes 1572864 | tf_op jit(solution)/shard_map/pallas_call | solution.py:402
  163.5 4.5 %all-to-all-done.2 = f32[12,16,128]{2,1,0:T(8,128)S(1)} async-done(((f32[12,16,128]{2,1,0:T(8,128)}), f32[12,16,128]{2,1,0:T(8,128)S(1)}, u32[]{:S(2)}, u32[]{:S(2)}) %all-to-all-start.2) | async-done | bytes 98336 | tf_op jit(solution)/shard_map/all_to_all | solution.py:388
  168.7 9.9 %all-to-all-start.3 = ((f32[16,8,128]{2,1,0:T(8,128)}), f32[16,8,128]{2,1,0:T(8,128)S(1)}, u32[]{:S(2)}, u32[]{:S(2)}) async-start(f32[16,8,128]{2,1,0:T(8,128)} %broadcast_in_dim.7), calls=%async_computation.3 | async-start | bytes 131072 | tf_op jit(solution)/shard_map/all_to_all | solution.py:392
  179.2 7.3 %all-to-all-done.3 = f32[16,8,128]{2,1,0:T(8,128)S(1)} async-done(((f32[16,8,128]{2,1,0:T(8,128)}), f32[16,8,128]{2,1,0:T(8,128)S(1)}, u32[]{:S(2)}, u32[]{:S(2)}) %all-to-all-start.3) | async-done | bytes 65568 | tf_op jit(solution)/shard_map/all_to_all | solution.py:392
  (41 shorter events, 7.8 us)
Async XLA Ops:
  4.1 19.4 %copy-start.4 = (bf16[4,128,128]{2,1,0:T(8,128)(2,1)S(1)}, bf16[4,128,128]{2,1,0:T(8,128)(2,1)}, u32[]{:S(2)}) copy-start(bf16[4,128,128]{2,1,0:T(8,128)(2,1)} %get-tuple-element.31.scaled_ref) | copy-start | bytes 393220
  4.2 19.4 %copy-start.7 = (s32[16,128]{1,0:T(8,128)S(1)}, s32[16,128]{1,0:T(8,128)}, u32[]{:S(2)}) copy-start(s32[16,128]{1,0:T(8,128)} %lists_ref.4) | copy-start | bytes 24580
  4.2 56.2 %copy-start = (bf16[80,128,128]{2,1,0:T(8,128)(2,1)S(1)}, bf16[80,128,128]{2,1,0:T(8,128)(2,1)}, u32[]{:S(2)}) copy-start(bf16[80,128,128]{2,1,0:T(8,128)(2,1)} %tiles_ref.5) | copy-start | bytes 7864324
  4.2 56.2 %copy-start.6 = (s32[80,2]{0,1:T(2,128)S(1)}, s32[80,2]{0,1:T(2,128)}, u32[]{:S(2)}) copy-start(s32[80,2]{0,1:T(2,128)} %param.12) | copy-start | bytes 1924
  4.2 71.9 %all-to-all-start = ((bf16[48,128,128]{2,1,0:T(8,128)(2,1)}), bf16[48,128,128]{2,1,0:T(8,128)(2,1)}, u32[]{:S(2)}, u32[]{:S(2)}) async-start(bf16[48,128,128]{2,1,0:T(8,128)(2,1)} %get-tuple-element.30), calls=%async_computation | async-start | bytes 3145728 | tf_op jit(solution)/shard_map/all_to_all | solution.py:329
  24.2 11.8 %collective-permute-start = (bf16[4,128,128]{2,1,0:T(8,128)(2,1)S(1)}, bf16[4,128,128]{2,1,0:T(8,128)(2,1)S(1)}, u32[]{:S(2)}, u32[]{:S(2)}) collective-permute-start(bf16[4,128,128]{2,1,0:T(8,128)(2,1)S(1)} %get-tuple-element.33), channel_id=1, source_target_pairs={{0,4},{1,5},{2,6},{3,7},{4,0},{5,1},{6,2},{7,3},{8,12},{9,13},{10,... | collective-permute-start | bytes 393224 | tf_op jit(solution)/shard_map/ppermute | solution.py:276
  28.5 10.1 %collective-permute-start.1 = (bf16[4,128,128]{2,1,0:T(8,128)(2,1)S(1)}, bf16[4,128,128]{2,1,0:T(8,128)(2,1)S(1)}, u32[]{:S(2)}, u32[]{:S(2)}) collective-permute-start(bf16[4,128,128]{2,1,0:T(8,128)(2,1)S(1)} %get-tuple-element.34), channel_id=1, source_target_pairs={{0,8},{1,9},{2,10},{3,11},{4,12},{5,13},{6,14},{7,15},{8,0},{9,1},... | collective-permute-start | bytes 393224 | tf_op jit(solution)/shard_map/ppermute | solution.py:276
  34.1 11.9 %collective-permute-start.2 = (bf16[4,128,128]{2,1,0:T(8,128)(2,1)S(1)}, bf16[4,128,128]{2,1,0:T(8,128)(2,1)S(1)}, u32[]{:S(2)}, u32[]{:S(2)}) collective-permute-start(bf16[4,128,128]{2,1,0:T(8,128)(2,1)S(1)} %get-tuple-element.35), channel_id=1, source_target_pairs={{0,12},{1,13},{2,14},{3,15},{4,8},{5,9},{6,10},{7,11},{8,4},{9,5},... | collective-permute-start | bytes 393224 | tf_op jit(solution)/shard_map/ppermute | solution.py:276
  46.1 8.6 %collective-permute-start.3 = (bf16[4,128,128]{2,1,0:T(8,128)(2,1)S(1)}, bf16[4,128,128]{2,1,0:T(8,128)(2,1)S(1)}, u32[]{:S(2)}, u32[]{:S(2)}) collective-permute-start(bf16[4,128,128]{2,1,0:T(8,128)(2,1)S(1)} %get-tuple-element.37), channel_id=1, source_target_pairs={{0,1},{1,0},{2,3},{3,2},{4,5},{5,4},{6,7},{7,6},{8,9},{9,8},{10,11... | collective-permute-start | bytes 393224 | tf_op jit(solution)/shard_map/ppermute | solution.py:276
  48.5 8.2 %collective-permute-start.4 = (bf16[4,128,128]{2,1,0:T(8,128)(2,1)S(1)}, bf16[4,128,128]{2,1,0:T(8,128)(2,1)S(1)}, u32[]{:S(2)}, u32[]{:S(2)}) collective-permute-start(bf16[4,128,128]{2,1,0:T(8,128)(2,1)S(1)} %get-tuple-element.38), channel_id=1, source_target_pairs={{0,2},{1,3},{2,0},{3,1},{4,6},{5,7},{6,4},{7,5},{8,10},{9,11},{10,... | collective-permute-start | bytes 393224 | tf_op jit(solution)/shard_map/ppermute | solution.py:276
  52.7 7.7 %collective-permute-start.5 = (bf16[4,128,128]{2,1,0:T(8,128)(2,1)S(1)}, bf16[4,128,128]{2,1,0:T(8,128)(2,1)S(1)}, u32[]{:S(2)}, u32[]{:S(2)}) collective-permute-start(bf16[4,128,128]{2,1,0:T(8,128)(2,1)S(1)} %get-tuple-element.39), channel_id=1, source_target_pairs={{0,3},{1,2},{2,1},{3,0},{4,7},{5,6},{6,5},{7,4},{8,11},{9,10},{10,... | collective-permute-start | bytes 393224 | tf_op jit(solution)/shard_map/ppermute | solution.py:276
  60.4 15.6 %copy-start.3 = (bf16[512,128]{1,0:T(8,128)(2,1)S(1)}, bf16[512,128]{1,0:T(8,128)(2,1)}, u32[]{:S(2)}) copy-start(bf16[512,128]{1,0:T(8,128)(2,1)} %cotangent_ref.1) | copy-start | bytes 393220
  60.4 15.6 %copy-start.5 = (bf16[128,128]{1,0:T(8,128)(2,1)S(1)}, bf16[128,128]{1,0:T(8,128)(2,1)}, u32[]{:S(2)}) copy-start(bf16[128,128]{1,0:T(8,128)(2,1)} %weight_ref.1) | copy-start | bytes 98308
  60.4 15.6 %copy-start.8 = (s32[512]{0:T(512)S(1)}, s32[512]{0:T(512)}, u32[]{:S(2)}) copy-start(s32[512]{0:T(512)} %param.10) | copy-start | bytes 6148
  60.4 15.6 %copy-start.9 = (f32[128]{0:T(128)S(1)}, f32[128]{0:T(128)}, u32[]{:S(2)}) copy-start(f32[128]{0:T(128)} %param.16) | copy-start | bytes 1540
  81.9 1.1 copy-start.2
  83.1 12.4 %copy-start.1 = (bf16[80,128,128]{2,1,0:T(8,128)(2,1)S(1)}, bf16[80,128,128]{2,1,0:T(8,128)(2,1)}, u32[]{:S(2)}) copy-start(bf16[80,128,128]{2,1,0:T(8,128)(2,1)} %tiles_ref.5) | copy-start | bytes 7864324
  83.1 65.1 %all-to-all-start.1 = ((bf16[48,128,128]{2,1,0:T(8,128)(2,1)}), bf16[48,128,128]{2,1,0:T(8,128)(2,1)}, u32[]{:S(2)}, u32[]{:S(2)}) async-start(bf16[48,128,128]{2,1,0:T(8,128)(2,1)} %copy-done.2), calls=%async_computation.1 | async-start | bytes 3145728 | tf_op jit(solution)/shard_map/all_to_all | solution.py:364
  96.6 62.1 %copy-start.10 = (s32[48,128]{1,0:T(8,128)S(1)}, s32[48,128]{1,0:T(8,128)}, u32[]{:S(2)}) copy-start(s32[48,128]{1,0:T(8,128)} %lists_ref.5) | copy-start | bytes 73732
  96.6 11.8 %collective-permute-start.6 = (bf16[4,160,128]{2,1,0:T(8,128)(2,1)S(1)}, bf16[4,160,128]{2,1,0:T(8,128)(2,1)S(1)}, u32[]{:S(2)}, u32[]{:S(2)}) collective-permute-start(bf16[4,160,128]{2,1,0:T(8,128)(2,1)S(1)} %get-tuple-element.46), channel_id=1, source_target_pairs={{0,4},{1,5},{2,6},{3,7},{4,0},{5,1},{6,2},{7,3},{8,12},{9,13},{10,... | collective-permute-start | bytes 491528 | tf_op jit(solution)/shard_map/ppermute | solution.py:276
  100.8 11.1 %collective-permute-start.7 = (bf16[4,160,128]{2,1,0:T(8,128)(2,1)S(1)}, bf16[4,160,128]{2,1,0:T(8,128)(2,1)S(1)}, u32[]{:S(2)}, u32[]{:S(2)}) collective-permute-start(bf16[4,160,128]{2,1,0:T(8,128)(2,1)S(1)} %get-tuple-element.47), channel_id=1, source_target_pairs={{0,8},{1,9},{2,10},{3,11},{4,12},{5,13},{6,14},{7,15},{8,0},{9,1},... | collective-permute-start | bytes 491528 | tf_op jit(solution)/shard_map/ppermute | solution.py:276
  106.5 15.6 %collective-permute-start.8 = (bf16[4,160,128]{2,1,0:T(8,128)(2,1)S(1)}, bf16[4,160,128]{2,1,0:T(8,128)(2,1)S(1)}, u32[]{:S(2)}, u32[]{:S(2)}) collective-permute-start(bf16[4,160,128]{2,1,0:T(8,128)(2,1)S(1)} %get-tuple-element.48), channel_id=1, source_target_pairs={{0,12},{1,13},{2,14},{3,15},{4,8},{5,9},{6,10},{7,11},{8,4},{9,5},... | collective-permute-start | bytes 491528 | tf_op jit(solution)/shard_map/ppermute | solution.py:276
  122.1 7.9 %collective-permute-start.9 = (bf16[4,160,128]{2,1,0:T(8,128)(2,1)S(1)}, bf16[4,160,128]{2,1,0:T(8,128)(2,1)S(1)}, u32[]{:S(2)}, u32[]{:S(2)}) collective-permute-start(bf16[4,160,128]{2,1,0:T(8,128)(2,1)S(1)} %get-tuple-element.50), channel_id=1, source_target_pairs={{0,1},{1,0},{2,3},{3,2},{4,5},{5,4},{6,7},{7,6},{8,9},{9,8},{10,11... | collective-permute-start | bytes 491528 | tf_op jit(solution)/shard_map/ppermute | solution.py:276
  124.5 7.8 %collective-permute-start.10 = (bf16[4,160,128]{2,1,0:T(8,128)(2,1)S(1)}, bf16[4,160,128]{2,1,0:T(8,128)(2,1)S(1)}, u32[]{:S(2)}, u32[]{:S(2)}) collective-permute-start(bf16[4,160,128]{2,1,0:T(8,128)(2,1)S(1)} %get-tuple-element.51), channel_id=1, source_target_pairs={{0,2},{1,3},{2,0},{3,1},{4,6},{5,7},{6,4},{7,5},{8,10},{9,11},{10,... | collective-permute-start | bytes 491528 | tf_op jit(solution)/shard_map/ppermute | solution.py:276
  127.0 8.8 %collective-permute-start.11 = (bf16[4,160,128]{2,1,0:T(8,128)(2,1)S(1)}, bf16[4,160,128]{2,1,0:T(8,128)(2,1)S(1)}, u32[]{:S(2)}, u32[]{:S(2)}) collective-permute-start(bf16[4,160,128]{2,1,0:T(8,128)(2,1)S(1)} %get-tuple-element.52), channel_id=1, source_target_pairs={{0,3},{1,2},{2,1},{3,0},{4,7},{5,6},{6,5},{7,4},{8,11},{9,10},{10,... | collective-permute-start | bytes 491528 | tf_op jit(solution)/shard_map/ppermute | solution.py:276
  148.8 19.2 %all-to-all-start.2 = ((f32[12,16,128]{2,1,0:T(8,128)}), f32[12,16,128]{2,1,0:T(8,128)S(1)}, u32[]{:S(2)}, u32[]{:S(2)}) async-start(f32[12,16,128]{2,1,0:T(8,128)} %broadcast_in_dim.6), calls=%async_computation.2 | async-start | bytes 196608 | tf_op jit(solution)/shard_map/all_to_all | solution.py:388
  168.7 17.8 %all-to-all-start.3 = ((f32[16,8,128]{2,1,0:T(8,128)}), f32[16,8,128]{2,1,0:T(8,128)S(1)}, u32[]{:S(2)}, u32[]{:S(2)}) async-start(f32[16,8,128]{2,1,0:T(8,128)} %broadcast_in_dim.7), calls=%async_computation.3 | async-start | bytes 131072 | tf_op jit(solution)/shard_map/all_to_all | solution.py:392

commit v4 on v3

--- a/solution.py
+++ b/solution.py
@@ -237,6 +237,10 @@
     out_ref[0:depth, :] = total[0:depth, :] + total[depth : 2 * depth, :]
     bias_term = total[2 * depth : 2 * depth + 1, :] + total[2 * depth + 1 : 2 * depth + 2, :]
     out_ref[depth:, :] = jnp.broadcast_to(bias_term, (8, TILE))
+
+
+def sum_copies(pieces_ref, out_ref):
+    out_ref[...] = jnp.broadcast_to(jnp.sum(pieces_ref[...], axis=0)[None], out_ref.shape)
 
 
 def near_scatter(me_ref, lists_ref, own_ref, *refs):
@@ -381,9 +385,16 @@
         nbytes=grp * block_bytes,
     )(*returned_grp)
     along_x, along_z = dom_groups(dom)
+    pieces = chunk[None]
     if len(along_x[0]) > 1:
-        chunk = jnp.sum(lax.all_gather(chunk, "dom", axis_index_groups=along_x), axis=0)
-    copies = jnp.broadcast_to(chunk, (len(along_z[0]), *chunk.shape))
+        pieces = lax.all_gather(chunk, "dom", axis_index_groups=along_x)
+    copies = call(
+        sum_copies,
+        shape((len(along_z[0]), *chunk.shape), f32),
+        [VMEM],
+        flops=product,
+        nbytes=8 * block_bytes,
+    )(pieces)
     copies, returned_dom = lax.optimization_barrier((copies, returned_dom))
     pieces = lax.all_to_all(copies, "dom", 0, 0, axis_index_groups=along_z, tiled=True)
     chunk = jnp.sum(pieces, axis=0) * (1.0 / math.sqrt(ROWS * dom * grp))

time: 188 us -> 187 us (level)
  no operation moved by 1% of the time
where the time goes in v4:
time: 187 us; the launch traced here: 186 us
  starting transfers between devices  90.7 us (49%)
  waiting for transfers between devices  62.5 us (33%)
  Pallas kernels  19 us (10%)
  blocking collectives  10.3 us (6%)
  local copies, waits for them, and re-layouts  2.99 us (2%)
    ppermute x12, starting transfers between devices, xor_permute(): return lax.ppermute(value, axis, [(i, i ^ k) for i in range(size)])  40 us
    ppermute x12, waiting for transfers between devices, xor_permute(): return lax.ppermute(value, axis, [(i, i ^ k) for i in range(size)])  35.2 us
    all_to_all x1, starting transfers between devices, body(): lax.all_to_all(to_dom, 'dom', split_axis=0, concat_axis=0, tiled=True)  19.3 us
    all_to_all x1, waiting for transfers between devices, body(): lax.all_to_all(to_dom, 'dom', split_axis=0, concat_axis=0, tiled=True)  14.1 us
    all_to_all x1, starting transfers between devices, body(): lax.all_to_all(to_lender, 'dom', split_axis=0, concat_axis=0, tiled=True)  12.3 us
    all_gather x1, blocking collectives, body(): pieces = lax.all_gather(chunk, 'dom', axis_index_groups=along_x)  10.3 us
    all_to_all x1, starting transfers between devices, body(): lax.all_to_all(copies, 'grp', split_axis=0, concat_axis=0, tiled=True)  9.96 us
    all_to_all x1, starting transfers between devices, body(): lax.all_to_all(copies, 'dom', 0, 0, axis_index_groups=along_z, tiled=True)  9.12 us
  transfers between devices with their start and end apart: 16, of which 12 were waited for; matrix products, arithmetic and copies ran while one was open for 0% of the time, Pallas kernels for 5%

profile of v4, /device:TPU:1, one launch (start us, length us, event | category | flops | bytes accessed | tf_op | source)
XLA Modules:
  0.0 186.5 jit_solution(1991278489948150624)
XLA Ops:
  0.6 3.5 %shard_map.120 = (bf16[48,128,128]{2,1,0:T(8,128)(2,1)}, bf16[4,128,128]{2,1,0:T(8,128)(2,1)}) custom-call(s32[4,128]{1,0:T(4,128)} %bitcast.12, bf16[512,128]{1,0:T(8,128)(2,1)} %features_hbm.1, s32[48,128]{1,0:T(8,128)} %lists_ref.5), custom_call_target="tpu_custom_call" | custom-call | flops 805306368 | bytes 1572864 | tf_op jit(solution)/shard_map/pallas_call | solution.py:316
  4.2 19.3 %all-to-all-start = ((bf16[48,128,128]{2,1,0:T(8,128)(2,1)}), bf16[48,128,128]{2,1,0:T(8,128)(2,1)}, u32[]{:S(2)}, u32[]{:S(2)}) async-start(bf16[48,128,128]{2,1,0:T(8,128)(2,1)} %get-tuple-element.30), calls=%async_computation | async-start | bytes 3145728 | tf_op jit(solution)/shard_map/all_to_all | solution.py:333
  24.3 4.2 %collective-permute-start = (bf16[4,128,128]{2,1,0:T(8,128)(2,1)S(1)}, bf16[4,128,128]{2,1,0:T(8,128)(2,1)S(1)}, u32[]{:S(2)}, u32[]{:S(2)}) collective-permute-start(bf16[4,128,128]{2,1,0:T(8,128)(2,1)S(1)} %get-tuple-element.33), channel_id=1, source_target_pairs={{0,4},{1,5},{2,6},{3,7},{4,0},{5,1},{6,2},{7,3},{8,12},{9,13},{10,... | collective-permute-start | bytes 393224 | tf_op jit(solution)/shard_map/ppermute | solution.py:280
  28.5 5.7 %collective-permute-start.1 = (bf16[4,128,128]{2,1,0:T(8,128)(2,1)S(1)}, bf16[4,128,128]{2,1,0:T(8,128)(2,1)S(1)}, u32[]{:S(2)}, u32[]{:S(2)}) collective-permute-start(bf16[4,128,128]{2,1,0:T(8,128)(2,1)S(1)} %get-tuple-element.34), channel_id=1, source_target_pairs={{0,8},{1,9},{2,10},{3,11},{4,12},{5,13},{6,14},{7,15},{8,0},{9,1},... | collective-permute-start | bytes 393224 | tf_op jit(solution)/shard_map/ppermute | solution.py:280
  34.1 1.9 %collective-permute-start.2 = (bf16[4,128,128]{2,1,0:T(8,128)(2,1)S(1)}, bf16[4,128,128]{2,1,0:T(8,128)(2,1)S(1)}, u32[]{:S(2)}, u32[]{:S(2)}) collective-permute-start(bf16[4,128,128]{2,1,0:T(8,128)(2,1)S(1)} %get-tuple-element.35), channel_id=1, source_target_pairs={{0,12},{1,13},{2,14},{3,15},{4,8},{5,9},{6,10},{7,11},{8,4},{9,5},... | collective-permute-start | bytes 393224 | tf_op jit(solution)/shard_map/ppermute | solution.py:280
  36.1 2.5 %collective-permute-done.1.refs_2_ = bf16[4,128,128]{2,1,0:T(8,128)(2,1)S(1)} collective-permute-done((bf16[4,128,128]{2,1,0:T(8,128)(2,1)S(1)}, bf16[4,128,128]{2,1,0:T(8,128)(2,1)S(1)}, u32[]{:S(2)}, u32[]{:S(2)}) %collective-permute-start.1) | collective-permute-done | bytes 131104 | tf_op jit(solution)/shard_map/ppermute | solution.py:280
  38.6 7.5 %collective-permute-done.2.refs_3_ = bf16[4,128,128]{2,1,0:T(8,128)(2,1)S(1)} collective-permute-done((bf16[4,128,128]{2,1,0:T(8,128)(2,1)S(1)}, bf16[4,128,128]{2,1,0:T(8,128)(2,1)S(1)}, u32[]{:S(2)}, u32[]{:S(2)}) %collective-permute-start.2) | collective-permute-done | bytes 131104 | tf_op jit(solution)/shard_map/ppermute | solution.py:280
  46.1 2.4 %collective-permute-start.3 = (bf16[4,128,128]{2,1,0:T(8,128)(2,1)S(1)}, bf16[4,128,128]{2,1,0:T(8,128)(2,1)S(1)}, u32[]{:S(2)}, u32[]{:S(2)}) collective-permute-start(bf16[4,128,128]{2,1,0:T(8,128)(2,1)S(1)} %get-tuple-element.37), channel_id=1, source_target_pairs={{0,1},{1,0},{2,3},{3,2},{4,5},{5,4},{6,7},{7,6},{8,9},{9,8},{10,11... | collective-permute-start | bytes 393224 | tf_op jit(solution)/shard_map/ppermute | solution.py:280
  48.5 4.2 %collective-permute-start.4 = (bf16[4,128,128]{2,1,0:T(8,128)(2,1)S(1)}, bf16[4,128,128]{2,1,0:T(8,128)(2,1)S(1)}, u32[]{:S(2)}, u32[]{:S(2)}) collective-permute-start(bf16[4,128,128]{2,1,0:T(8,128)(2,1)S(1)} %get-tuple-element.38), channel_id=1, source_target_pairs={{0,2},{1,3},{2,0},{3,1},{4,6},{5,7},{6,4},{7,5},{8,10},{9,11},{10,... | collective-permute-start | bytes 393224 | tf_op jit(solution)/shard_map/ppermute | solution.py:280
  52.7 1.9 %collective-permute-start.5 = (bf16[4,128,128]{2,1,0:T(8,128)(2,1)S(1)}, bf16[4,128,128]{2,1,0:T(8,128)(2,1)S(1)}, u32[]{:S(2)}, u32[]{:S(2)}) collective-permute-start(bf16[4,128,128]{2,1,0:T(8,128)(2,1)S(1)} %get-tuple-element.39), channel_id=1, source_target_pairs={{0,3},{1,2},{2,1},{3,0},{4,7},{5,6},{6,5},{7,4},{8,11},{9,10},{10,... | collective-permute-start | bytes 393224 | tf_op jit(solution)/shard_map/ppermute | solution.py:280
  54.7 2.0 %collective-permute-done.4.refs_2_ = bf16[4,128,128]{2,1,0:T(8,128)(2,1)S(1)} collective-permute-done((bf16[4,128,128]{2,1,0:T(8,128)(2,1)S(1)}, bf16[4,128,128]{2,1,0:T(8,128)(2,1)S(1)}, u32[]{:S(2)}, u32[]{:S(2)}) %collective-permute-start.4) | collective-permute-done | bytes 131104 | tf_op jit(solution)/shard_map/ppermute | solution.py:280
  56.7 3.7 %collective-permute-done.5.refs_3_ = bf16[4,128,128]{2,1,0:T(8,128)(2,1)S(1)} collective-permute-done((bf16[4,128,128]{2,1,0:T(8,128)(2,1)S(1)}, bf16[4,128,128]{2,1,0:T(8,128)(2,1)S(1)}, u32[]{:S(2)}, u32[]{:S(2)}) %collective-permute-start.5) | collective-permute-done | bytes 131104 | tf_op jit(solution)/shard_map/ppermute | solution.py:280
  60.5 1.5 shard_map.123.near_ref
  61.9 14.1 %all-to-all-done.recv_ref = bf16[48,128,128]{2,1,0:T(8,128)(2,1)} async-done(((bf16[48,128,128]{2,1,0:T(8,128)(2,1)}), bf16[48,128,128]{2,1,0:T(8,128)(2,1)}, u32[]{:S(2)}, u32[]{:S(2)}) %all-to-all-start) | async-done | bytes 1572896 | tf_op jit(solution)/shard_map/all_to_all | solution.py:333
  76.1 5.8 %shard_map.124 = (bf16[512,128]{1,0:T(8,128)(2,1)}, bf16[48,128,128]{2,1,0:T(8,128)(2,1)S(1)}, bf16[5,128,128]{2,1,0:T(8,128)(2,1)S(1)}, f32[128,128]{1,0:T(8,128)S(1)}, f32[1,128]{1,0:T(1,128)S(1)}) custom-call(s32[2,80]{1,0:T(2,128)S(1)} %bitcast.10, s32[4,128]{1,0:T(4,128)S(1)} %bitcast.13, bf16[80,128,128]{2,1,0:T(8,128)(2,1)} %tiles_ref.5, ...), custom_call_target="tpu_custom_call" | custom-call | flops 671088640 | bytes 7864320 | tf_op jit(solution)/shard_map/pallas_call | solution.py:351
  83.1 12.3 %all-to-all-start.1 = ((bf16[48,128,128]{2,1,0:T(8,128)(2,1)}), bf16[48,128,128]{2,1,0:T(8,128)(2,1)}, u32[]{:S(2)}, u32[]{:S(2)}) async-start(bf16[48,128,128]{2,1,0:T(8,128)(2,1)} %copy-done.2), calls=%async_computation.1 | async-start | bytes 3145728 | tf_op jit(solution)/shard_map/all_to_all | solution.py:368
  96.6 4.2 %collective-permute-start.6 = (bf16[4,160,128]{2,1,0:T(8,128)(2,1)S(1)}, bf16[4,160,128]{2,1,0:T(8,128)(2,1)S(1)}, u32[]{:S(2)}, u32[]{:S(2)}) collective-permute-start(bf16[4,160,128]{2,1,0:T(8,128)(2,1)S(1)} %get-tuple-element.46), channel_id=1, source_target_pairs={{0,4},{1,5},{2,6},{3,7},{4,0},{5,1},{6,2},{7,3},{8,12},{9,13},{10,... | collective-permute-start | bytes 491528 | tf_op jit(solution)/shard_map/ppermute | solution.py:280
  100.8 5.7 %collective-permute-start.7 = (bf16[4,160,128]{2,1,0:T(8,128)(2,1)S(1)}, bf16[4,160,128]{2,1,0:T(8,128)(2,1)S(1)}, u32[]{:S(2)}, u32[]{:S(2)}) collective-permute-start(bf16[4,160,128]{2,1,0:T(8,128)(2,1)S(1)} %get-tuple-element.47), channel_id=1, source_target_pairs={{0,8},{1,9},{2,10},{3,11},{4,12},{5,13},{6,14},{7,15},{8,0},{9,1},... | collective-permute-start | bytes 491528 | tf_op jit(solution)/shard_map/ppermute | solution.py:280
  106.5 1.9 %collective-permute-start.8 = (bf16[4,160,128]{2,1,0:T(8,128)(2,1)S(1)}, bf16[4,160,128]{2,1,0:T(8,128)(2,1)S(1)}, u32[]{:S(2)}, u32[]{:S(2)}) collective-permute-start(bf16[4,160,128]{2,1,0:T(8,128)(2,1)S(1)} %get-tuple-element.48), channel_id=1, source_target_pairs={{0,12},{1,13},{2,14},{3,15},{4,8},{5,9},{6,10},{7,11},{8,4},{9,5},... | collective-permute-start | bytes 491528 | tf_op jit(solution)/shard_map/ppermute | solution.py:280
  108.4 3.4 %collective-permute-done.7.refs_2_ = bf16[4,160,128]{2,1,0:T(8,128)(2,1)S(1)} collective-permute-done((bf16[4,160,128]{2,1,0:T(8,128)(2,1)S(1)}, bf16[4,160,128]{2,1,0:T(8,128)(2,1)S(1)}, u32[]{:S(2)}, u32[]{:S(2)}) %collective-permute-start.7) | collective-permute-done | bytes 163872 | tf_op jit(solution)/shard_map/ppermute | solution.py:280
  111.9 10.2 %collective-permute-done.8.refs_3_ = bf16[4,160,128]{2,1,0:T(8,128)(2,1)S(1)} collective-permute-done((bf16[4,160,128]{2,1,0:T(8,128)(2,1)S(1)}, bf16[4,160,128]{2,1,0:T(8,128)(2,1)S(1)}, u32[]{:S(2)}, u32[]{:S(2)}) %collective-permute-start.8) | collective-permute-done | bytes 163872 | tf_op jit(solution)/shard_map/ppermute | solution.py:280
  122.1 2.4 %collective-permute-start.9 = (bf16[4,160,128]{2,1,0:T(8,128)(2,1)S(1)}, bf16[4,160,128]{2,1,0:T(8,128)(2,1)S(1)}, u32[]{:S(2)}, u32[]{:S(2)}) collective-permute-start(bf16[4,160,128]{2,1,0:T(8,128)(2,1)S(1)} %get-tuple-element.50), channel_id=1, source_target_pairs={{0,1},{1,0},{2,3},{3,2},{4,5},{5,4},{6,7},{7,6},{8,9},{9,8},{10,11... | collective-permute-start | bytes 491528 | tf_op jit(solution)/shard_map/ppermute | solution.py:280
  124.5 2.5 %collective-permute-start.10 = (bf16[4,160,128]{2,1,0:T(8,128)(2,1)S(1)}, bf16[4,160,128]{2,1,0:T(8,128)(2,1)S(1)}, u32[]{:S(2)}, u32[]{:S(2)}) collective-permute-start(bf16[4,160,128]{2,1,0:T(8,128)(2,1)S(1)} %get-tuple-element.51), channel_id=1, source_target_pairs={{0,2},{1,3},{2,0},{3,1},{4,6},{5,7},{6,4},{7,5},{8,10},{9,11},{10,... | collective-permute-start | bytes 491528 | tf_op jit(solution)/shard_map/ppermute | solution.py:280
  127.0 3.0 %collective-permute-start.11 = (bf16[4,160,128]{2,1,0:T(8,128)(2,1)S(1)}, bf16[4,160,128]{2,1,0:T(8,128)(2,1)S(1)}, u32[]{:S(2)}, u32[]{:S(2)}) collective-permute-start(bf16[4,160,128]{2,1,0:T(8,128)(2,1)S(1)} %get-tuple-element.52), channel_id=1, source_target_pairs={{0,3},{1,2},{2,1},{3,0},{4,7},{5,6},{6,5},{7,4},{8,11},{9,10},{10,... | collective-permute-start | bytes 491528 | tf_op jit(solution)/shard_map/ppermute | solution.py:280
  130.0 2.3 %collective-permute-done.10.refs_2_ = bf16[4,160,128]{2,1,0:T(8,128)(2,1)S(1)} collective-permute-done((bf16[4,160,128]{2,1,0:T(8,128)(2,1)S(1)}, bf16[4,160,128]{2,1,0:T(8,128)(2,1)S(1)}, u32[]{:S(2)}, u32[]{:S(2)}) %collective-permute-start.10) | collective-permute-done | bytes 163872 | tf_op jit(solution)/shard_map/ppermute | solution.py:280
  132.3 3.5 %collective-permute-done.11.refs_3_ = bf16[4,160,128]{2,1,0:T(8,128)(2,1)S(1)} collective-permute-done((bf16[4,160,128]{2,1,0:T(8,128)(2,1)S(1)}, bf16[4,160,128]{2,1,0:T(8,128)(2,1)S(1)}, u32[]{:S(2)}, u32[]{:S(2)}) %collective-permute-start.11) | collective-permute-done | bytes 163872 | tf_op jit(solution)/shard_map/ppermute | solution.py:280
  135.9 10.3 %all-gather = f32[64,128]{1,0:T(8,128)S(1)} all-gather(f32[16,128]{1,0:T(8,128)S(1)} %shard_map.128), channel_id=2, replica_groups={{0,192,384,576},{16,208,400,592},{32,224,416,608},{48,240,432,624},{64,..., dimensions={0}, use_global_device_ids=true | all-gather | bytes 40960 | tf_op jit(solution)/shard_map/all_gather | solution.py:390
  148.2 9.1 %all-to-all-start.2 = ((f32[12,16,128]{2,1,0:T(8,128)}), f32[12,16,128]{2,1,0:T(8,128)S(1)}, u32[]{:S(2)}, u32[]{:S(2)}) async-start(f32[12,16,128]{2,1,0:T(8,128)} %shard_map.129), calls=%async_computation.2 | async-start | bytes 196608 | tf_op jit(solution)/shard_map/all_to_all | solution.py:399
  158.0 4.8 %shard_map.130 = bf16[512,128]{1,0:T(8,128)(2,1)} custom-call(s32[4,128]{1,0:T(4,128)S(1)} %bitcast.14, s32[48,128]{1,0:T(8,128)S(1)} %copy-done.10, f32[512,128]{1,0:T(8,128)S(1)} %shard_map.127.near_ref, bf16[48,128,128]{2,1,0:T(8,128)(2,1)} %all-to-all-done.1.recv_ref), custom_call_target="tpu_custom_call" | custom-call | flops 805306368 | bytes 1572864 | tf_op jit(solution)/shard_map/pallas_call | solution.py:413
  162.9 4.5 %all-to-all-done.2 = f32[12,16,128]{2,1,0:T(8,128)S(1)} async-done(((f32[12,16,128]{2,1,0:T(8,128)}), f32[12,16,128]{2,1,0:T(8,128)S(1)}, u32[]{:S(2)}, u32[]{:S(2)}) %all-to-all-start.2) | async-done | bytes 98336 | tf_op jit(solution)/shard_map/all_to_all | solution.py:399
  168.1 10.0 %all-to-all-start.3 = ((f32[16,8,128]{2,1,0:T(8,128)}), f32[16,8,128]{2,1,0:T(8,128)S(1)}, u32[]{:S(2)}, u32[]{:S(2)}) async-start(f32[16,8,128]{2,1,0:T(8,128)} %broadcast_in_dim.3), calls=%async_computation.3 | async-start | bytes 131072 | tf_op jit(solution)/shard_map/all_to_all | solution.py:403
  178.6 7.3 %all-to-all-done.3 = f32[16,8,128]{2,1,0:T(8,128)S(1)} async-done(((f32[16,8,128]{2,1,0:T(8,128)}), f32[16,8,128]{2,1,0:T(8,128)S(1)}, u32[]{:S(2)}, u32[]{:S(2)}) %all-to-all-start.3) | async-done | bytes 65568 | tf_op jit(solution)/shard_map/all_to_all | solution.py:403
  (40 shorter events, 7.7 us)
Async XLA Ops:
  4.2 19.4 %copy-start.4 = (bf16[4,128,128]{2,1,0:T(8,128)(2,1)S(1)}, bf16[4,128,128]{2,1,0:T(8,128)(2,1)}, u32[]{:S(2)}) copy-start(bf16[4,128,128]{2,1,0:T(8,128)(2,1)} %get-tuple-element.31.scaled_ref) | copy-start | bytes 393220
  4.2 19.4 %copy-start.7 = (s32[16,128]{1,0:T(8,128)S(1)}, s32[16,128]{1,0:T(8,128)}, u32[]{:S(2)}) copy-start(s32[16,128]{1,0:T(8,128)} %lists_ref.4) | copy-start | bytes 24580
  4.2 56.2 %copy-start = (bf16[80,128,128]{2,1,0:T(8,128)(2,1)S(1)}, bf16[80,128,128]{2,1,0:T(8,128)(2,1)}, u32[]{:S(2)}) copy-start(bf16[80,128,128]{2,1,0:T(8,128)(2,1)} %tiles_ref.5) | copy-start | bytes 7864324
  4.2 56.2 %copy-start.6 = (s32[80,2]{0,1:T(2,128)S(1)}, s32[80,2]{0,1:T(2,128)}, u32[]{:S(2)}) copy-start(s32[80,2]{0,1:T(2,128)} %param.12) | copy-start | bytes 1924
  4.2 71.9 %all-to-all-start = ((bf16[48,128,128]{2,1,0:T(8,128)(2,1)}), bf16[48,128,128]{2,1,0:T(8,128)(2,1)}, u32[]{:S(2)}, u32[]{:S(2)}) async-start(bf16[48,128,128]{2,1,0:T(8,128)(2,1)} %get-tuple-element.30), calls=%async_computation | async-start | bytes 3145728 | tf_op jit(solution)/shard_map/all_to_all | solution.py:333
  24.3 11.8 %collective-permute-start = (bf16[4,128,128]{2,1,0:T(8,128)(2,1)S(1)}, bf16[4,128,128]{2,1,0:T(8,128)(2,1)S(1)}, u32[]{:S(2)}, u32[]{:S(2)}) collective-permute-start(bf16[4,128,128]{2,1,0:T(8,128)(2,1)S(1)} %get-tuple-element.33), channel_id=1, source_target_pairs={{0,4},{1,5},{2,6},{3,7},{4,0},{5,1},{6,2},{7,3},{8,12},{9,13},{10,... | collective-permute-start | bytes 393224 | tf_op jit(solution)/shard_map/ppermute | solution.py:280
  28.5 10.1 %collective-permute-start.1 = (bf16[4,128,128]{2,1,0:T(8,128)(2,1)S(1)}, bf16[4,128,128]{2,1,0:T(8,128)(2,1)S(1)}, u32[]{:S(2)}, u32[]{:S(2)}) collective-permute-start(bf16[4,128,128]{2,1,0:T(8,128)(2,1)S(1)} %get-tuple-element.34), channel_id=1, source_target_pairs={{0,8},{1,9},{2,10},{3,11},{4,12},{5,13},{6,14},{7,15},{8,0},{9,1},... | collective-permute-start | bytes 393224 | tf_op jit(solution)/shard_map/ppermute | solution.py:280
  34.1 11.9 %collective-permute-start.2 = (bf16[4,128,128]{2,1,0:T(8,128)(2,1)S(1)}, bf16[4,128,128]{2,1,0:T(8,128)(2,1)S(1)}, u32[]{:S(2)}, u32[]{:S(2)}) collective-permute-start(bf16[4,128,128]{2,1,0:T(8,128)(2,1)S(1)} %get-tuple-element.35), channel_id=1, source_target_pairs={{0,12},{1,13},{2,14},{3,15},{4,8},{5,9},{6,10},{7,11},{8,4},{9,5},... | collective-permute-start | bytes 393224 | tf_op jit(solution)/shard_map/ppermute | solution.py:280
  46.1 8.6 %collective-permute-start.3 = (bf16[4,128,128]{2,1,0:T(8,128)(2,1)S(1)}, bf16[4,128,128]{2,1,0:T(8,128)(2,1)S(1)}, u32[]{:S(2)}, u32[]{:S(2)}) collective-permute-start(bf16[4,128,128]{2,1,0:T(8,128)(2,1)S(1)} %get-tuple-element.37), channel_id=1, source_target_pairs={{0,1},{1,0},{2,3},{3,2},{4,5},{5,4},{6,7},{7,6},{8,9},{9,8},{10,11... | collective-permute-start | bytes 393224 | tf_op jit(solution)/shard_map/ppermute | solution.py:280
  48.5 8.2 %collective-permute-start.4 = (bf16[4,128,128]{2,1,0:T(8,128)(2,1)S(1)}, bf16[4,128,128]{2,1,0:T(8,128)(2,1)S(1)}, u32[]{:S(2)}, u32[]{:S(2)}) collective-permute-start(bf16[4,128,128]{2,1,0:T(8,128)(2,1)S(1)} %get-tuple-element.38), channel_id=1, source_target_pairs={{0,2},{1,3},{2,0},{3,1},{4,6},{5,7},{6,4},{7,5},{8,10},{9,11},{10,... | collective-permute-start | bytes 393224 | tf_op jit(solution)/shard_map/ppermute | solution.py:280
  52.7 7.7 %collective-permute-start.5 = (bf16[4,128,128]{2,1,0:T(8,128)(2,1)S(1)}, bf16[4,128,128]{2,1,0:T(8,128)(2,1)S(1)}, u32[]{:S(2)}, u32[]{:S(2)}) collective-permute-start(bf16[4,128,128]{2,1,0:T(8,128)(2,1)S(1)} %get-tuple-element.39), channel_id=1, source_target_pairs={{0,3},{1,2},{2,1},{3,0},{4,7},{5,6},{6,5},{7,4},{8,11},{9,10},{10,... | collective-permute-start | bytes 393224 | tf_op jit(solution)/shard_map/ppermute | solution.py:280
  60.4 15.6 %copy-start.3 = (bf16[512,128]{1,0:T(8,128)(2,1)S(1)}, bf16[512,128]{1,0:T(8,128)(2,1)}, u32[]{:S(2)}) copy-start(bf16[512,128]{1,0:T(8,128)(2,1)} %cotangent_ref.1) | copy-start | bytes 393220
  60.4 15.6 %copy-start.5 = (bf16[128,128]{1,0:T(8,128)(2,1)S(1)}, bf16[128,128]{1,0:T(8,128)(2,1)}, u32[]{:S(2)}) copy-start(bf16[128,128]{1,0:T(8,128)(2,1)} %weight_ref.1) | copy-start | bytes 98308
  60.4 15.6 %copy-start.8 = (s32[512]{0:T(512)S(1)}, s32[512]{0:T(512)}, u32[]{:S(2)}) copy-start(s32[512]{0:T(512)} %param.10) | copy-start | bytes 6148
  60.4 15.6 %copy-start.9 = (f32[128]{0:T(128)S(1)}, f32[128]{0:T(128)}, u32[]{:S(2)}) copy-start(f32[128]{0:T(128)} %param.16) | copy-start | bytes 1540
  81.9 1.2 copy-start.2
  83.1 12.4 %copy-start.1 = (bf16[80,128,128]{2,1,0:T(8,128)(2,1)S(1)}, bf16[80,128,128]{2,1,0:T(8,128)(2,1)}, u32[]{:S(2)}) copy-start(bf16[80,128,128]{2,1,0:T(8,128)(2,1)} %tiles_ref.5) | copy-start | bytes 7864324
  83.1 65.1 %all-to-all-start.1 = ((bf16[48,128,128]{2,1,0:T(8,128)(2,1)}), bf16[48,128,128]{2,1,0:T(8,128)(2,1)}, u32[]{:S(2)}, u32[]{:S(2)}) async-start(bf16[48,128,128]{2,1,0:T(8,128)(2,1)} %copy-done.2), calls=%async_computation.1 | async-start | bytes 3145728 | tf_op jit(solution)/shard_map/all_to_all | solution.py:368
  96.6 61.4 %copy-start.10 = (s32[48,128]{1,0:T(8,128)S(1)}, s32[48,128]{1,0:T(8,128)}, u32[]{:S(2)}) copy-start(s32[48,128]{1,0:T(8,128)} %lists_ref.5) | copy-start | bytes 73732
  96.6 11.8 %collective-permute-start.6 = (bf16[4,160,128]{2,1,0:T(8,128)(2,1)S(1)}, bf16[4,160,128]{2,1,0:T(8,128)(2,1)S(1)}, u32[]{:S(2)}, u32[]{:S(2)}) collective-permute-start(bf16[4,160,128]{2,1,0:T(8,128)(2,1)S(1)} %get-tuple-element.46), channel_id=1, source_target_pairs={{0,4},{1,5},{2,6},{3,7},{4,0},{5,1},{6,2},{7,3},{8,12},{9,13},{10,... | collective-permute-start | bytes 491528 | tf_op jit(solution)/shard_map/ppermute | solution.py:280
  100.8 11.1 %collective-permute-start.7 = (bf16[4,160,128]{2,1,0:T(8,128)(2,1)S(1)}, bf16[4,160,128]{2,1,0:T(8,128)(2,1)S(1)}, u32[]{:S(2)}, u32[]{:S(2)}) collective-permute-start(bf16[4,160,128]{2,1,0:T(8,128)(2,1)S(1)} %get-tuple-element.47), channel_id=1, source_target_pairs={{0,8},{1,9},{2,10},{3,11},{4,12},{5,13},{6,14},{7,15},{8,0},{9,1},... | collective-permute-start | bytes 491528 | tf_op jit(solution)/shard_map/ppermute | solution.py:280
  106.5 15.6 %collective-permute-start.8 = (bf16[4,160,128]{2,1,0:T(8,128)(2,1)S(1)}, bf16[4,160,128]{2,1,0:T(8,128)(2,1)S(1)}, u32[]{:S(2)}, u32[]{:S(2)}) collective-permute-start(bf16[4,160,128]{2,1,0:T(8,128)(2,1)S(1)} %get-tuple-element.48), channel_id=1, source_target_pairs={{0,12},{1,13},{2,14},{3,15},{4,8},{5,9},{6,10},{7,11},{8,4},{9,5},... | collective-permute-start | bytes 491528 | tf_op jit(solution)/shard_map/ppermute | solution.py:280
  122.1 7.9 %collective-permute-start.9 = (bf16[4,160,128]{2,1,0:T(8,128)(2,1)S(1)}, bf16[4,160,128]{2,1,0:T(8,128)(2,1)S(1)}, u32[]{:S(2)}, u32[]{:S(2)}) collective-permute-start(bf16[4,160,128]{2,1,0:T(8,128)(2,1)S(1)} %get-tuple-element.50), channel_id=1, source_target_pairs={{0,1},{1,0},{2,3},{3,2},{4,5},{5,4},{6,7},{7,6},{8,9},{9,8},{10,11... | collective-permute-start | bytes 491528 | tf_op jit(solution)/shard_map/ppermute | solution.py:280
  124.5 7.8 %collective-permute-start.10 = (bf16[4,160,128]{2,1,0:T(8,128)(2,1)S(1)}, bf16[4,160,128]{2,1,0:T(8,128)(2,1)S(1)}, u32[]{:S(2)}, u32[]{:S(2)}) collective-permute-start(bf16[4,160,128]{2,1,0:T(8,128)(2,1)S(1)} %get-tuple-element.51), channel_id=1, source_target_pairs={{0,2},{1,3},{2,0},{3,1},{4,6},{5,7},{6,4},{7,5},{8,10},{9,11},{10,... | collective-permute-start | bytes 491528 | tf_op jit(solution)/shard_map/ppermute | solution.py:280
  127.0 8.8 %collective-permute-start.11 = (bf16[4,160,128]{2,1,0:T(8,128)(2,1)S(1)}, bf16[4,160,128]{2,1,0:T(8,128)(2,1)S(1)}, u32[]{:S(2)}, u32[]{:S(2)}) collective-permute-start(bf16[4,160,128]{2,1,0:T(8,128)(2,1)S(1)} %get-tuple-element.52), channel_id=1, source_target_pairs={{0,3},{1,2},{2,1},{3,0},{4,7},{5,6},{6,5},{7,4},{8,11},{9,10},{10,... | collective-permute-start | bytes 491528 | tf_op jit(solution)/shard_map/ppermute | solution.py:280
  148.2 19.2 %all-to-all-start.2 = ((f32[12,16,128]{2,1,0:T(8,128)}), f32[12,16,128]{2,1,0:T(8,128)S(1)}, u32[]{:S(2)}, u32[]{:S(2)}) async-start(f32[12,16,128]{2,1,0:T(8,128)} %shard_map.129), calls=%async_computation.2 | async-start | bytes 196608 | tf_op jit(solution)/shard_map/all_to_all | solution.py:399
  168.1 17.8 %all-to-all-start.3 = ((f32[16,8,128]{2,1,0:T(8,128)}), f32[16,8,128]{2,1,0:T(8,128)S(1)}, u32[]{:S(2)}, u32[]{:S(2)}) async-start(f32[16,8,128]{2,1,0:T(8,128)} %broadcast_in_dim.3), calls=%async_computation.3 | async-start | bytes 131072 | tf_op jit(solution)/shard_map/all_to_all | solution.py:403

commit v5 on v4

--- a/solution.py
+++ b/solution.py
@@ -399,9 +399,7 @@
     pieces = lax.all_to_all(copies, "dom", 0, 0, axis_index_groups=along_z, tiled=True)
     chunk = jnp.sum(pieces, axis=0) * (1.0 / math.sqrt(ROWS * dom * grp))
     grad_bias = chunk[depth]
-    copies = jnp.broadcast_to(chunk[:depth], (grp, depth, TILE))
-    grad_weight = lax.all_to_all(copies, "grp", split_axis=0, concat_axis=0, tiled=True)
-    grad_weight = grad_weight.reshape(TILE, TILE)
+    grad_weight = lax.all_gather(chunk[:depth], "grp", tiled=True)
 
     near_grad = call(
         near_scatter,

time: 187 us -> 190 us (1.016)
  blocking collectives: 10.3 us -> 30.8 us
  starting transfers between devices: 90.7 us -> 80.8 us
  waiting for transfers between devices: 62.5 us -> 55.3 us
    all_gather x0 -> x1, blocking collectives: none -> 20.5 us  [body(): grad_weight = lax.all_gather(chunk[:depth], 'grp', tiled=True)]
    all_to_all x1 -> x0, starting transfers between devices: 9.96 us -> none  [body(): lax.all_to_all(copies, 'grp', split_axis=0, concat_axis=0, tiled=True)]
    all_to_all x1 -> x0, waiting for transfers between devices: 7.3 us -> none  [body(): lax.all_to_all(copies, 'grp', split_axis=0, concat_axis=0, tiled=True)]
  transfers between devices with their start and end apart: 16 -> 15, of which waited for: 12 -> 11; matrix products, arithmetic and copies ran while one was open for 0% -> 0% of each run, Pallas kernels for 5% -> 5%
where the time goes in v5:
time: 190 us; the launch traced here: 189 us
  starting transfers between devices  80.8 us (43%)
  waiting for transfers between devices  55.3 us (29%)
  blocking collectives  30.8 us (16%)
  Pallas kernels  18.9 us (10%)
  local copies, waits for them, and re-layouts  2.34 us (1%)
    ppermute x12, starting transfers between devices, xor_permute(): return lax.ppermute(value, axis, [(i, i ^ k) for i in range(size)])  40 us
    ppermute x12, waiting for transfers between devices, xor_permute(): return lax.ppermute(value, axis, [(i, i ^ k) for i in range(size)])  35.2 us
    all_gather x1, blocking collectives, body(): grad_weight = lax.all_gather(chunk[:depth], 'grp', tiled=True)  20.5 us
    all_to_all x1, starting transfers between devices, body(): lax.all_to_all(to_dom, 'dom', split_axis=0, concat_axis=0, tiled=True)  19.3 us
    all_to_all x1, waiting for transfers between devices, body(): lax.all_to_all(to_dom, 'dom', split_axis=0, concat_axis=0, tiled=True)  14.1 us
    all_to_all x1, starting transfers between devices, body(): lax.all_to_all(to_lender, 'dom', split_axis=0, concat_axis=0, tiled=True)  12.4 us
    all_gather x1, blocking collectives, body(): pieces = lax.all_gather(chunk, 'dom', axis_index_groups=along_x)  10.3 us
    all_to_all x1, starting transfers between devices, body(): lax.all_to_all(copies, 'dom', 0, 0, axis_index_groups=along_z, tiled=True)  9.09 us
  transfers between devices with their start and end apart: 15, of which 11 were waited for; matrix products, arithmetic and copies ran while one was open for 0% of the time, Pallas kernels for 5%

profile of v5, /device:TPU:1, one launch (start us, length us, event | category | flops | bytes accessed | tf_op | source)
XLA Modules:
  0.0 189.1 jit_solution(6571186824863007754)
XLA Ops:
  0.6 3.5 %shard_map.120 = (bf16[48,128,128]{2,1,0:T(8,128)(2,1)}, bf16[4,128,128]{2,1,0:T(8,128)(2,1)}) custom-call(s32[4,128]{1,0:T(4,128)} %bitcast.11, bf16[512,128]{1,0:T(8,128)(2,1)} %features_hbm.1, s32[48,128]{1,0:T(8,128)} %lists_ref.5), custom_call_target="tpu_custom_call" | custom-call | flops 805306368 | bytes 1572864 | tf_op jit(solution)/shard_map/pallas_call | solution.py:316
  4.2 19.3 %all-to-all-start = ((bf16[48,128,128]{2,1,0:T(8,128)(2,1)}), bf16[48,128,128]{2,1,0:T(8,128)(2,1)}, u32[]{:S(2)}, u32[]{:S(2)}) async-start(bf16[48,128,128]{2,1,0:T(8,128)(2,1)} %get-tuple-element.30), calls=%async_computation | async-start | bytes 3145728 | tf_op jit(solution)/shard_map/all_to_all | solution.py:333
  24.2 4.2 %collective-permute-start = (bf16[4,128,128]{2,1,0:T(8,128)(2,1)S(1)}, bf16[4,128,128]{2,1,0:T(8,128)(2,1)S(1)}, u32[]{:S(2)}, u32[]{:S(2)}) collective-permute-start(bf16[4,128,128]{2,1,0:T(8,128)(2,1)S(1)} %get-tuple-element.33), channel_id=1, source_target_pairs={{0,4},{1,5},{2,6},{3,7},{4,0},{5,1},{6,2},{7,3},{8,12},{9,13},{10,... | collective-permute-start | bytes 393224 | tf_op jit(solution)/shard_map/ppermute | solution.py:280
  28.5 5.7 %collective-permute-start.1 = (bf16[4,128,128]{2,1,0:T(8,128)(2,1)S(1)}, bf16[4,128,128]{2,1,0:T(8,128)(2,1)S(1)}, u32[]{:S(2)}, u32[]{:S(2)}) collective-permute-start(bf16[4,128,128]{2,1,0:T(8,128)(2,1)S(1)} %get-tuple-element.34), channel_id=1, source_target_pairs={{0,8},{1,9},{2,10},{3,11},{4,12},{5,13},{6,14},{7,15},{8,0},{9,1},... | collective-permute-start | bytes 393224 | tf_op jit(solution)/shard_map/ppermute | solution.py:280
  34.1 1.9 %collective-permute-start.2 = (bf16[4,128,128]{2,1,0:T(8,128)(2,1)S(1)}, bf16[4,128,128]{2,1,0:T(8,128)(2,1)S(1)}, u32[]{:S(2)}, u32[]{:S(2)}) collective-permute-start(bf16[4,128,128]{2,1,0:T(8,128)(2,1)S(1)} %get-tuple-element.35), channel_id=1, source_target_pairs={{0,12},{1,13},{2,14},{3,15},{4,8},{5,9},{6,10},{7,11},{8,4},{9,5},... | collective-permute-start | bytes 393224 | tf_op jit(solution)/shard_map/ppermute | solution.py:280
  36.1 2.5 %collective-permute-done.1.refs_2_ = bf16[4,128,128]{2,1,0:T(8,128)(2,1)S(1)} collective-permute-done((bf16[4,128,128]{2,1,0:T(8,128)(2,1)S(1)}, bf16[4,128,128]{2,1,0:T(8,128)(2,1)S(1)}, u32[]{:S(2)}, u32[]{:S(2)}) %collective-permute-start.1) | collective-permute-done | bytes 131104 | tf_op jit(solution)/shard_map/ppermute | solution.py:280
  38.6 7.5 %collective-permute-done.2.refs_3_ = bf16[4,128,128]{2,1,0:T(8,128)(2,1)S(1)} collective-permute-done((bf16[4,128,128]{2,1,0:T(8,128)(2,1)S(1)}, bf16[4,128,128]{2,1,0:T(8,128)(2,1)S(1)}, u32[]{:S(2)}, u32[]{:S(2)}) %collective-permute-start.2) | collective-permute-done | bytes 131104 | tf_op jit(solution)/shard_map/ppermute | solution.py:280
  46.1 2.4 %collective-permute-start.3 = (bf16[4,128,128]{2,1,0:T(8,128)(2,1)S(1)}, bf16[4,128,128]{2,1,0:T(8,128)(2,1)S(1)}, u32[]{:S(2)}, u32[]{:S(2)}) collective-permute-start(bf16[4,128,128]{2,1,0:T(8,128)(2,1)S(1)} %get-tuple-element.37), channel_id=1, source_target_pairs={{0,1},{1,0},{2,3},{3,2},{4,5},{5,4},{6,7},{7,6},{8,9},{9,8},{10,11... | collective-permute-start | bytes 393224 | tf_op jit(solution)/shard_map/ppermute | solution.py:280
  48.5 4.2 %collective-permute-start.4 = (bf16[4,128,128]{2,1,0:T(8,128)(2,1)S(1)}, bf16[4,128,128]{2,1,0:T(8,128)(2,1)S(1)}, u32[]{:S(2)}, u32[]{:S(2)}) collective-permute-start(bf16[4,128,128]{2,1,0:T(8,128)(2,1)S(1)} %get-tuple-element.38), channel_id=1, source_target_pairs={{0,2},{1,3},{2,0},{3,1},{4,6},{5,7},{6,4},{7,5},{8,10},{9,11},{10,... | collective-permute-start | bytes 393224 | tf_op jit(solution)/shard_map/ppermute | solution.py:280
  52.7 1.9 %collective-permute-start.5 = (bf16[4,128,128]{2,1,0:T(8,128)(2,1)S(1)}, bf16[4,128,128]{2,1,0:T(8,128)(2,1)S(1)}, u32[]{:S(2)}, u32[]{:S(2)}) collective-permute-start(bf16[4,128,128]{2,1,0:T(8,128)(2,1)S(1)} %get-tuple-element.39), channel_id=1, source_target_pairs={{0,3},{1,2},{2,1},{3,0},{4,7},{5,6},{6,5},{7,4},{8,11},{9,10},{10,... | collective-permute-start | bytes 393224 | tf_op jit(solution)/shard_map/ppermute | solution.py:280
  54.6 2.0 %collective-permute-done.4.refs_2_ = bf16[4,128,128]{2,1,0:T(8,128)(2,1)S(1)} collective-permute-done((bf16[4,128,128]{2,1,0:T(8,128)(2,1)S(1)}, bf16[4,128,128]{2,1,0:T(8,128)(2,1)S(1)}, u32[]{:S(2)}, u32[]{:S(2)}) %collective-permute-start.4) | collective-permute-done | bytes 131104 | tf_op jit(solution)/shard_map/ppermute | solution.py:280
  56.7 3.7 %collective-permute-done.5.refs_3_ = bf16[4,128,128]{2,1,0:T(8,128)(2,1)S(1)} collective-permute-done((bf16[4,128,128]{2,1,0:T(8,128)(2,1)S(1)}, bf16[4,128,128]{2,1,0:T(8,128)(2,1)S(1)}, u32[]{:S(2)}, u32[]{:S(2)}) %collective-permute-start.5) | collective-permute-done | bytes 131104 | tf_op jit(solution)/shard_map/ppermute | solution.py:280
  60.4 1.5 shard_map.123.near_ref
  61.9 14.1 %all-to-all-done.recv_ref = bf16[48,128,128]{2,1,0:T(8,128)(2,1)} async-done(((bf16[48,128,128]{2,1,0:T(8,128)(2,1)}), bf16[48,128,128]{2,1,0:T(8,128)(2,1)}, u32[]{:S(2)}, u32[]{:S(2)}) %all-to-all-start) | async-done | bytes 1572896 | tf_op jit(solution)/shard_map/all_to_all | solution.py:333
  76.1 5.8 %shard_map.124 = (bf16[512,128]{1,0:T(8,128)(2,1)}, bf16[48,128,128]{2,1,0:T(8,128)(2,1)S(1)}, bf16[5,128,128]{2,1,0:T(8,128)(2,1)S(1)}, f32[128,128]{1,0:T(8,128)S(1)}, f32[1,128]{1,0:T(1,128)S(1)}) custom-call(s32[2,80]{1,0:T(2,128)S(1)} %bitcast.9, s32[4,128]{1,0:T(4,128)S(1)} %bitcast.12, bf16[80,128,128]{2,1,0:T(8,128)(2,1)} %tiles_ref.5, ...), custom_call_target="tpu_custom_call" | custom-call | flops 671088640 | bytes 7864320 | tf_op jit(solution)/shard_map/pallas_call | solution.py:351
  83.0 12.4 %all-to-all-start.1 = ((bf16[48,128,128]{2,1,0:T(8,128)(2,1)}), bf16[48,128,128]{2,1,0:T(8,128)(2,1)}, u32[]{:S(2)}, u32[]{:S(2)}) async-start(bf16[48,128,128]{2,1,0:T(8,128)(2,1)} %copy-done.2), calls=%async_computation.1 | async-start | bytes 3145728 | tf_op jit(solution)/shard_map/all_to_all | solution.py:368
  96.6 4.2 %collective-permute-start.6 = (bf16[4,160,128]{2,1,0:T(8,128)(2,1)S(1)}, bf16[4,160,128]{2,1,0:T(8,128)(2,1)S(1)}, u32[]{:S(2)}, u32[]{:S(2)}) collective-permute-start(bf16[4,160,128]{2,1,0:T(8,128)(2,1)S(1)} %get-tuple-element.46), channel_id=1, source_target_pairs={{0,4},{1,5},{2,6},{3,7},{4,0},{5,1},{6,2},{7,3},{8,12},{9,13},{10,... | collective-permute-start | bytes 491528 | tf_op jit(solution)/shard_map/ppermute | solution.py:280
  100.8 5.6 %collective-permute-start.7 = (bf16[4,160,128]{2,1,0:T(8,128)(2,1)S(1)}, bf16[4,160,128]{2,1,0:T(8,128)(2,1)S(1)}, u32[]{:S(2)}, u32[]{:S(2)}) collective-permute-start(bf16[4,160,128]{2,1,0:T(8,128)(2,1)S(1)} %get-tuple-element.47), channel_id=1, source_target_pairs={{0,8},{1,9},{2,10},{3,11},{4,12},{5,13},{6,14},{7,15},{8,0},{9,1},... | collective-permute-start | bytes 491528 | tf_op jit(solution)/shard_map/ppermute | solution.py:280
  106.5 1.9 %collective-permute-start.8 = (bf16[4,160,128]{2,1,0:T(8,128)(2,1)S(1)}, bf16[4,160,128]{2,1,0:T(8,128)(2,1)S(1)}, u32[]{:S(2)}, u32[]{:S(2)}) collective-permute-start(bf16[4,160,128]{2,1,0:T(8,128)(2,1)S(1)} %get-tuple-element.48), channel_id=1, source_target_pairs={{0,12},{1,13},{2,14},{3,15},{4,8},{5,9},{6,10},{7,11},{8,4},{9,5},... | collective-permute-start | bytes 491528 | tf_op jit(solution)/shard_map/ppermute | solution.py:280
  108.4 3.4 %collective-permute-done.7.refs_2_ = bf16[4,160,128]{2,1,0:T(8,128)(2,1)S(1)} collective-permute-done((bf16[4,160,128]{2,1,0:T(8,128)(2,1)S(1)}, bf16[4,160,128]{2,1,0:T(8,128)(2,1)S(1)}, u32[]{:S(2)}, u32[]{:S(2)}) %collective-permute-start.7) | collective-permute-done | bytes 163872 | tf_op jit(solution)/shard_map/ppermute | solution.py:280
  111.8 10.2 %collective-permute-done.8.refs_3_ = bf16[4,160,128]{2,1,0:T(8,128)(2,1)S(1)} collective-permute-done((bf16[4,160,128]{2,1,0:T(8,128)(2,1)S(1)}, bf16[4,160,128]{2,1,0:T(8,128)(2,1)S(1)}, u32[]{:S(2)}, u32[]{:S(2)}) %collective-permute-start.8) | collective-permute-done | bytes 163872 | tf_op jit(solution)/shard_map/ppermute | solution.py:280
  122.1 2.4 %collective-permute-start.9 = (bf16[4,160,128]{2,1,0:T(8,128)(2,1)S(1)}, bf16[4,160,128]{2,1,0:T(8,128)(2,1)S(1)}, u32[]{:S(2)}, u32[]{:S(2)}) collective-permute-start(bf16[4,160,128]{2,1,0:T(8,128)(2,1)S(1)} %get-tuple-element.50), channel_id=1, source_target_pairs={{0,1},{1,0},{2,3},{3,2},{4,5},{5,4},{6,7},{7,6},{8,9},{9,8},{10,11... | collective-permute-start | bytes 491528 | tf_op jit(solution)/shard_map/ppermute | solution.py:280
  124.5 2.5 %collective-permute-start.10 = (bf16[4,160,128]{2,1,0:T(8,128)(2,1)S(1)}, bf16[4,160,128]{2,1,0:T(8,128)(2,1)S(1)}, u32[]{:S(2)}, u32[]{:S(2)}) collective-permute-start(bf16[4,160,128]{2,1,0:T(8,128)(2,1)S(1)} %get-tuple-element.51), channel_id=1, source_target_pairs={{0,2},{1,3},{2,0},{3,1},{4,6},{5,7},{6,4},{7,5},{8,10},{9,11},{10,... | collective-permute-start | bytes 491528 | tf_op jit(solution)/shard_map/ppermute | solution.py:280
  127.0 3.0 %collective-permute-start.11 = (bf16[4,160,128]{2,1,0:T(8,128)(2,1)S(1)}, bf16[4,160,128]{2,1,0:T(8,128)(2,1)S(1)}, u32[]{:S(2)}, u32[]{:S(2)}) collective-permute-start(bf16[4,160,128]{2,1,0:T(8,128)(2,1)S(1)} %get-tuple-element.52), channel_id=1, source_target_pairs={{0,3},{1,2},{2,1},{3,0},{4,7},{5,6},{6,5},{7,4},{8,11},{9,10},{10,... | collective-permute-start | bytes 491528 | tf_op jit(solution)/shard_map/ppermute | solution.py:280
  130.0 2.3 %collective-permute-done.10.refs_2_ = bf16[4,160,128]{2,1,0:T(8,128)(2,1)S(1)} collective-permute-done((bf16[4,160,128]{2,1,0:T(8,128)(2,1)S(1)}, bf16[4,160,128]{2,1,0:T(8,128)(2,1)S(1)}, u32[]{:S(2)}, u32[]{:S(2)}) %collective-permute-start.10) | collective-permute-done | bytes 163872 | tf_op jit(solution)/shard_map/ppermute | solution.py:280
  132.3 3.5 %collective-permute-done.11.refs_3_ = bf16[4,160,128]{2,1,0:T(8,128)(2,1)S(1)} collective-permute-done((bf16[4,160,128]{2,1,0:T(8,128)(2,1)S(1)}, bf16[4,160,128]{2,1,0:T(8,128)(2,1)S(1)}, u32[]{:S(2)}, u32[]{:S(2)}) %collective-permute-start.11) | collective-permute-done | bytes 163872 | tf_op jit(solution)/shard_map/ppermute | solution.py:280
  135.9 10.3 %all-gather = f32[64,128]{1,0:T(8,128)S(1)} all-gather(f32[16,128]{1,0:T(8,128)S(1)} %shard_map.128), channel_id=2, replica_groups={{0,192,384,576},{16,208,400,592},{32,224,416,608},{48,240,432,624},{64,..., dimensions={0}, use_global_device_ids=true | all-gather | bytes 40960 | tf_op jit(solution)/shard_map/all_gather | solution.py:390
  146.8 1.4 all-to-all-done.1.recv_ref
  148.2 9.1 %all-to-all-start.2 = ((f32[12,16,128]{2,1,0:T(8,128)}), f32[12,16,128]{2,1,0:T(8,128)S(1)}, u32[]{:S(2)}, u32[]{:S(2)}) async-start(f32[12,16,128]{2,1,0:T(8,128)} %shard_map.129), calls=%async_computation.2 | async-start | bytes 196608 | tf_op jit(solution)/shard_map/all_to_all | solution.py:399
  158.0 4.8 %shard_map.130 = bf16[512,128]{1,0:T(8,128)(2,1)} custom-call(s32[4,128]{1,0:T(4,128)S(1)} %bitcast.13, s32[48,128]{1,0:T(8,128)S(1)} %copy-done.10, f32[512,128]{1,0:T(8,128)S(1)} %shard_map.127.near_ref, bf16[48,128,128]{2,1,0:T(8,128)(2,1)} %all-to-all-done.1.recv_ref), custom_call_target="tpu_custom_call" | custom-call | flops 805306368 | bytes 1572864 | tf_op jit(solution)/shard_map/pallas_call | solution.py:411
  162.9 4.5 %all-to-all-done.2 = f32[12,16,128]{2,1,0:T(8,128)S(1)} async-done(((f32[12,16,128]{2,1,0:T(8,128)}), f32[12,16,128]{2,1,0:T(8,128)S(1)}, u32[]{:S(2)}, u32[]{:S(2)}) %all-to-all-start.2) | async-done | bytes 98336 | tf_op jit(solution)/shard_map/all_to_all | solution.py:399
  168.0 20.5 %all_gather.11 = f32[128,128]{1,0:T(8,128)S(1)} all-gather(f32[8,128]{1,0:T(8,128)S(1)} %slice.8), channel_id=1, replica_groups=mesh['dom'=48,'grp'=16] {'grp'}, dimensions={0}, use_global_device_ids=true | all-gather | bytes 69632 | tf_op jit(solution)/shard_map/all_gather | solution.py:402
  (38 shorter events, 5.7 us)
Async XLA Ops:
  4.1 19.4 %copy-start.4 = (bf16[4,128,128]{2,1,0:T(8,128)(2,1)S(1)}, bf16[4,128,128]{2,1,0:T(8,128)(2,1)}, u32[]{:S(2)}) copy-start(bf16[4,128,128]{2,1,0:T(8,128)(2,1)} %get-tuple-element.31.scaled_ref) | copy-start | bytes 393220
  4.2 19.4 %copy-start.7 = (s32[16,128]{1,0:T(8,128)S(1)}, s32[16,128]{1,0:T(8,128)}, u32[]{:S(2)}) copy-start(s32[16,128]{1,0:T(8,128)} %lists_ref.4) | copy-start | bytes 24580
  4.2 56.2 %copy-start = (bf16[80,128,128]{2,1,0:T(8,128)(2,1)S(1)}, bf16[80,128,128]{2,1,0:T(8,128)(2,1)}, u32[]{:S(2)}) copy-start(bf16[80,128,128]{2,1,0:T(8,128)(2,1)} %tiles_ref.5) | copy-start | bytes 7864324
  4.2 56.2 %copy-start.6 = (s32[80,2]{0,1:T(2,128)S(1)}, s32[80,2]{0,1:T(2,128)}, u32[]{:S(2)}) copy-start(s32[80,2]{0,1:T(2,128)} %param.12) | copy-start | bytes 1924
  4.2 71.9 %all-to-all-start = ((bf16[48,128,128]{2,1,0:T(8,128)(2,1)}), bf16[48,128,128]{2,1,0:T(8,128)(2,1)}, u32[]{:S(2)}, u32[]{:S(2)}) async-start(bf16[48,128,128]{2,1,0:T(8,128)(2,1)} %get-tuple-element.30), calls=%async_computation | async-start | bytes 3145728 | tf_op jit(solution)/shard_map/all_to_all | solution.py:333
  24.2 11.8 %collective-permute-start = (bf16[4,128,128]{2,1,0:T(8,128)(2,1)S(1)}, bf16[4,128,128]{2,1,0:T(8,128)(2,1)S(1)}, u32[]{:S(2)}, u32[]{:S(2)}) collective-permute-start(bf16[4,128,128]{2,1,0:T(8,128)(2,1)S(1)} %get-tuple-element.33), channel_id=1, source_target_pairs={{0,4},{1,5},{2,6},{3,7},{4,0},{5,1},{6,2},{7,3},{8,12},{9,13},{10,... | collective-permute-start | bytes 393224 | tf_op jit(solution)/shard_map/ppermute | solution.py:280
  28.5 10.1 %collective-permute-start.1 = (bf16[4,128,128]{2,1,0:T(8,128)(2,1)S(1)}, bf16[4,128,128]{2,1,0:T(8,128)(2,1)S(1)}, u32[]{:S(2)}, u32[]{:S(2)}) collective-permute-start(bf16[4,128,128]{2,1,0:T(8,128)(2,1)S(1)} %get-tuple-element.34), channel_id=1, source_target_pairs={{0,8},{1,9},{2,10},{3,11},{4,12},{5,13},{6,14},{7,15},{8,0},{9,1},... | collective-permute-start | bytes 393224 | tf_op jit(solution)/shard_map/ppermute | solution.py:280
  34.1 11.9 %collective-permute-start.2 = (bf16[4,128,128]{2,1,0:T(8,128)(2,1)S(1)}, bf16[4,128,128]{2,1,0:T(8,128)(2,1)S(1)}, u32[]{:S(2)}, u32[]{:S(2)}) collective-permute-start(bf16[4,128,128]{2,1,0:T(8,128)(2,1)S(1)} %get-tuple-element.35), channel_id=1, source_target_pairs={{0,12},{1,13},{2,14},{3,15},{4,8},{5,9},{6,10},{7,11},{8,4},{9,5},... | collective-permute-start | bytes 393224 | tf_op jit(solution)/shard_map/ppermute | solution.py:280
  46.1 8.6 %collective-permute-start.3 = (bf16[4,128,128]{2,1,0:T(8,128)(2,1)S(1)}, bf16[4,128,128]{2,1,0:T(8,128)(2,1)S(1)}, u32[]{:S(2)}, u32[]{:S(2)}) collective-permute-start(bf16[4,128,128]{2,1,0:T(8,128)(2,1)S(1)} %get-tuple-element.37), channel_id=1, source_target_pairs={{0,1},{1,0},{2,3},{3,2},{4,5},{5,4},{6,7},{7,6},{8,9},{9,8},{10,11... | collective-permute-start | bytes 393224 | tf_op jit(solution)/shard_map/ppermute | solution.py:280
  48.5 8.2 %collective-permute-start.4 = (bf16[4,128,128]{2,1,0:T(8,128)(2,1)S(1)}, bf16[4,128,128]{2,1,0:T(8,128)(2,1)S(1)}, u32[]{:S(2)}, u32[]{:S(2)}) collective-permute-start(bf16[4,128,128]{2,1,0:T(8,128)(2,1)S(1)} %get-tuple-element.38), channel_id=1, source_target_pairs={{0,2},{1,3},{2,0},{3,1},{4,6},{5,7},{6,4},{7,5},{8,10},{9,11},{10,... | collective-permute-start | bytes 393224 | tf_op jit(solution)/shard_map/ppermute | solution.py:280
  52.7 7.7 %collective-permute-start.5 = (bf16[4,128,128]{2,1,0:T(8,128)(2,1)S(1)}, bf16[4,128,128]{2,1,0:T(8,128)(2,1)S(1)}, u32[]{:S(2)}, u32[]{:S(2)}) collective-permute-start(bf16[4,128,128]{2,1,0:T(8,128)(2,1)S(1)} %get-tuple-element.39), channel_id=1, source_target_pairs={{0,3},{1,2},{2,1},{3,0},{4,7},{5,6},{6,5},{7,4},{8,11},{9,10},{10,... | collective-permute-start | bytes 393224 | tf_op jit(solution)/shard_map/ppermute | solution.py:280
  60.4 15.6 %copy-start.3 = (bf16[512,128]{1,0:T(8,128)(2,1)S(1)}, bf16[512,128]{1,0:T(8,128)(2,1)}, u32[]{:S(2)}) copy-start(bf16[512,128]{1,0:T(8,128)(2,1)} %cotangent_ref.1) | copy-start | bytes 393220
  60.4 15.6 %copy-start.5 = (bf16[128,128]{1,0:T(8,128)(2,1)S(1)}, bf16[128,128]{1,0:T(8,128)(2,1)}, u32[]{:S(2)}) copy-start(bf16[128,128]{1,0:T(8,128)(2,1)} %weight_ref.1) | copy-start | bytes 98308
  60.4 15.6 %copy-start.8 = (s32[512]{0:T(512)S(1)}, s32[512]{0:T(512)}, u32[]{:S(2)}) copy-start(s32[512]{0:T(512)} %param.10) | copy-start | bytes 6148
  60.4 15.6 %copy-start.9 = (f32[128]{0:T(128)S(1)}, f32[128]{0:T(128)}, u32[]{:S(2)}) copy-start(f32[128]{0:T(128)} %param.16) | copy-start | bytes 1540
  81.9 1.1 copy-start.2
  83.0 12.4 %copy-start.1 = (bf16[80,128,128]{2,1,0:T(8,128)(2,1)S(1)}, bf16[80,128,128]{2,1,0:T(8,128)(2,1)}, u32[]{:S(2)}) copy-start(bf16[80,128,128]{2,1,0:T(8,128)(2,1)} %tiles_ref.5) | copy-start | bytes 7864324
  83.0 65.2 %all-to-all-start.1 = ((bf16[48,128,128]{2,1,0:T(8,128)(2,1)}), bf16[48,128,128]{2,1,0:T(8,128)(2,1)}, u32[]{:S(2)}, u32[]{:S(2)}) async-start(bf16[48,128,128]{2,1,0:T(8,128)(2,1)} %copy-done.2), calls=%async_computation.1 | async-start | bytes 3145728 | tf_op jit(solution)/shard_map/all_to_all | solution.py:368
  96.6 61.4 %copy-start.10 = (s32[48,128]{1,0:T(8,128)S(1)}, s32[48,128]{1,0:T(8,128)}, u32[]{:S(2)}) copy-start(s32[48,128]{1,0:T(8,128)} %lists_ref.5) | copy-start | bytes 73732
  96.6 11.8 %collective-permute-start.6 = (bf16[4,160,128]{2,1,0:T(8,128)(2,1)S(1)}, bf16[4,160,128]{2,1,0:T(8,128)(2,1)S(1)}, u32[]{:S(2)}, u32[]{:S(2)}) collective-permute-start(bf16[4,160,128]{2,1,0:T(8,128)(2,1)S(1)} %get-tuple-element.46), channel_id=1, source_target_pairs={{0,4},{1,5},{2,6},{3,7},{4,0},{5,1},{6,2},{7,3},{8,12},{9,13},{10,... | collective-permute-start | bytes 491528 | tf_op jit(solution)/shard_map/ppermute | solution.py:280
  100.8 11.0 %collective-permute-start.7 = (bf16[4,160,128]{2,1,0:T(8,128)(2,1)S(1)}, bf16[4,160,128]{2,1,0:T(8,128)(2,1)S(1)}, u32[]{:S(2)}, u32[]{:S(2)}) collective-permute-start(bf16[4,160,128]{2,1,0:T(8,128)(2,1)S(1)} %get-tuple-element.47), channel_id=1, source_target_pairs={{0,8},{1,9},{2,10},{3,11},{4,12},{5,13},{6,14},{7,15},{8,0},{9,1},... | collective-permute-start | bytes 491528 | tf_op jit(solution)/shard_map/ppermute | solution.py:280
  106.5 15.6 %collective-permute-start.8 = (bf16[4,160,128]{2,1,0:T(8,128)(2,1)S(1)}, bf16[4,160,128]{2,1,0:T(8,128)(2,1)S(1)}, u32[]{:S(2)}, u32[]{:S(2)}) collective-permute-start(bf16[4,160,128]{2,1,0:T(8,128)(2,1)S(1)} %get-tuple-element.48), channel_id=1, source_target_pairs={{0,12},{1,13},{2,14},{3,15},{4,8},{5,9},{6,10},{7,11},{8,4},{9,5},... | collective-permute-start | bytes 491528 | tf_op jit(solution)/shard_map/ppermute | solution.py:280
  122.1 7.9 %collective-permute-start.9 = (bf16[4,160,128]{2,1,0:T(8,128)(2,1)S(1)}, bf16[4,160,128]{2,1,0:T(8,128)(2,1)S(1)}, u32[]{:S(2)}, u32[]{:S(2)}) collective-permute-start(bf16[4,160,128]{2,1,0:T(8,128)(2,1)S(1)} %get-tuple-element.50), channel_id=1, source_target_pairs={{0,1},{1,0},{2,3},{3,2},{4,5},{5,4},{6,7},{7,6},{8,9},{9,8},{10,11... | collective-permute-start | bytes 491528 | tf_op jit(solution)/shard_map/ppermute | solution.py:280
  124.5 7.8 %collective-permute-start.10 = (bf16[4,160,128]{2,1,0:T(8,128)(2,1)S(1)}, bf16[4,160,128]{2,1,0:T(8,128)(2,1)S(1)}, u32[]{:S(2)}, u32[]{:S(2)}) collective-permute-start(bf16[4,160,128]{2,1,0:T(8,128)(2,1)S(1)} %get-tuple-element.51), channel_id=1, source_target_pairs={{0,2},{1,3},{2,0},{3,1},{4,6},{5,7},{6,4},{7,5},{8,10},{9,11},{10,... | collective-permute-start | bytes 491528 | tf_op jit(solution)/shard_map/ppermute | solution.py:280
  127.0 8.9 %collective-permute-start.11 = (bf16[4,160,128]{2,1,0:T(8,128)(2,1)S(1)}, bf16[4,160,128]{2,1,0:T(8,128)(2,1)S(1)}, u32[]{:S(2)}, u32[]{:S(2)}) collective-permute-start(bf16[4,160,128]{2,1,0:T(8,128)(2,1)S(1)} %get-tuple-element.52), channel_id=1, source_target_pairs={{0,3},{1,2},{2,1},{3,0},{4,7},{5,6},{6,5},{7,4},{8,11},{9,10},{10,... | collective-permute-start | bytes 491528 | tf_op jit(solution)/shard_map/ppermute | solution.py:280
  148.2 19.2 %all-to-all-start.2 = ((f32[12,16,128]{2,1,0:T(8,128)}), f32[12,16,128]{2,1,0:T(8,128)S(1)}, u32[]{:S(2)}, u32[]{:S(2)}) async-start(f32[12,16,128]{2,1,0:T(8,128)} %shard_map.129), calls=%async_computation.2 | async-start | bytes 196608 | tf_op jit(solution)/shard_map/all_to_all | solution.py:399
